TPU v7x, 256 devices: a whole 4x4x8 slice. The times are simulated.
256 devices in a mesh: space: 32 (over z_hi, x, core), mode: 8 (over z_lo, y).
Axes of the slice: x: 4, y: 4, z: 8 (z_hi: 4, z_lo: 2; z = z_hi * 2 + z_lo), core: 2. Of those that a mesh axis runs over, the one named last changes fastest.
Arguments:
- field: float32 [3, 16, 256, 64, 256], P(None, 'mode', 'space'), may hold values from -6 to 6
- velocity: float32 [256, 64, 256], P('space'), may hold values from 0.1 to 1
- dispersion: float32 [256, 64, 256], P('space'), may hold values from 0.05 to 0.3
- mobility: float32 [3, 8, 16], replicated, may hold values from -0.2 to 0.2
- material: int32 [256, 64, 256], P('space'), may hold values from 0 to 7
- fixed_mask: int32 [256, 64, 256], P('space'), may hold values 0 or 1
Outputs:
- advanced: float32 [3, 16, 256, 64, 256], P(None, 'mode', 'space')
All inputs are finite; a program needn't handle non-finite values. No bound on the sum of `fixed_mask` on one device may be relied on, other than what follows from the above.
Results may differ from a plain program's by a relative error of at most 0.0001.
Values sent between devices are 32-bit elements; how exact they have to be, the bound alone decides.
No kernel may reach another device: no remote copies, remote signals or barrier semaphores. Data moves between devices by JAX's collectives and lax.ppermute only.
A program may use at most 64 MiB of HBM per device.

v0:
```python
import math

import jax
import jax.numpy as jnp
from jax import lax
from jax.sharding import PartitionSpec as P

STEPS = 2


TIME_STEP = 0.1
MOBILE_BASE = 0.7


def padded(array, sides, width):
    for axis, dim in sides:
        size, length = (lax.axis_size(axis), array.shape[dim])
        up = [(i, (i + 1) % size) for i in range(size - 1)]
        down = [(j, i) for i, j in up]
        last = lax.slice_in_dim(array, length - width, length, axis=dim)
        first = lax.slice_in_dim(array, 0, width, axis=dim)
        before = lax.ppermute(last, axis, up)
        after = lax.ppermute(first, axis, down)
        array = jnp.concatenate([before, array, after], axis=dim)
    return array


def legendre_weight(order):
    return math.comb(2 * order, order) / 4.0**order


def triple_table(terms_count):
    entries = []
    for degree_a in range(terms_count):
        slab_values = []
        for degree_b in range(terms_count):
            row_values = []
            for degree_c in range(terms_count):
                degree_sum = degree_a + degree_b + degree_c
                halfsum = degree_sum // 2
                amount = 0.0
                if (
                    degree_sum % 2 == 0
                    and halfsum >= degree_a
                    and (halfsum >= degree_b)
                    and (halfsum >= degree_c)
                ):
                    amount = (
                        legendre_weight(halfsum - degree_a)
                        * legendre_weight(halfsum - degree_b)
                        * legendre_weight(halfsum - degree_c)
                    )
                    amount = amount / legendre_weight(halfsum) / (degree_sum + 1)
                    amount = amount * math.sqrt(
                        (2 * degree_a + 1) * (2 * degree_b + 1) * (2 * degree_c + 1)
                    )
                row_values.append(amount)
            slab_values.append(row_values)
        entries.append(slab_values)
    return jnp.asarray(entries, jnp.float32)


def stencil(x_padded, y_padded, velocity, dispersion):
    middle = x_padded[:, :, 2:-2]
    left_two = x_padded[:, :, :-4]
    left_one = x_padded[:, :, 1:-3]
    right_one = x_padded[:, :, 3:-1]
    right_two = x_padded[:, :, 4:]
    lower_y = y_padded[:, :, :, :-2]
    upper_y = y_padded[:, :, :, 2:]
    z_padded = jnp.pad(middle, ((0, 0), (0, 0), (0, 0), (0, 0), (1, 1)))
    lower_z = z_padded[:, :, :, :, :-2]
    upper_z = z_padded[:, :, :, :, 2:]
    spread = (16.0 * (left_one + right_one) - (left_two + right_two) - 30.0 * middle) / 12.0
    spread = spread + (lower_y + upper_y) + (lower_z + upper_z) - 4.0 * middle
    carried = (2.0 * right_one + 3.0 * middle - 6.0 * left_one + left_two) / 6.0
    return dispersion[None, None] * spread - velocity[None, None] * carried


def class_terms(total, class_mats, piece, picks):

    def add_class(klass, running):
        matrix = lax.dynamic_index_in_dim(class_mats, klass, 1, keepdims=False)
        mixed = jnp.einsum("mij,mjxyz->mixyz", matrix, piece, precision=lax.Precision.HIGHEST)
        chosen = lax.dynamic_index_in_dim(picks, klass, 0, keepdims=False)
        return running + chosen[None, None] * mixed

    return lax.fori_loop(0, class_mats.shape[1], add_class, total)


def on_device(field, velocity, dispersion, mobility, material, fixed_mask):
    modes = mobility.shape[2]
    classes = mobility.shape[1]
    triple = triple_table(modes)
    class_mats = jnp.einsum("ijk,mck->mcij", triple, mobility, precision=lax.Precision.HIGHEST)
    mode_count = lax.axis_size("mode")
    mode_index = lax.axis_index("mode")
    rows_local = field.shape[3] // mode_count
    picks = (material[None] == jnp.arange(classes, dtype=jnp.int32)[:, None, None, None]).astype(
        jnp.float32
    )
    movable = (1 - fixed_mask).astype(jnp.float32)
    state = field
    picks_cells = lax.dynamic_slice_in_dim(picks, mode_index * rows_local, rows_local, 2)
    for sweep_index in range(STEPS):
        x_padded = padded(state, (("space", 2),), 2)
        y_padded = jnp.pad(state, ((0, 0), (0, 0), (0, 0), (1, 1), (0, 0)))
        operated = stencil(x_padded, y_padded, velocity, dispersion)
        by_cells = lax.all_to_all(operated, "mode", split_axis=3, concat_axis=1, tiled=True)
        mixed_cells = class_terms(MOBILE_BASE * by_cells, class_mats, by_cells, picks_cells)
        coupled = lax.all_to_all(mixed_cells, "mode", split_axis=1, concat_axis=3, tiled=True)
        state = state + TIME_STEP * movable[None, None] * coupled
    return state


def solution(mesh):
    in_specs = (
        P(None, "mode", "space", None, None),
        P("space", None, None),
        P("space", None, None),
        P(),
        P("space", None, None),
        P("space", None, None),
    )
    out_specs = P(None, "mode", "space", None, None)
    return jax.shard_map(
        on_device, mesh=mesh, in_specs=in_specs, out_specs=out_specs, check_vma=False
    )
```

profile of v0, /device:TPU:71, one launch (start us, length us, event | category | flops | bytes accessed | tf_op | source)
XLA Modules:
  0.0 351.9 jit_solution(16040759682894328915)
XLA Ops:
  1.7 6.7 %collective-permute-start = (f32[3,2,2,64,256]{4,3,2,1,0:T(8,128)S(1)}, f32[3,2,2,64,256]{4,3,2,1,0:T(8,128)S(1)}, u32[]{:S(2)}, u32[]{:S(2)}) collective-permute-start(f32[3,2,2,64,256]{4,3,2,1,0:T(8,128)S(1)} %get-tuple-element.247), channel_id=1, source_target_pairs={{0,8},{8,16},{16,24},{24,32},{32,40},{40,48},{48,56},{56,64},{64,7... | collective-permute-start | bytes 2359304 | tf_op jit(solution)/shard_map/ppermute | solution.py:22
  13.9 11.8 %collective-permute-done = f32[3,2,2,64,256]{4,3,2,1,0:T(8,128)S(1)} collective-permute-done((f32[3,2,2,64,256]{4,3,2,1,0:T(8,128)S(1)}, f32[3,2,2,64,256]{4,3,2,1,0:T(8,128)S(1)}, u32[]{:S(2)}, u32[]{:S(2)}) %collective-permute-start) | collective-permute-done | bytes 786464 | tf_op jit(solution)/shard_map/ppermute | solution.py:22
  26.3 7.9 %collective-permute-done.1 = f32[3,2,2,64,256]{4,3,2,1,0:T(8,128)S(1)} collective-permute-done((f32[3,2,2,64,256]{4,3,2,1,0:T(8,128)S(1)}, f32[3,2,2,64,256]{4,3,2,1,0:T(8,128)S(1)}, u32[]{:S(2)}, u32[]{:S(2)}) %collective-permute-start.1) | collective-permute-done | bytes 786464 | tf_op jit(solution)/shard_map/ppermute | solution.py:23
  35.2 5.7 %fusion.10 = f32[3,2,8,64,256]{4,2,1,0,3:T(8,128)} fusion(f32[3,2,8,64,256]{4,2,1,0,3:T(8,128)S(1)} %get-tuple-element.250, f32[3,2,10,64,256]{4,2,1,0,3:T(8,128)S(1)} %copy_dynamic-update-slice_fusion, f32[3,2,2,64,256]{4,2,1,0,3:T(2,128)S(1)} %copy.38, f32[8,64,256]{2,0,1:T(8,128)S(1)} %copy.47, f32[8,64,256]{2,0,1:T(8,128)S(1)} %copy.37), kind=kLoop, calls=%fused_computation.24 | loop fusion | flops 18874368 | bytes 14417920 | tf_op jit(solution)/shard_map/sub | solution.py:77
  47.7 20.6 %all-to-all-done = f32[3,2,8,64,256]{4,2,1,0,3:T(8,128)} async-done(((f32[3,2,8,64,256]{4,2,1,0,3:T(8,128)}), f32[3,2,8,64,256]{4,2,1,0,3:T(8,128)}, u32[]{:S(2)}, u32[]{:S(2)}) %all-to-all-start) | async-done | bytes 3145760 | tf_op jit(solution)/shard_map/all_to_all | solution.py:109
  79.6 51.3 %while.26 = (s32[]{:T(128)}, f32[3,16,8,8,256]{4,1,3,2,0:T(8,128)}, f32[8,8,8,256]{3,2,1,0:T(8,128)}, f32[3,8,16,16]{3,2,0,1:T(8,128)S(1)}, f32[3,16,8,8,256]{4,1,3,2,0:T(8,128)S(1)}, /*index=5*/s32[]{:T(128)}) while((s32[]{:T(128)}, f32[3,16,8,8,256]{4,1,3,2,0:T(8,128)}, f32[8,8,8,256]{3,2,1,0:T(8,128)}, f32[3,8,16,16]{3,2,0,1:T(8,128)S(1)}, ...), condition=%wide.region_1.2_spmd, body=%wide.region_0.1_spmd.sunk | while | flops 152567808 | bytes 9658453 | solution.py:88
  80.4 5.6 %multiply_add_fusion.4 = f32[3,16,8,8,256]{4,1,3,2,0:T(8,128)} fusion(f32[3,16,8,8,256]{4,1,3,2,0:T(8,128)} %get-tuple-element.320, f32[3,16,8,8,256]{4,1,3,2,0:T(8,128)S(1)} %get-tuple-element.329, f32[8,8,256]{2,1,0:T(8,128)S(1)} %dynamic-slice_bitcast_fusion.4, f32[3,8,16,16]{3,2,0,1:T(8,128)S(1)} %get-tuple-element.328, s32[]{:T(128)S(6)} %copy.72), kind=kOutput, calls=%fused_computation.clone.1 | convolution fusion | flops 152567808 | bytes 9527300 | tf_op jit(solution)/shard_map/while/body/eval_jaxpr/mij,mjxyz->mixyz/dot_general | solution.py:84
  93.3 5.6 %multiply_add_fusion.4 = f32[3,16,8,8,256]{4,1,3,2,0:T(8,128)} fusion(f32[3,16,8,8,256]{4,1,3,2,0:T(8,128)} %get-tuple-element.320, f32[3,16,8,8,256]{4,1,3,2,0:T(8,128)S(1)} %get-tuple-element.329, f32[8,8,256]{2,1,0:T(8,128)S(1)} %dynamic-slice_bitcast_fusion.4, f32[3,8,16,16]{3,2,0,1:T(8,128)S(1)} %get-tuple-element.328, s32[]{:T(128)S(6)} %copy.72), kind=kOutput, calls=%fused_computation.clone.1 | convolution fusion | flops 152567808 | bytes 9527300 | tf_op jit(solution)/shard_map/while/body/eval_jaxpr/mij,mjxyz->mixyz/dot_general | solution.py:84
  106.1 5.6 %multiply_add_fusion.4 = f32[3,16,8,8,256]{4,1,3,2,0:T(8,128)} fusion(f32[3,16,8,8,256]{4,1,3,2,0:T(8,128)} %get-tuple-element.320, f32[3,16,8,8,256]{4,1,3,2,0:T(8,128)S(1)} %get-tuple-element.329, f32[8,8,256]{2,1,0:T(8,128)S(1)} %dynamic-slice_bitcast_fusion.4, f32[3,8,16,16]{3,2,0,1:T(8,128)S(1)} %get-tuple-element.328, s32[]{:T(128)S(6)} %copy.72), kind=kOutput, calls=%fused_computation.clone.1 | convolution fusion | flops 152567808 | bytes 9527300 | tf_op jit(solution)/shard_map/while/body/eval_jaxpr/mij,mjxyz->mixyz/dot_general | solution.py:84
  125.3 5.6 %multiply_add_fusion.4 = f32[3,16,8,8,256]{4,1,3,2,0:T(8,128)} fusion(f32[3,16,8,8,256]{4,1,3,2,0:T(8,128)} %get-tuple-element.320, f32[3,16,8,8,256]{4,1,3,2,0:T(8,128)S(1)} %get-tuple-element.329, f32[8,8,256]{2,1,0:T(8,128)S(1)} %dynamic-slice_bitcast_fusion.4, f32[3,8,16,16]{3,2,0,1:T(8,128)S(1)} %get-tuple-element.328, s32[]{:T(128)S(6)} %copy.72), kind=kOutput, calls=%fused_computation.clone.1 | convolution fusion | flops 152567808 | bytes 9527300 | tf_op jit(solution)/shard_map/while/body/eval_jaxpr/mij,mjxyz->mixyz/dot_general | solution.py:84
  142.1 33.9 %all-to-all-done.1 = f32[3,16,8,8,256]{4,3,2,0,1:T(8,128)S(1)} async-done(((f32[3,16,8,8,256]{4,3,2,0,1:T(8,128)}), f32[3,16,8,8,256]{4,3,2,0,1:T(8,128)S(1)}, u32[]{:S(2)}, u32[]{:S(2)}) %all-to-all-start.1) | async-done | bytes 3145760 | tf_op jit(solution)/shard_map/all_to_all | solution.py:111
  183.2 7.8 %collective-permute-start.2 = (f32[3,2,2,64,256]{4,3,2,1,0:T(8,128)S(1)}, f32[3,2,2,64,256]{4,3,2,1,0:T(8,128)S(1)}, u32[]{:S(2)}, u32[]{:S(2)}) collective-permute-start(f32[3,2,2,64,256]{4,3,2,1,0:T(8,128)S(1)} %copy.53), channel_id=1, source_target_pairs={{0,8},{8,16},{16,24},{24,32},{32,40},{40,48},{48,56},{56,64},{64,7... | collective-permute-start | bytes 2359304 | tf_op jit(solution)/shard_map/ppermute | solution.py:22
  191.0 15.8 %collective-permute-done.3 = f32[3,2,2,64,256]{4,3,2,1,0:T(8,128)S(1)} collective-permute-done((f32[3,2,2,64,256]{4,3,2,1,0:T(8,128)S(1)}, f32[3,2,2,64,256]{4,3,2,1,0:T(8,128)S(1)}, u32[]{:S(2)}, u32[]{:S(2)}) %collective-permute-start.3) | collective-permute-done | bytes 786464 | tf_op jit(solution)/shard_map/ppermute | solution.py:23
  213.7 33.2 %all_to_all.72 = f32[3,2,8,64,256]{4,2,1,0,3:T(8,128)S(1)} all-to-all(f32[3,2,8,64,256]{4,2,1,0,3:T(8,128)S(1)} %fusion.15), channel_id=1, replica_groups=mesh['space'=32,'mode'=8] {'mode'}, dimensions={3} | all-to-all | bytes 6291456 | tf_op jit(solution)/shard_map/all_to_all | solution.py:109
  256.5 51.8 %while.27 = (s32[]{:T(128)}, f32[3,16,8,8,256]{4,1,3,2,0:T(8,128)}, f32[8,8,8,256]{3,2,1,0:T(8,128)}, f32[3,8,16,16]{3,2,0,1:T(8,128)S(1)}, f32[3,16,8,8,256]{4,1,3,2,0:T(8,128)S(1)}, /*index=5*/s32[]{:T(128)}) while((s32[]{:T(128)}, f32[3,16,8,8,256]{4,1,3,2,0:T(8,128)}, f32[8,8,8,256]{3,2,1,0:T(8,128)}, f32[3,8,16,16]{3,2,0,1:T(8,128)S(1)}, ...), condition=%wide.region_3.4_spmd, body=%wide.region_2.3_spmd.sunk | while | flops 152567808 | bytes 9658453 | solution.py:88
  257.3 5.6 %multiply_add_fusion.5 = f32[3,16,8,8,256]{4,1,3,2,0:T(8,128)} fusion(f32[3,16,8,8,256]{4,1,3,2,0:T(8,128)} %get-tuple-element.338, f32[3,16,8,8,256]{4,1,3,2,0:T(8,128)S(1)} %get-tuple-element.347, f32[8,8,256]{2,1,0:T(8,128)S(1)} %dynamic-slice_bitcast_fusion.5, f32[3,8,16,16]{3,2,0,1:T(8,128)S(1)} %get-tuple-element.346, s32[]{:T(128)S(6)} %copy.78), kind=kOutput, calls=%fused_computation.5.clone.1 | convolution fusion | flops 152567808 | bytes 9527300 | tf_op jit(solution)/shard_map/while/body/eval_jaxpr/mij,mjxyz->mixyz/dot_general | solution.py:84
  263.8 5.6 %multiply_add_fusion.5 = f32[3,16,8,8,256]{4,1,3,2,0:T(8,128)} fusion(f32[3,16,8,8,256]{4,1,3,2,0:T(8,128)} %get-tuple-element.338, f32[3,16,8,8,256]{4,1,3,2,0:T(8,128)S(1)} %get-tuple-element.347, f32[8,8,256]{2,1,0:T(8,128)S(1)} %dynamic-slice_bitcast_fusion.5, f32[3,8,16,16]{3,2,0,1:T(8,128)S(1)} %get-tuple-element.346, s32[]{:T(128)S(6)} %copy.78), kind=kOutput, calls=%fused_computation.5.clone.1 | convolution fusion | flops 152567808 | bytes 9527300 | tf_op jit(solution)/shard_map/while/body/eval_jaxpr/mij,mjxyz->mixyz/dot_general | solution.py:84
  270.3 5.6 %multiply_add_fusion.5 = f32[3,16,8,8,256]{4,1,3,2,0:T(8,128)} fusion(f32[3,16,8,8,256]{4,1,3,2,0:T(8,128)} %get-tuple-element.338, f32[3,16,8,8,256]{4,1,3,2,0:T(8,128)S(1)} %get-tuple-element.347, f32[8,8,256]{2,1,0:T(8,128)S(1)} %dynamic-slice_bitcast_fusion.5, f32[3,8,16,16]{3,2,0,1:T(8,128)S(1)} %get-tuple-element.346, s32[]{:T(128)S(6)} %copy.78), kind=kOutput, calls=%fused_computation.5.clone.1 | convolution fusion | flops 152567808 | bytes 9527300 | tf_op jit(solution)/shard_map/while/body/eval_jaxpr/mij,mjxyz->mixyz/dot_general | solution.py:84
  276.7 5.6 %multiply_add_fusion.5 = f32[3,16,8,8,256]{4,1,3,2,0:T(8,128)} fusion(f32[3,16,8,8,256]{4,1,3,2,0:T(8,128)} %get-tuple-element.338, f32[3,16,8,8,256]{4,1,3,2,0:T(8,128)S(1)} %get-tuple-element.347, f32[8,8,256]{2,1,0:T(8,128)S(1)} %dynamic-slice_bitcast_fusion.5, f32[3,8,16,16]{3,2,0,1:T(8,128)S(1)} %get-tuple-element.346, s32[]{:T(128)S(6)} %copy.78), kind=kOutput, calls=%fused_computation.5.clone.1 | convolution fusion | flops 152567808 | bytes 9527300 | tf_op jit(solution)/shard_map/while/body/eval_jaxpr/mij,mjxyz->mixyz/dot_general | solution.py:84
  283.2 5.6 %multiply_add_fusion.5 = f32[3,16,8,8,256]{4,1,3,2,0:T(8,128)} fusion(f32[3,16,8,8,256]{4,1,3,2,0:T(8,128)} %get-tuple-element.338, f32[3,16,8,8,256]{4,1,3,2,0:T(8,128)S(1)} %get-tuple-element.347, f32[8,8,256]{2,1,0:T(8,128)S(1)} %dynamic-slice_bitcast_fusion.5, f32[3,8,16,16]{3,2,0,1:T(8,128)S(1)} %get-tuple-element.346, s32[]{:T(128)S(6)} %copy.78), kind=kOutput, calls=%fused_computation.5.clone.1 | convolution fusion | flops 152567808 | bytes 9527300 | tf_op jit(solution)/shard_map/while/body/eval_jaxpr/mij,mjxyz->mixyz/dot_general | solution.py:84
  289.7 5.6 %multiply_add_fusion.5 = f32[3,16,8,8,256]{4,1,3,2,0:T(8,128)} fusion(f32[3,16,8,8,256]{4,1,3,2,0:T(8,128)} %get-tuple-element.338, f32[3,16,8,8,256]{4,1,3,2,0:T(8,128)S(1)} %get-tuple-element.347, f32[8,8,256]{2,1,0:T(8,128)S(1)} %dynamic-slice_bitcast_fusion.5, f32[3,8,16,16]{3,2,0,1:T(8,128)S(1)} %get-tuple-element.346, s32[]{:T(128)S(6)} %copy.78), kind=kOutput, calls=%fused_computation.5.clone.1 | convolution fusion | flops 152567808 | bytes 9527300 | tf_op jit(solution)/shard_map/while/body/eval_jaxpr/mij,mjxyz->mixyz/dot_general | solution.py:84
  296.1 5.6 %multiply_add_fusion.5 = f32[3,16,8,8,256]{4,1,3,2,0:T(8,128)} fusion(f32[3,16,8,8,256]{4,1,3,2,0:T(8,128)} %get-tuple-element.338, f32[3,16,8,8,256]{4,1,3,2,0:T(8,128)S(1)} %get-tuple-element.347, f32[8,8,256]{2,1,0:T(8,128)S(1)} %dynamic-slice_bitcast_fusion.5, f32[3,8,16,16]{3,2,0,1:T(8,128)S(1)} %get-tuple-element.346, s32[]{:T(128)S(6)} %copy.78), kind=kOutput, calls=%fused_computation.5.clone.1 | convolution fusion | flops 152567808 | bytes 9527300 | tf_op jit(solution)/shard_map/while/body/eval_jaxpr/mij,mjxyz->mixyz/dot_general | solution.py:84
  302.6 5.6 %multiply_add_fusion.5 = f32[3,16,8,8,256]{4,1,3,2,0:T(8,128)} fusion(f32[3,16,8,8,256]{4,1,3,2,0:T(8,128)} %get-tuple-element.338, f32[3,16,8,8,256]{4,1,3,2,0:T(8,128)S(1)} %get-tuple-element.347, f32[8,8,256]{2,1,0:T(8,128)S(1)} %dynamic-slice_bitcast_fusion.5, f32[3,8,16,16]{3,2,0,1:T(8,128)S(1)} %get-tuple-element.346, s32[]{:T(128)S(6)} %copy.78), kind=kOutput, calls=%fused_computation.5.clone.1 | convolution fusion | flops 152567808 | bytes 9527300 | tf_op jit(solution)/shard_map/while/body/eval_jaxpr/mij,mjxyz->mixyz/dot_general | solution.py:84
  312.0 33.5 %all_to_all.73 = f32[3,16,8,8,256]{4,3,2,0,1:T(8,128)S(1)} all-to-all(f32[3,16,8,8,256]{4,3,2,0,1:T(8,128)S(1)} %copy.59), channel_id=1, replica_groups=mesh['space'=32,'mode'=8] {'mode'}, dimensions={1} | all-to-all | bytes 6291456 | tf_op jit(solution)/shard_map/all_to_all | solution.py:111
  (87 shorter events, 107.2 us)
Async XLA Ops:
  0.0 46.8 %copy-start = (s32[8,64,256]{2,1,0:T(8,128)S(1)}, s32[8,64,256]{2,1,0:T(8,128)}, u32[]{:S(2)}) copy-start(s32[8,64,256]{2,1,0:T(8,128)} %param.15) | copy-start | bytes 1572868
  0.0 12.1 %copy-start.4 = (f32[3,2,8,64,256]{4,3,2,1,0:T(8,128)S(1)}, f32[3,2,8,64,256]{4,3,2,1,0:T(8,128)}, u32[]{:S(2)}) copy-start(f32[3,2,8,64,256]{4,3,2,1,0:T(8,128)} %param.11) | copy-start | bytes 9437188
  0.0 11.8 %copy-start.12 = (f32[8,64,256]{2,1,0:T(8,128)S(1)}, f32[8,64,256]{2,1,0:T(8,128)}, u32[]{:S(2)}) copy-start(f32[8,64,256]{2,1,0:T(8,128)} %param.13) | copy-start | bytes 1572868
  1.7 24.0 %collective-permute-start = (f32[3,2,2,64,256]{4,3,2,1,0:T(8,128)S(1)}, f32[3,2,2,64,256]{4,3,2,1,0:T(8,128)S(1)}, u32[]{:S(2)}, u32[]{:S(2)}) collective-permute-start(f32[3,2,2,64,256]{4,3,2,1,0:T(8,128)S(1)} %get-tuple-element.247), channel_id=1, source_target_pairs={{0,8},{8,16},{16,24},{24,32},{32,40},{40,48},{48,56},{56,64},{64,7... | collective-permute-start | bytes 2359304 | tf_op jit(solution)/shard_map/ppermute | solution.py:22
  8.4 25.8 %collective-permute-start.1 = (f32[3,2,2,64,256]{4,3,2,1,0:T(8,128)S(1)}, f32[3,2,2,64,256]{4,3,2,1,0:T(8,128)S(1)}, u32[]{:S(2)}, u32[]{:S(2)}) collective-permute-start(f32[3,2,2,64,256]{4,3,2,1,0:T(8,128)S(1)} %get-tuple-element.248), channel_id=1, source_target_pairs={{8,0},{16,8},{24,16},{32,24},{40,32},{48,40},{56,48},{64,56},{72,6... | collective-permute-start | bytes 2359304 | tf_op jit(solution)/shard_map/ppermute | solution.py:23
  11.8 23.4 %copy-start.6 = (f32[8,64,256]{2,0,1:T(8,128)}, f32[8,64,256]{2,0,1:T(8,128)S(1)}, u32[]{:S(2)}) copy-start(f32[8,64,256]{2,0,1:T(8,128)S(1)} %copy.47) | copy-start | bytes 1572868
  12.1 23.0 %copy-start.8 = (f32[8,64,256]{2,0,1:T(8,128)}, f32[8,64,256]{2,0,1:T(8,128)S(1)}, u32[]{:S(2)}) copy-start(f32[8,64,256]{2,0,1:T(8,128)S(1)} %copy.37) | copy-start | bytes 1572868
  40.9 4.8 %copy-start.13 = (f32[16,16,16,1]{2,1,3,0:T(8,128)S(1)}, f32[16,16,16,1]{2,1,3,0:T(8,128)}, u32[]{:S(2)}) copy-start(f32[16,16,16,1]{2,1,3,0:T(8,128)} %constant.105) | copy-start | bytes 49156
  40.9 4.8 %copy-start.14 = (f32[3,8,16]{2,1,0:T(8,128)S(1)}, f32[3,8,16]{2,1,0:T(8,128)}, u32[]{:S(2)}) copy-start(f32[3,8,16]{2,1,0:T(8,128)} %param.14) | copy-start | bytes 4612
  40.9 27.4 %all-to-all-start = ((f32[3,2,8,64,256]{4,2,1,0,3:T(8,128)}), f32[3,2,8,64,256]{4,2,1,0,3:T(8,128)}, u32[]{:S(2)}, u32[]{:S(2)}) async-start(f32[3,2,8,64,256]{4,2,1,0,3:T(8,128)} %fusion.10), calls=%async_computation | async-start | bytes 6291456 | tf_op jit(solution)/shard_map/all_to_all | solution.py:109
  136.2 39.8 %all-to-all-start.1 = ((f32[3,16,8,8,256]{4,3,2,0,1:T(8,128)}), f32[3,16,8,8,256]{4,3,2,0,1:T(8,128)S(1)}, u32[]{:S(2)}, u32[]{:S(2)}) async-start(f32[3,16,8,8,256]{4,3,2,0,1:T(8,128)} %copy.50), calls=%async_computation.1 | async-start | bytes 6291456 | tf_op jit(solution)/shard_map/all_to_all | solution.py:111
  176.0 1.9 copy-start.5
  176.0 2.0 copy-start.10
  180.1 28.6 %copy-start.2 = (f32[3,2,8,64,256]{4,2,1,0,3:T(8,128)}, f32[3,2,8,64,256]{4,2,1,0,3:T(8,128)S(1)}, u32[]{:S(2)}) copy-start(f32[3,2,8,64,256]{4,2,1,0,3:T(8,128)S(1)} %fusion.31) | copy-start | bytes 9437188
  180.5 28.1 %copy-start.7 = (f32[8,64,256]{2,0,1:T(8,128)S(1)}, f32[8,64,256]{2,0,1:T(8,128)}, u32[]{:S(2)}) copy-start(f32[8,64,256]{2,0,1:T(8,128)} %copy-done.6) | copy-start | bytes 1572868
  180.6 28.1 %copy-start.9 = (f32[8,64,256]{2,0,1:T(8,128)S(1)}, f32[8,64,256]{2,0,1:T(8,128)}, u32[]{:S(2)}) copy-start(f32[8,64,256]{2,0,1:T(8,128)} %copy-done.8) | copy-start | bytes 1572868
  180.7 26.1 %collective-permute-start.3 = (f32[3,2,2,64,256]{4,3,2,1,0:T(8,128)S(1)}, f32[3,2,2,64,256]{4,3,2,1,0:T(8,128)S(1)}, u32[]{:S(2)}, u32[]{:S(2)}) collective-permute-start(f32[3,2,2,64,256]{4,3,2,1,0:T(8,128)S(1)} %copy.55), channel_id=1, source_target_pairs={{8,0},{16,8},{24,16},{32,24},{40,32},{48,40},{56,48},{64,56},{72,6... | collective-permute-start | bytes 2359304 | tf_op jit(solution)/shard_map/ppermute | solution.py:23
  183.2 24.9 %collective-permute-start.2 = (f32[3,2,2,64,256]{4,3,2,1,0:T(8,128)S(1)}, f32[3,2,2,64,256]{4,3,2,1,0:T(8,128)S(1)}, u32[]{:S(2)}, u32[]{:S(2)}) collective-permute-start(f32[3,2,2,64,256]{4,3,2,1,0:T(8,128)S(1)} %copy.53), channel_id=1, source_target_pairs={{0,8},{8,16},{16,24},{24,32},{32,40},{40,48},{48,56},{56,64},{64,7... | collective-permute-start | bytes 2359304 | tf_op jit(solution)/shard_map/ppermute | solution.py:22
  345.5 1.9 copy-start.3
  345.5 2.0 copy-start.11
  347.4 4.4 %copy-start.1 = (s32[8,64,256]{2,1,0:T(8,128)S(1)}, s32[8,64,256]{2,1,0:T(8,128)}, u32[]{:S(2)}) copy-start(s32[8,64,256]{2,1,0:T(8,128)} %param.15) | copy-start | bytes 1572868
where the time goes:
time: 357 us; the launch traced here: 352 us
  waiting for transfers between devices  90.7 us (25%)
  matrix products  90.6 us (25%)
  blocking collectives  66.7 us (19%)
  local copies, waits for them, and re-layouts  55.2 us (15%)
  starting transfers between devices  27.2 us (8%)
  other arithmetic  21.2 us (6%)
    dot_general x16, matrix products, add_class(): jnp.einsum('mij,mjxyz->mixyz', matrix, piece, precision=lax.Precision.HIG...  89.6 us
    all_to_all x1, waiting for transfers between devices, on_device(): lax.all_to_all(mixed_cells, 'mode', split_axis=1, concat_axis=3, tiled=True)  33.9 us
    all_to_all x1, blocking collectives, on_device(): lax.all_to_all(mixed_cells, 'mode', split_axis=1, concat_axis=3, tiled=True)  33.5 us
    all_to_all x1, blocking collectives, on_device(): lax.all_to_all(operated, 'mode', split_axis=3, concat_axis=1, tiled=True)  33.2 us
    ppermute x2, waiting for transfers between devices, padded(): after = lax.ppermute(first, axis, down)  23.7 us
    all_to_all x1, waiting for transfers between devices, on_device(): lax.all_to_all(operated, 'mode', split_axis=3, concat_axis=1, tiled=True)  20.6 us
    all_to_all x4, local copies, waits for them, and re-layouts, on_device(): lax.all_to_all(operated, 'mode', split_axis=3, concat_axis=1, tiled=True)  16.4 us
    ppermute x2, starting transfers between devices, padded(): before = lax.ppermute(last, axis, up)  14.6 us
  transfers between devices with their start and end apart: 6, of which 6 were waited for; matrix products, arithmetic and copies ran while one was open for 3% of the time, Pallas kernels for 0%

commit v1 on v0

v1 whole, which is shorter than its diff:
```python
import functools
import math

import jax
import jax.numpy as jnp
import numpy as np
from jax import lax
from jax.experimental import pallas as pl
from jax.experimental.pallas import tpu as pltpu
from jax.sharding import PartitionSpec as P


TIME_STEP = 0.1
MOBILE_BASE = 0.7
CHUNKS = ((0, 1), (1, 1), (2, 1))
VMEM_LIMIT = 40 * 1024 * 1024


def legendre_weight(order):
    return math.comb(2 * order, order) / 4.0**order


def triple_table(terms_count):
    table = np.zeros((terms_count,) * 3, np.float64)
    for a in range(terms_count):
        for b in range(terms_count):
            for c in range(terms_count):
                total = a + b + c
                half = total // 2
                if total % 2 == 0 and max(a, b, c) <= half:
                    amount = legendre_weight(half - a) * legendre_weight(half - b) * legendre_weight(half - c)
                    amount = amount / legendre_weight(half) / (total + 1)
                    table[a, b, c] = amount * math.sqrt((2 * a + 1) * (2 * b + 1) * (2 * c + 1))
    return table.astype(np.float32)


def class_weights(mobility):
    metals, classes, modes = mobility.shape
    triple = jnp.asarray(triple_table(modes))
    mats = jnp.einsum("ijk,mck->mcij", triple, mobility, precision=lax.Precision.HIGHEST)
    mats = TIME_STEP * (mats + MOBILE_BASE * jnp.eye(modes, dtype=jnp.float32))
    mats = mats.reshape(metals, classes * modes, modes)
    high = lax.reduce_precision(mats, exponent_bits=8, mantissa_bits=7)
    return jnp.concatenate([high, high, mats - high], axis=2).astype(jnp.bfloat16)


def lane_neighbours(v):
    lane = lax.broadcasted_iota(jnp.int32, v.shape, v.ndim - 1)
    size = v.shape[-1]
    lower = jnp.where(lane == 0, 0.0, pltpu.roll(v, 1, v.ndim - 1))
    upper = jnp.where(lane == size - 1, 0.0, pltpu.roll(v, size - 1, v.ndim - 1))
    return lower + upper


def combine(l2, l1, mid, r1, r2, sides, vel, disp):
    spread = (16.0 / 12.0) * (l1 + r1) - (1.0 / 12.0) * (l2 + r2) - 6.5 * mid + sides
    carried = (1.0 / 3.0) * r1 + 0.5 * mid - l1 + (1.0 / 6.0) * l2
    return disp * spread - vel * carried


def spread_kernel(f_ref, lo_ref, hi_ref, vel_ref, disp_ref, out_ref):
    depth, rows, width = f_ref.shape[2:]
    blocks = out_ref.shape[0]
    part = rows // blocks
    row = lax.broadcasted_iota(jnp.int32, (rows, width), 0)

    def layer(x):
        if x < 0:
            return lo_ref[0, 0, x + 2]
        if x >= depth:
            return hi_ref[0, 0, x - depth]
        return f_ref[0, 0, x]

    zero_row = jnp.zeros((1, width), jnp.float32)
    for x in range(depth):
        mid = layer(x)
        sides = lane_neighbours(mid)
        sides += jnp.where(row == 0, 0.0, pltpu.roll(mid, 1, 0))
        sides += jnp.where(row == rows - 1, 0.0, pltpu.roll(mid, rows - 1, 0))
        value = combine(
            layer(x - 2), layer(x - 1), mid, layer(x + 1), layer(x + 2), sides, vel_ref[x], disp_ref[x]
        )
        for b in range(blocks):
            out_ref[b, 0, 0, x] = value[b * part : (b + 1) * part]
            below = value[b * part - 1 : b * part] if b else zero_row
            above = value[(b + 1) * part : (b + 1) * part + 1] if b < blocks - 1 else zero_row
            out_ref[b, 0, 0, depth, x : x + 1] = below
            out_ref[b, 0, 0, depth + 1, x : x + 1] = above


def couple(value, weights, classes, cls_row):
    modes, width = value.shape
    high = value.astype(jnp.bfloat16)
    low = (value - high.astype(jnp.float32)).astype(jnp.bfloat16)
    stacked = jnp.concatenate([high, low, high], axis=0)
    mixed = jnp.dot(weights, stacked, preferred_element_type=jnp.float32)
    picked = jnp.broadcast_to(cls_row, (modes, width))
    total = jnp.zeros((modes, width), jnp.float32)
    for c in range(classes):
        total = jnp.where(picked == c, mixed[c * modes : (c + 1) * modes], total)
    return total


def first_kernel(r_ref, w_ref, cls_ref, g_ref, l_ref, lo_ref, hi_ref):
    sources, _, each, slots, part, width = r_ref.shape
    modes = sources * each
    depth = slots - 2
    classes = w_ref.shape[1] // modes
    weights = w_ref[0]
    for s in range(slots):
        values = jnp.swapaxes(r_ref[:, 0, :, s].reshape(modes, part, width), 0, 1)
        for y in range(part):
            got = couple(values[y], weights, classes, cls_ref[s, y : y + 1])
            if s < depth:
                l_ref[0, s, y] = values[y]
                g_ref[0, s, y + 1] = got
                if s < 2:
                    lo_ref[0, s, y] = got
                if s >= depth - 2:
                    hi_ref[0, s - depth + 2, y] = got
            elif s == depth:
                g_ref[0, y, 0] = got
            else:
                g_ref[0, y, part + 1] = got


def second_kernel(g_ref, l_ref, lo_ref, hi_ref, w_ref, cls_ref, vel_ref, disp_ref, out_ref):
    _, depth, padded_rows, modes, width = g_ref.shape
    part = padded_rows - 2
    targets, _, each = out_ref.shape[:3]
    classes = w_ref.shape[1] // modes
    weights = w_ref[0]

    def at(x, y):
        if x < 0:
            return lo_ref[0, x + 2, y]
        if x >= depth:
            return hi_ref[0, x - depth, y]
        return g_ref[0, x, y + 1]

    for x in range(depth):
        rows = []
        for y in range(part):
            mid = at(x, y)
            sides = lane_neighbours(mid) + (g_ref[0, x, y] + g_ref[0, x, y + 2])
            vel = jnp.broadcast_to(vel_ref[x, y : y + 1], (modes, width))
            disp = jnp.broadcast_to(disp_ref[x, y : y + 1], (modes, width))
            value = combine(at(x - 2, y), at(x - 1, y), mid, at(x + 1, y), at(x + 2, y), sides, vel, disp)
            value += 2.0 * l_ref[0, x, y]
            rows.append(couple(value, weights, classes, cls_ref[x, y : y + 1]))
        out_ref[:, 0, :, x] = jnp.swapaxes(jnp.stack(rows), 0, 1).reshape(targets, each, part, width)


def last_kernel(f_ref, r_ref, *rest):
    out_ref = rest[-1]
    blocks = r_ref.shape[0]
    part = r_ref.shape[4]
    for b in range(blocks):
        rows = slice(b * part, (b + 1) * part)
        out_ref[0, 0, :, rows] = f_ref[0, 0, :, rows] + r_ref[b, 0, 0]


def whole(array):
    return pl.BlockSpec(array.shape, lambda *_: (0,) * array.ndim)


def params(grid):
    return pltpu.CompilerParams(dimension_semantics=("arbitrary",) * grid, vmem_limit_bytes=VMEM_LIMIT)


def cost(flops, *arrays):
    moved = sum(math.prod(a.shape) * 4 for a in arrays)
    return pl.CostEstimate(flops=flops, bytes_accessed=moved, transcendentals=0)


def on_device(field, velocity, dispersion, mobility, material, fixed_mask):
    metals, each, depth, rows, width = field.shape
    modes = mobility.shape[2]
    classes = mobility.shape[1]
    blocks = lax.axis_size("mode")
    part = rows // blocks
    space = lax.axis_size("space")
    up = [(i, i + 1) for i in range(space - 1)]
    down = [(i + 1, i) for i in range(space - 1)]

    weights = class_weights(mobility)
    here = lax.axis_index("mode") * part
    cls = jnp.where(fixed_mask == 1, classes, material)
    cls = jnp.pad(cls, ((0, 0), (1, 1), (0, 0)))
    cls = lax.dynamic_slice_in_dim(cls, here, part + 2, 1)
    cls = jnp.concatenate([cls[:, 1:-1], cls[None, :, 0], cls[None, :, -1]], axis=0)
    vel = lax.dynamic_slice_in_dim(velocity, here, part, 1)
    disp = lax.dynamic_slice_in_dim(dispersion, here, part, 1)

    def row_block(shape, count=None):
        return pl.BlockSpec(shape, lambda m: (m,) + (0,) * (len(shape) - 1))

    halos = []
    for first, count in CHUNKS:
        some = field[first : first + count]
        halos.append(
            (
                lax.ppermute(some[:, :, depth - 2 :], "space", up),
                lax.ppermute(some[:, :, :2], "space", down),
            )
        )

    arrived = []
    for (first, count), (lo, hi) in zip(CHUNKS, halos):
        sent = jax.ShapeDtypeStruct((blocks, count, each, depth + 2, part, width), jnp.float32)
        spread = pl.pallas_call(
            spread_kernel,
            grid=(count, each),
            in_specs=[
                pl.BlockSpec((1, 1, depth, rows, width), lambda m, e, first=first: (m + first, e, 0, 0, 0)),
                pl.BlockSpec((1, 1, 2, rows, width), lambda m, e: (m, e, 0, 0, 0)),
                pl.BlockSpec((1, 1, 2, rows, width), lambda m, e: (m, e, 0, 0, 0)),
                whole(velocity),
                whole(dispersion),
            ],
            out_specs=pl.BlockSpec((blocks, 1, 1, depth + 2, part, width), lambda m, e: (0, m, e, 0, 0, 0)),
            out_shape=sent,
            compiler_params=params(2),
            cost_estimate=cost(20 * math.prod(sent.shape), sent, sent),
            name="spread",
        )(field, lo, hi, velocity, dispersion)
        arrived.append(lax.all_to_all(spread, "mode", split_axis=0, concat_axis=0, tiled=True))

    mixed = []
    for (first, count), got in zip(CHUNKS, arrived):
        shapes = [
            jax.ShapeDtypeStruct((count, depth, part + 2, modes, width), jnp.float32),
            jax.ShapeDtypeStruct((count, depth, part, modes, width), jnp.float32),
            jax.ShapeDtypeStruct((count, 2, part, modes, width), jnp.float32),
            jax.ShapeDtypeStruct((count, 2, part, modes, width), jnp.float32),
        ]
        g, l, low_side, high_side = pl.pallas_call(
            first_kernel,
            grid=(count,),
            in_specs=[
                pl.BlockSpec((blocks, 1) + got.shape[2:], lambda m: (0, m, 0, 0, 0, 0)),
                pl.BlockSpec((1,) + weights.shape[1:], lambda m, first=first: (m + first, 0, 0)),
                whole(cls),
            ],
            out_specs=[row_block((1,) + s.shape[1:]) for s in shapes],
            out_shape=shapes,
            compiler_params=params(1),
            cost_estimate=cost(300 * math.prod(got.shape), got, *shapes),
            name="first",
        )(got, weights, cls)
        lo = lax.ppermute(high_side, "space", up)
        hi = lax.ppermute(low_side, "space", down)
        mixed.append((g, l, lo, hi))

    back = []
    for (first, count), (g, l, lo, hi) in zip(CHUNKS, mixed):
        sent = jax.ShapeDtypeStruct((blocks, count, each, depth, part, width), jnp.float32)
        second = pl.pallas_call(
            second_kernel,
            grid=(count,),
            in_specs=[row_block((1,) + a.shape[1:]) for a in (g, l, lo, hi)]
            + [
                pl.BlockSpec((1,) + weights.shape[1:], lambda m, first=first: (m + first, 0, 0)),
                whole(cls),
                whole(vel),
                whole(disp),
            ],
            out_specs=pl.BlockSpec((blocks, 1) + sent.shape[2:], lambda m: (0, m, 0, 0, 0, 0)),
            out_shape=sent,
            compiler_params=params(1),
            cost_estimate=cost(300 * math.prod(sent.shape), g, l, sent),
            name="second",
        )(g, l, lo, hi, weights, cls, vel, disp)
        back.append(lax.all_to_all(second, "mode", split_axis=0, concat_axis=0, tiled=True))

    out = None
    for (first, count), got in zip(CHUNKS, back):
        block = pl.BlockSpec((1, 1, depth, rows, width), lambda m, e, first=first: (m + first, e, 0, 0, 0))
        operands = [field, got]
        specs = [block, pl.BlockSpec((blocks, 1, 1, depth, part, width), lambda m, e: (0, m, e, 0, 0, 0))]
        aliases = {}
        if out is not None:
            operands.append(out)
            specs.append(pl.BlockSpec(memory_space=pl.ANY))
            aliases = {2: 0}
        out = pl.pallas_call(
            last_kernel,
            grid=(count, each),
            in_specs=specs,
            out_specs=block,
            out_shape=jax.ShapeDtypeStruct(field.shape, jnp.float32),
            input_output_aliases=aliases,
            compiler_params=params(2),
            cost_estimate=cost(math.prod(got.shape), got, got, got),
            name="last",
        )(*operands)
    return out


def solution(mesh):
    in_specs = (
        P(None, "mode", "space", None, None),
        P("space", None, None),
        P("space", None, None),
        P(),
        P("space", None, None),
        P("space", None, None),
    )
    out_specs = P(None, "mode", "space", None, None)
    return jax.shard_map(
        on_device, mesh=mesh, in_specs=in_specs, out_specs=out_specs, check_vma=False
    )
```

time: 357 us -> 196 us (0.55)
  matrix products: 90.6 us -> 1.04 us
  blocking collectives: 66.7 us -> 0 us
  starting transfers between devices: 27.2 us -> 63.8 us
  local copies, waits for them, and re-layouts: 55.2 us -> 22.9 us
  Pallas kernels: 0 us -> 27.2 us
  other arithmetic: 21.2 us -> 2.75 us
  waiting for transfers between devices: 90.7 us -> 76.4 us
    dot_general x17 -> x1, matrix products: 90.6 us -> 1.04 us  [class_weights(): jnp.einsum('ijk,mck->mcij', triple, mobility, precision=lax.Precision.HIG...]
    all_to_all x2 -> x0, blocking collectives: 66.7 us -> none  [the longest x1 33.5 us: on_device(): lax.all_to_all(mixed_cells, 'mode', split_axis=1, concat_axis=3, tiled=True)]
    all_to_all x2 -> x6, waiting for transfers between devices: 54.5 us -> 5.4 us  [the longest x3 5.39 us: on_device(): lax.all_to_all(second, 'mode', split_axis=0, concat_axis=0, tiled=True)]
    ppermute x4 -> x12, waiting for transfers between devices: 36.1 us -> 71 us  [the longest x3 26.8 us: on_device(): hi = lax.ppermute(low_side, 'space', down)]
    pallas_call x0 -> x12, Pallas kernels: none -> 27.2 us  [the longest x3 8.97 us: on_device(): pl.pallas_call(first_kernel, grid=(count,), in_specs=[pl.BlockSpec((block...]
    all_to_all x2 -> x6, starting transfers between devices: 8.41 us -> 30.9 us  [the longest x3 16 us: on_device(): lax.all_to_all(second, 'mode', split_axis=0, concat_axis=0, tiled=True)]
    all_to_all x6 -> x0, local copies, waits for them, and re-layouts: 18.3 us -> none  [the longest x4 16.4 us: on_device(): lax.all_to_all(operated, 'mode', split_axis=3, concat_axis=1, tiled=True)]
    mul x18 -> x1, local copies, waits for them, and re-layouts: 14.9 us -> 0.14 us  [class_weights(): mats = TIME_STEP * (mats + MOBILE_BASE * jnp.eye(modes, dtype=jnp.float32))]
  transfers between devices with their start and end apart: 6 -> 18, of which waited for: 6 -> 13; matrix products, arithmetic and copies ran while one was open for 3% -> 3% of each run, Pallas kernels for 0% -> 12%
where the time goes in v1:
time: 196 us; the launch traced here: 194 us
  waiting for transfers between devices  76.4 us (39%)
  starting transfers between devices  63.8 us (33%)
  Pallas kernels  27.2 us (14%)
  local copies, waits for them, and re-layouts  22.9 us (12%)
  other arithmetic  2.75 us (1%)
    ppermute x3, waiting for transfers between devices, on_device(): hi = lax.ppermute(low_side, 'space', down)  26.8 us
    ppermute x3, waiting for transfers between devices, on_device(): lax.ppermute(some[:, :, depth - 2:], 'space', up)  19.9 us
    unnamed x40, local copies, waits for them, and re-layouts  17.8 us
    ppermute x3, waiting for transfers between devices, on_device(): lax.ppermute(some[:, :, :2], 'space', down)  16.6 us
    all_to_all x3, starting transfers between devices, on_device(): lax.all_to_all(second, 'mode', split_axis=0, concat_axis=0, tiled=True)  16 us
    all_to_all x3, starting transfers between devices, on_device(): lax.all_to_all(spread, 'mode', split_axis=0, concat_axis=0, tiled=True)  14.8 us
    ppermute x3, starting transfers between devices, on_device(): lax.ppermute(some[:, :, depth - 2:], 'space', up)  12.5 us
    pallas_call x3, Pallas kernels, on_device(): pl.pallas_call(first_kernel, grid=(count,), in_specs=[pl.BlockSpec((block...  8.97 us
  transfers between devices with their start and end apart: 18, of which 13 were waited for; matrix products, arithmetic and copies ran while one was open for 3% of the time, Pallas kernels for 12%

profile of v1, /device:TPU:71, one launch (start us, length us, event | category | flops | bytes accessed | tf_op | source)
XLA Modules:
  0.0 194.3 jit_solution(12530968670682931121)
XLA Ops:
  2.4 6.6 %collective-permute-start.8 = (f32[1,2,2,64,256]{4,3,2,1,0:T(8,128)S(1)}, f32[1,2,2,64,256]{4,3,2,1,0:T(8,128)S(1)}, u32[]{:S(2)}, u32[]{:S(2)}) collective-permute-start(f32[1,2,2,64,256]{4,3,2,1,0:T(8,128)S(1)} %get-tuple-element.30), channel_id=1, source_target_pairs={{0,8},{8,16},{16,24},{24,32},{32,40},{40,48},{48,56},{56,64},{64,7... | collective-permute-start | bytes 786440 | tf_op jit(solution)/shard_map/ppermute | solution.py:203
  11.0 4.1 %collective-permute-done.8.lo_ref = f32[1,2,2,64,256]{4,3,2,1,0:T(8,128)S(1)} collective-permute-done((f32[1,2,2,64,256]{4,3,2,1,0:T(8,128)S(1)}, f32[1,2,2,64,256]{4,3,2,1,0:T(8,128)S(1)}, u32[]{:S(2)}, u32[]{:S(2)}) %collective-permute-start.8) | collective-permute-done | bytes 262176 | tf_op jit(solution)/shard_map/ppermute | solution.py:203
  15.0 8.6 %collective-permute-done.9.hi_ref = f32[1,2,2,64,256]{4,3,2,1,0:T(8,128)S(1)} collective-permute-done((f32[1,2,2,64,256]{4,3,2,1,0:T(8,128)S(1)}, f32[1,2,2,64,256]{4,3,2,1,0:T(8,128)S(1)}, u32[]{:S(2)}, u32[]{:S(2)}) %collective-permute-start.9) | collective-permute-done | bytes 262176 | tf_op jit(solution)/shard_map/ppermute | solution.py:204
  28.1 4.3 %all-to-all-start.4 = ((f32[8,1,2,10,8,256]{5,4,3,2,1,0:T(8,128)}), f32[8,1,2,10,8,256]{5,4,3,2,1,0:T(8,128)}, u32[]{:S(2)}, u32[]{:S(2)}) async-start(f32[8,1,2,10,8,256]{5,4,3,2,1,0:T(8,128)} %copy-done.4), calls=%async_computation.4 | async-start | bytes 2621440 | tf_op jit(solution)/shard_map/all_to_all | solution.py:227
  36.8 8.4 %collective-permute-done.4.lo_ref = f32[1,2,2,64,256]{4,3,2,1,0:T(8,128)S(1)} collective-permute-done((f32[1,2,2,64,256]{4,3,2,1,0:T(8,128)}, f32[1,2,2,64,256]{4,3,2,1,0:T(8,128)S(1)}, u32[]{:S(2)}, u32[]{:S(2)}) %collective-permute-start.4) | collective-permute-done | bytes 262176 | tf_op jit(solution)/shard_map/ppermute | solution.py:203
  52.4 6.0 %all-to-all-start.2 = ((f32[8,1,2,10,8,256]{5,4,3,2,1,0:T(8,128)}), f32[8,1,2,10,8,256]{5,4,3,2,1,0:T(8,128)}, u32[]{:S(2)}, u32[]{:S(2)}) async-start(f32[8,1,2,10,8,256]{5,4,3,2,1,0:T(8,128)} %copy-done.3), calls=%async_computation.2 | async-start | bytes 2621440 | tf_op jit(solution)/shard_map/all_to_all | solution.py:227
  58.4 4.1 %collective-permute-start = (f32[1,2,2,64,256]{4,3,2,1,0:T(8,128)}, f32[1,2,2,64,256]{4,3,2,1,0:T(8,128)S(1)}, u32[]{:S(2)}, u32[]{:S(2)}) collective-permute-start(f32[1,2,2,64,256]{4,3,2,1,0:T(8,128)} %get-tuple-element.34), channel_id=1, source_target_pairs={{0,8},{8,16},{16,24},{24,32},{32,40},{40,48},{48,56},{56,64},{64,7... | collective-permute-start | bytes 786440 | tf_op jit(solution)/shard_map/ppermute | solution.py:203
  64.4 7.5 %collective-permute-done.lo_ref = f32[1,2,2,64,256]{4,3,2,1,0:T(8,128)S(1)} collective-permute-done((f32[1,2,2,64,256]{4,3,2,1,0:T(8,128)}, f32[1,2,2,64,256]{4,3,2,1,0:T(8,128)S(1)}, u32[]{:S(2)}, u32[]{:S(2)}) %collective-permute-start) | collective-permute-done | bytes 262176 | tf_op jit(solution)/shard_map/ppermute | solution.py:203
  71.9 5.3 %collective-permute-done.1.hi_ref = f32[1,2,2,64,256]{4,3,2,1,0:T(8,128)S(1)} collective-permute-done((f32[1,2,2,64,256]{4,3,2,1,0:T(8,128)S(1)}, f32[1,2,2,64,256]{4,3,2,1,0:T(8,128)S(1)}, u32[]{:S(2)}, u32[]{:S(2)}) %collective-permute-start.1) | collective-permute-done | bytes 262176 | tf_op jit(solution)/shard_map/ppermute | solution.py:204
  81.7 4.5 %all-to-all-start = ((f32[8,1,2,10,8,256]{5,4,3,2,1,0:T(8,128)}), f32[8,1,2,10,8,256]{5,4,3,2,1,0:T(8,128)}, u32[]{:S(2)}, u32[]{:S(2)}) async-start(f32[8,1,2,10,8,256]{5,4,3,2,1,0:T(8,128)} %copy-done.2), calls=%async_computation | async-start | bytes 2621440 | tf_op jit(solution)/shard_map/all_to_all | solution.py:227
  92.6 3.3 %first.5 = (f32[1,8,10,16,256]{4,3,2,1,0:T(8,128)S(1)}, f32[1,8,8,16,256]{4,3,2,1,0:T(8,128)S(1)}, f32[1,2,8,16,256]{4,3,2,1,0:T(8,128)}, f32[1,2,8,16,256]{4,3,2,1,0:T(8,128)}) custom-call(f32[8,1,2,10,8,256]{5,4,3,2,1,0:T(8,128)} %all-to-all-done.4.r_ref, bf16[3,128,48]{2,1,0:T(8,128)(2,1)S(1)} %copy.27.w_ref, s32[10,8,256]{2,1,0:T(8,128)S(1)} %pad_add_fusion.cls_ref), custom_call_target="tpu_custom_call" | custom-call | flops 98304000 | bytes 4194304 | tf_op jit(solution)/shard_map/first/pallas_call | solution.py:237
  98.0 3.4 %collective-permute-start.10 = (f32[1,2,8,16,256]{4,3,2,1,0:T(8,128)}, f32[1,2,8,16,256]{4,3,2,1,0:T(8,128)}, u32[]{:S(2)}, u32[]{:S(2)}) collective-permute-start(f32[1,2,8,16,256]{4,3,2,1,0:T(8,128)} %get-tuple-element.27), channel_id=1, source_target_pairs={{0,8},{8,16},{16,24},{24,32},{32,40},{40,48},{48,56},{56,64},{64,7... | collective-permute-start | bytes 786440 | tf_op jit(solution)/shard_map/ppermute | solution.py:251
  105.0 9.0 %collective-permute-done.11.hi_ref = f32[1,2,8,16,256]{4,3,2,1,0:T(8,128)} collective-permute-done((f32[1,2,8,16,256]{4,3,2,1,0:T(8,128)}, f32[1,2,8,16,256]{4,3,2,1,0:T(8,128)}, u32[]{:S(2)}, u32[]{:S(2)}) %collective-permute-start.11) | collective-permute-done | bytes 262176 | tf_op jit(solution)/shard_map/ppermute | solution.py:252
  116.6 3.3 %second.5 = f32[8,1,2,8,8,256]{5,4,3,2,1,0:T(8,128)S(1)} custom-call(f32[1,8,10,16,256]{4,3,2,1,0:T(8,128)S(1)} %copy-done.15, f32[1,8,8,16,256]{4,3,2,1,0:T(8,128)S(1)} %copy-done.17, f32[1,2,8,16,256]{4,3,2,1,0:T(8,128)} %collective-permute-done.10.lo_ref, f32[1,2,8,16,256]{4,3,2,1,0:T(8,128)} %collective-permute-done.11.hi_ref, ...), custom_call_target="tpu_custom_call" | custom-call | flops 78643200 | bytes 3407872 | tf_op jit(solution)/shard_map/second/pallas_call | solution.py:258
  120.9 6.9 %all-to-all-start.5 = ((f32[8,1,2,8,8,256]{5,4,3,2,1,0:T(8,128)}), f32[8,1,2,8,8,256]{5,4,3,2,1,0:T(8,128)}, u32[]{:S(2)}, u32[]{:S(2)}) async-start(f32[8,1,2,8,8,256]{5,4,3,2,1,0:T(8,128)} %copy-done.12), calls=%async_computation.5 | async-start | bytes 2097152 | tf_op jit(solution)/shard_map/all_to_all | solution.py:274
  127.8 2.8 %first.4 = (f32[1,8,10,16,256]{4,3,2,1,0:T(8,128)S(1)}, f32[1,8,8,16,256]{4,3,2,1,0:T(8,128)S(1)}, f32[1,2,8,16,256]{4,3,2,1,0:T(8,128)S(1)}, f32[1,2,8,16,256]{4,3,2,1,0:T(8,128)S(1)}) custom-call(f32[8,1,2,10,8,256]{5,4,3,2,1,0:T(8,128)} %all-to-all-done.2.r_ref, bf16[3,128,48]{2,1,0:T(8,128)(2,1)S(1)} %copy.27.w_ref, s32[10,8,256]{2,1,0:T(8,128)S(1)} %pad_add_fusion.cls_ref), custom_call_target="tpu_custom_call" | custom-call | flops 98304000 | bytes 4194304 | tf_op jit(solution)/shard_map/first/pallas_call | solution.py:237
  135.2 3.8 %collective-permute-done.6.lo_ref = f32[1,2,8,16,256]{4,3,2,1,0:T(8,128)S(1)} collective-permute-done((f32[1,2,8,16,256]{4,3,2,1,0:T(8,128)S(1)}, f32[1,2,8,16,256]{4,3,2,1,0:T(8,128)S(1)}, u32[]{:S(2)}, u32[]{:S(2)}) %collective-permute-start.6) | collective-permute-done | bytes 262176 | tf_op jit(solution)/shard_map/ppermute | solution.py:251
  138.9 8.5 %collective-permute-done.7.hi_ref = f32[1,2,8,16,256]{4,3,2,1,0:T(8,128)S(1)} collective-permute-done((f32[1,2,8,16,256]{4,3,2,1,0:T(8,128)S(1)}, f32[1,2,8,16,256]{4,3,2,1,0:T(8,128)S(1)}, u32[]{:S(2)}, u32[]{:S(2)}) %collective-permute-start.7) | collective-permute-done | bytes 262176 | tf_op jit(solution)/shard_map/ppermute | solution.py:252
  150.7 4.6 %all-to-all-start.3 = ((f32[8,1,2,8,8,256]{5,4,3,2,1,0:T(8,128)}), f32[8,1,2,8,8,256]{5,4,3,2,1,0:T(8,128)}, u32[]{:S(2)}, u32[]{:S(2)}) async-start(f32[8,1,2,8,8,256]{5,4,3,2,1,0:T(8,128)} %copy-done.11), calls=%async_computation.3 | async-start | bytes 2097152 | tf_op jit(solution)/shard_map/all_to_all | solution.py:274
  155.3 2.8 %first.3 = (f32[1,8,10,16,256]{4,3,2,1,0:T(8,128)S(1)}, f32[1,8,8,16,256]{4,3,2,1,0:T(8,128)S(1)}, f32[1,2,8,16,256]{4,3,2,1,0:T(8,128)S(1)}, f32[1,2,8,16,256]{4,3,2,1,0:T(8,128)S(1)}) custom-call(f32[8,1,2,10,8,256]{5,4,3,2,1,0:T(8,128)} %all-to-all-done.r_ref, bf16[3,128,48]{2,1,0:T(8,128)(2,1)S(1)} %copy.27.w_ref, s32[10,8,256]{2,1,0:T(8,128)S(1)} %pad_add_fusion.cls_ref), custom_call_target="tpu_custom_call" | custom-call | flops 98304000 | bytes 4194304 | tf_op jit(solution)/shard_map/first/pallas_call | solution.py:237
  162.4 3.1 %collective-permute-done.2.lo_ref = f32[1,2,8,16,256]{4,3,2,1,0:T(8,128)S(1)} collective-permute-done((f32[1,2,8,16,256]{4,3,2,1,0:T(8,128)S(1)}, f32[1,2,8,16,256]{4,3,2,1,0:T(8,128)S(1)}, u32[]{:S(2)}, u32[]{:S(2)}) %collective-permute-start.2) | collective-permute-done | bytes 262176 | tf_op jit(solution)/shard_map/ppermute | solution.py:251
  165.6 9.3 %collective-permute-done.3.hi_ref = f32[1,2,8,16,256]{4,3,2,1,0:T(8,128)S(1)} collective-permute-done((f32[1,2,8,16,256]{4,3,2,1,0:T(8,128)S(1)}, f32[1,2,8,16,256]{4,3,2,1,0:T(8,128)S(1)}, u32[]{:S(2)}, u32[]{:S(2)}) %collective-permute-start.3) | collective-permute-done | bytes 262176 | tf_op jit(solution)/shard_map/ppermute | solution.py:252
  178.2 4.5 %all-to-all-start.1 = ((f32[8,1,2,8,8,256]{5,4,3,2,1,0:T(8,128)}), f32[8,1,2,8,8,256]{5,4,3,2,1,0:T(8,128)}, u32[]{:S(2)}, u32[]{:S(2)}) async-start(f32[8,1,2,8,8,256]{5,4,3,2,1,0:T(8,128)} %copy-done.13), calls=%async_computation.1 | async-start | bytes 2097152 | tf_op jit(solution)/shard_map/all_to_all | solution.py:274
  186.9 5.4 %all-to-all-done.1.r_ref = f32[8,1,2,8,8,256]{5,4,3,2,1,0:T(8,128)} async-done(((f32[8,1,2,8,8,256]{5,4,3,2,1,0:T(8,128)}), f32[8,1,2,8,8,256]{5,4,3,2,1,0:T(8,128)}, u32[]{:S(2)}, u32[]{:S(2)}) %all-to-all-start.1) | async-done | bytes 1048608 | tf_op jit(solution)/shard_map/all_to_all | solution.py:274
  (78 shorter events, 64.1 us)
Async XLA Ops:
  0.0 89.6 %copy-start = (f32[3,8,16]{2,1,0:T(8,128)S(1)}, f32[3,8,16]{2,1,0:T(8,128)}, u32[]{:S(2)}) copy-start(f32[3,8,16]{2,1,0:T(8,128)} %param.10) | copy-start | bytes 4612
  0.0 23.6 %copy-start.1 = (f32[3,2,8,64,256]{4,3,2,1,0:T(8,128)S(1)}, f32[3,2,8,64,256]{4,3,2,1,0:T(8,128)}, u32[]{:S(2)}) copy-start(f32[3,2,8,64,256]{4,3,2,1,0:T(8,128)} %f_ref.11) | copy-start | bytes 9437188
  2.4 12.6 %collective-permute-start.8 = (f32[1,2,2,64,256]{4,3,2,1,0:T(8,128)S(1)}, f32[1,2,2,64,256]{4,3,2,1,0:T(8,128)S(1)}, u32[]{:S(2)}, u32[]{:S(2)}) collective-permute-start(f32[1,2,2,64,256]{4,3,2,1,0:T(8,128)S(1)} %get-tuple-element.30), channel_id=1, source_target_pairs={{0,8},{8,16},{16,24},{24,32},{32,40},{40,48},{48,56},{56,64},{64,7... | collective-permute-start | bytes 786440 | tf_op jit(solution)/shard_map/ppermute | solution.py:203
  9.0 14.6 %collective-permute-start.9 = (f32[1,2,2,64,256]{4,3,2,1,0:T(8,128)S(1)}, f32[1,2,2,64,256]{4,3,2,1,0:T(8,128)S(1)}, u32[]{:S(2)}, u32[]{:S(2)}) collective-permute-start(f32[1,2,2,64,256]{4,3,2,1,0:T(8,128)S(1)} %get-tuple-element.29), channel_id=1, source_target_pairs={{8,0},{16,8},{24,16},{32,24},{40,32},{48,40},{56,48},{64,56},{72,6... | collective-permute-start | bytes 786440 | tf_op jit(solution)/shard_map/ppermute | solution.py:204
  28.1 24.3 %all-to-all-start.4 = ((f32[8,1,2,10,8,256]{5,4,3,2,1,0:T(8,128)}), f32[8,1,2,10,8,256]{5,4,3,2,1,0:T(8,128)}, u32[]{:S(2)}, u32[]{:S(2)}) async-start(f32[8,1,2,10,8,256]{5,4,3,2,1,0:T(8,128)} %copy-done.4), calls=%async_computation.4 | async-start | bytes 2621440 | tf_op jit(solution)/shard_map/all_to_all | solution.py:227
  32.4 12.7 %collective-permute-start.4 = (f32[1,2,2,64,256]{4,3,2,1,0:T(8,128)}, f32[1,2,2,64,256]{4,3,2,1,0:T(8,128)S(1)}, u32[]{:S(2)}, u32[]{:S(2)}) collective-permute-start(f32[1,2,2,64,256]{4,3,2,1,0:T(8,128)} %get-tuple-element.32), channel_id=1, source_target_pairs={{0,8},{8,16},{16,24},{24,32},{32,40},{40,48},{48,56},{56,64},{64,7... | collective-permute-start | bytes 786440 | tf_op jit(solution)/shard_map/ppermute | solution.py:203
  34.4 13.5 %collective-permute-start.5 = (f32[1,2,2,64,256]{4,3,2,1,0:T(8,128)}, f32[1,2,2,64,256]{4,3,2,1,0:T(8,128)S(1)}, u32[]{:S(2)}, u32[]{:S(2)}) collective-permute-start(f32[1,2,2,64,256]{4,3,2,1,0:T(8,128)} %get-tuple-element.31), channel_id=1, source_target_pairs={{8,0},{16,8},{24,16},{32,24},{40,32},{48,40},{56,48},{64,56},{72,6... | collective-permute-start | bytes 786440 | tf_op jit(solution)/shard_map/ppermute | solution.py:204
  51.3 1.1 copy-start.3
  52.4 29.3 %all-to-all-start.2 = ((f32[8,1,2,10,8,256]{5,4,3,2,1,0:T(8,128)}), f32[8,1,2,10,8,256]{5,4,3,2,1,0:T(8,128)}, u32[]{:S(2)}, u32[]{:S(2)}) async-start(f32[8,1,2,10,8,256]{5,4,3,2,1,0:T(8,128)} %copy-done.3), calls=%async_computation.2 | async-start | bytes 2621440 | tf_op jit(solution)/shard_map/all_to_all | solution.py:227
  58.4 13.5 %collective-permute-start = (f32[1,2,2,64,256]{4,3,2,1,0:T(8,128)}, f32[1,2,2,64,256]{4,3,2,1,0:T(8,128)S(1)}, u32[]{:S(2)}, u32[]{:S(2)}) collective-permute-start(f32[1,2,2,64,256]{4,3,2,1,0:T(8,128)} %get-tuple-element.34), channel_id=1, source_target_pairs={{0,8},{8,16},{16,24},{24,32},{32,40},{40,48},{48,56},{56,64},{64,7... | collective-permute-start | bytes 786440 | tf_op jit(solution)/shard_map/ppermute | solution.py:203
  62.5 14.7 %collective-permute-start.1 = (f32[1,2,2,64,256]{4,3,2,1,0:T(8,128)S(1)}, f32[1,2,2,64,256]{4,3,2,1,0:T(8,128)S(1)}, u32[]{:S(2)}, u32[]{:S(2)}) collective-permute-start(f32[1,2,2,64,256]{4,3,2,1,0:T(8,128)S(1)} %get-tuple-element.33), channel_id=1, source_target_pairs={{8,0},{16,8},{24,16},{32,24},{40,32},{48,40},{56,48},{64,56},{72,6... | collective-permute-start | bytes 786440 | tf_op jit(solution)/shard_map/ppermute | solution.py:204
  81.7 39.2 %all-to-all-start = ((f32[8,1,2,10,8,256]{5,4,3,2,1,0:T(8,128)}), f32[8,1,2,10,8,256]{5,4,3,2,1,0:T(8,128)}, u32[]{:S(2)}, u32[]{:S(2)}) async-start(f32[8,1,2,10,8,256]{5,4,3,2,1,0:T(8,128)} %copy-done.2), calls=%async_computation | async-start | bytes 2621440 | tf_op jit(solution)/shard_map/all_to_all | solution.py:227
  86.2 3.4 %copy-start.19 = (f32[16,16,16,1]{2,1,3,0:T(8,128)S(1)}, f32[16,16,16,1]{2,1,3,0:T(8,128)}, u32[]{:S(2)}) copy-start(f32[16,16,16,1]{2,1,3,0:T(8,128)} %constant.30) | copy-start | bytes 49156
  98.0 7.0 %collective-permute-start.10 = (f32[1,2,8,16,256]{4,3,2,1,0:T(8,128)}, f32[1,2,8,16,256]{4,3,2,1,0:T(8,128)}, u32[]{:S(2)}, u32[]{:S(2)}) collective-permute-start(f32[1,2,8,16,256]{4,3,2,1,0:T(8,128)} %get-tuple-element.27), channel_id=1, source_target_pairs={{0,8},{8,16},{16,24},{24,32},{32,40},{40,48},{48,56},{56,64},{64,7... | collective-permute-start | bytes 786440 | tf_op jit(solution)/shard_map/ppermute | solution.py:251
  101.4 12.6 %collective-permute-start.11 = (f32[1,2,8,16,256]{4,3,2,1,0:T(8,128)}, f32[1,2,8,16,256]{4,3,2,1,0:T(8,128)}, u32[]{:S(2)}, u32[]{:S(2)}) collective-permute-start(f32[1,2,8,16,256]{4,3,2,1,0:T(8,128)} %get-tuple-element.28), channel_id=1, source_target_pairs={{8,0},{16,8},{24,16},{32,24},{40,32},{48,40},{56,48},{64,56},{72,6... | collective-permute-start | bytes 786440 | tf_op jit(solution)/shard_map/ppermute | solution.py:252
  114.0 1.3 copy-start.15
  115.3 1.2 copy-start.17
  120.9 29.8 %all-to-all-start.5 = ((f32[8,1,2,8,8,256]{5,4,3,2,1,0:T(8,128)}), f32[8,1,2,8,8,256]{5,4,3,2,1,0:T(8,128)}, u32[]{:S(2)}, u32[]{:S(2)}) async-start(f32[8,1,2,8,8,256]{5,4,3,2,1,0:T(8,128)} %copy-done.12), calls=%async_computation.5 | async-start | bytes 2097152 | tf_op jit(solution)/shard_map/all_to_all | solution.py:274
  130.6 8.3 %collective-permute-start.6 = (f32[1,2,8,16,256]{4,3,2,1,0:T(8,128)S(1)}, f32[1,2,8,16,256]{4,3,2,1,0:T(8,128)S(1)}, u32[]{:S(2)}, u32[]{:S(2)}) collective-permute-start(f32[1,2,8,16,256]{4,3,2,1,0:T(8,128)S(1)} %get-tuple-element.23), channel_id=1, source_target_pairs={{0,8},{8,16},{16,24},{24,32},{32,40},{40,48},{48,56},{56,64},{64,7... | collective-permute-start | bytes 786440 | tf_op jit(solution)/shard_map/ppermute | solution.py:251
  132.6 14.8 %collective-permute-start.7 = (f32[1,2,8,16,256]{4,3,2,1,0:T(8,128)S(1)}, f32[1,2,8,16,256]{4,3,2,1,0:T(8,128)S(1)}, u32[]{:S(2)}, u32[]{:S(2)}) collective-permute-start(f32[1,2,8,16,256]{4,3,2,1,0:T(8,128)S(1)} %get-tuple-element.24), channel_id=1, source_target_pairs={{8,0},{16,8},{24,16},{32,24},{40,32},{48,40},{56,48},{64,56},{72,6... | collective-permute-start | bytes 786440 | tf_op jit(solution)/shard_map/ppermute | solution.py:252
  150.7 27.5 %all-to-all-start.3 = ((f32[8,1,2,8,8,256]{5,4,3,2,1,0:T(8,128)}), f32[8,1,2,8,8,256]{5,4,3,2,1,0:T(8,128)}, u32[]{:S(2)}, u32[]{:S(2)}) async-start(f32[8,1,2,8,8,256]{5,4,3,2,1,0:T(8,128)} %copy-done.11), calls=%async_computation.3 | async-start | bytes 2097152 | tf_op jit(solution)/shard_map/all_to_all | solution.py:274
  158.1 7.5 %collective-permute-start.2 = (f32[1,2,8,16,256]{4,3,2,1,0:T(8,128)S(1)}, f32[1,2,8,16,256]{4,3,2,1,0:T(8,128)S(1)}, u32[]{:S(2)}, u32[]{:S(2)}) collective-permute-start(f32[1,2,8,16,256]{4,3,2,1,0:T(8,128)S(1)} %get-tuple-element.19), channel_id=1, source_target_pairs={{0,8},{8,16},{16,24},{24,32},{32,40},{40,48},{48,56},{56,64},{64,7... | collective-permute-start | bytes 786440 | tf_op jit(solution)/shard_map/ppermute | solution.py:251
  160.1 14.8 %collective-permute-start.3 = (f32[1,2,8,16,256]{4,3,2,1,0:T(8,128)S(1)}, f32[1,2,8,16,256]{4,3,2,1,0:T(8,128)S(1)}, u32[]{:S(2)}, u32[]{:S(2)}) collective-permute-start(f32[1,2,8,16,256]{4,3,2,1,0:T(8,128)S(1)} %get-tuple-element.20), channel_id=1, source_target_pairs={{8,0},{16,8},{24,16},{32,24},{40,32},{48,40},{56,48},{64,56},{72,6... | collective-permute-start | bytes 786440 | tf_op jit(solution)/shard_map/ppermute | solution.py:252
  178.2 14.1 %all-to-all-start.1 = ((f32[8,1,2,8,8,256]{5,4,3,2,1,0:T(8,128)}), f32[8,1,2,8,8,256]{5,4,3,2,1,0:T(8,128)}, u32[]{:S(2)}, u32[]{:S(2)}) async-start(f32[8,1,2,8,8,256]{5,4,3,2,1,0:T(8,128)} %copy-done.13), calls=%async_computation.1 | async-start | bytes 2097152 | tf_op jit(solution)/shard_map/all_to_all | solution.py:274
  (14 other events, 14.2 us)

commit v2 on v1

v2 whole, which is shorter than its diff:
```python
import functools
import math

import jax
import jax.numpy as jnp
import numpy as np
from jax import lax
from jax.experimental import pallas as pl
from jax.experimental.pallas import tpu as pltpu
from jax.sharding import PartitionSpec as P


TIME_STEP = 0.1
MOBILE_BASE = 0.7
VMEM_LIMIT = 30 * 1024 * 1024


def legendre_weight(order):
    return math.comb(2 * order, order) / 4.0**order


def triple_table(terms_count):
    table = np.zeros((terms_count,) * 3, np.float64)
    for a in range(terms_count):
        for b in range(terms_count):
            for c in range(terms_count):
                total = a + b + c
                half = total // 2
                if total % 2 == 0 and max(a, b, c) <= half:
                    amount = legendre_weight(half - a) * legendre_weight(half - b) * legendre_weight(half - c)
                    amount = amount / legendre_weight(half) / (total + 1)
                    table[a, b, c] = amount * math.sqrt((2 * a + 1) * (2 * b + 1) * (2 * c + 1))
    return table.astype(np.float32)


def class_weights(mobility):
    metals, classes, modes = mobility.shape
    triple = jnp.asarray(triple_table(modes))
    mats = jnp.einsum("ijk,mck->mcij", triple, mobility, precision=lax.Precision.HIGHEST)
    mats = TIME_STEP * (mats + MOBILE_BASE * jnp.eye(modes, dtype=jnp.float32))
    mats = mats.reshape(metals, classes * modes, modes)
    high = lax.reduce_precision(mats, exponent_bits=8, mantissa_bits=7)
    return jnp.concatenate([high, high, mats - high], axis=2).astype(jnp.bfloat16)


def lane_neighbours(v):
    lane = lax.broadcasted_iota(jnp.int32, v.shape, v.ndim - 1)
    size = v.shape[-1]
    lower = jnp.where(lane == 0, 0.0, pltpu.roll(v, 1, v.ndim - 1))
    upper = jnp.where(lane == size - 1, 0.0, pltpu.roll(v, size - 1, v.ndim - 1))
    return lower + upper


def combine(l2, l1, mid, r1, r2, sides, vel, disp):
    spread = (16.0 / 12.0) * (l1 + r1) - (1.0 / 12.0) * (l2 + r2) - 6.5 * mid + sides
    carried = (1.0 / 3.0) * r1 + 0.5 * mid - l1 + (1.0 / 6.0) * l2
    return disp * spread - vel * carried


def spread_kernel(layers, f_ref, vel_ref, disp_ref, *rest):
    lo_ref, hi_ref = rest[:2] if len(rest) == 3 else (None, None)
    out_ref = rest[-1]
    depth, rows, width = f_ref.shape[2:]
    blocks = out_ref.shape[0]
    part = rows // blocks
    count = len(layers)
    row = lax.broadcasted_iota(jnp.int32, (rows, width), 0)

    def layer(e, x):
        if x < 0:
            return lo_ref[0, e, x + 2]
        if x >= depth:
            return hi_ref[0, e, x - depth]
        return f_ref[0, e, x]

    zero_row = jnp.zeros((1, width), jnp.float32)
    for e in range(f_ref.shape[1]):
        for i, x in enumerate(layers):
            mid = layer(e, x)
            sides = lane_neighbours(mid)
            sides += jnp.where(row == 0, 0.0, pltpu.roll(mid, 1, 0))
            sides += jnp.where(row == rows - 1, 0.0, pltpu.roll(mid, rows - 1, 0))
            around = [layer(e, x + k) for k in (-2, -1, 0, 1, 2)]
            value = combine(*around, sides, vel_ref[x], disp_ref[x])
            for b in range(blocks):
                out_ref[b, 0, e, i] = value[b * part : (b + 1) * part]
                below = value[b * part - 1 : b * part] if b else zero_row
                above = value[(b + 1) * part : (b + 1) * part + 1] if b < blocks - 1 else zero_row
                out_ref[b, 0, e, count, i : i + 1] = below
                out_ref[b, 0, e, count, count + i : count + i + 1] = above


def couple(value, weights, classes, cls_row):
    modes, width = value.shape
    high = value.astype(jnp.bfloat16)
    low = (value - high.astype(jnp.float32)).astype(jnp.bfloat16)
    stacked = jnp.concatenate([high, low, high], axis=0)
    mixed = jnp.dot(weights, stacked, preferred_element_type=jnp.float32)
    picked = jnp.broadcast_to(cls_row, (modes, width))
    total = jnp.zeros((modes, width), jnp.float32)
    for c in range(classes):
        total = jnp.where(picked == c, mixed[c * modes : (c + 1) * modes], total)
    return total


def first_kernel(layers, r_ref, w_ref, cls_ref, l_ref, beside_ref, *g_refs):
    sources, _, each, slots, part, width = r_ref.shape
    modes = sources * each
    count = len(layers)
    share = count // len(g_refs)
    classes = w_ref.shape[1] // modes
    weights = w_ref[0]
    for s in range(slots):
        values = jnp.swapaxes(r_ref[:, 0, :, s].reshape(modes, part, width), 0, 1)
        for y in range(part):
            if s < count:
                x, row = layers[s], y + 1
            else:
                x, row = layers[y % count], (part + 1) * (y // count)
            got = couple(values[y], weights, classes, cls_ref[x, row : row + 1])
            if s < count:
                l_ref[0, s, y] = values[y]
                g_refs[s // share][0, s % share, y] = got
            else:
                beside_ref[0, y % count, y // count] = got


def second_kernel(layers, g_ref, low_ref, high_ref, l_ref, beside_ref, w_ref, cls_ref, vel_ref, disp_ref, *rest):
    lo_ref, hi_ref = rest[:2] if len(rest) == 3 else (None, None)
    out_ref = rest[-1]
    inner, part, modes, width = g_ref.shape[1:]
    depth = inner + 4
    targets, _, each = out_ref.shape[:3]
    classes = w_ref.shape[1] // modes
    weights = w_ref[0]

    def at(x, y):
        if x < 0:
            return lo_ref[0, x + 2, y]
        if x < 2:
            return low_ref[0, x, y]
        if x < depth - 2:
            return g_ref[0, x - 2, y]
        if x < depth:
            return high_ref[0, x - depth + 2, y]
        return hi_ref[0, x - depth, y]

    for i, x in enumerate(layers):
        rows = []
        for y in range(part):
            mid = at(x, y)
            below = at(x, y - 1) if y else beside_ref[0, i, 0]
            above = at(x, y + 1) if y < part - 1 else beside_ref[0, i, 1]
            sides = lane_neighbours(mid) + (below + above)
            vel = jnp.broadcast_to(vel_ref[x, y : y + 1], (modes, width))
            disp = jnp.broadcast_to(disp_ref[x, y : y + 1], (modes, width))
            value = combine(at(x - 2, y), at(x - 1, y), mid, at(x + 1, y), at(x + 2, y), sides, vel, disp)
            value += 2.0 * l_ref[0, i, y]
            rows.append(couple(value, weights, classes, cls_ref[x, y + 1 : y + 2]))
        out_ref[:, 0, :, i] = jnp.swapaxes(jnp.stack(rows), 0, 1).reshape(targets, each, part, width)


def last_kernel(f_ref, r_ref, *rest):
    out_ref = rest[-1]
    blocks = r_ref.shape[0]
    part = r_ref.shape[4]
    for b in range(blocks):
        rows = slice(b * part, (b + 1) * part)
        out_ref[0, :, :, rows] = f_ref[0, :, :, rows] + r_ref[b, 0]


def whole(array):
    return pl.BlockSpec(array.shape, lambda *_: (0,) * array.ndim)


def params(grid):
    return pltpu.CompilerParams(dimension_semantics=("arbitrary",) * grid, vmem_limit_bytes=VMEM_LIMIT)


def cost(flops, *arrays):
    moved = sum(math.prod(a.shape) * 4 for a in arrays)
    return pl.CostEstimate(flops=flops, bytes_accessed=moved, transcendentals=0)


def on_device(field, velocity, dispersion, mobility, material, fixed_mask):
    metals, each, depth, rows, width = field.shape
    modes = mobility.shape[2]
    classes = mobility.shape[1]
    blocks = lax.axis_size("mode")
    part = rows // blocks
    space = lax.axis_size("space")
    up = [(i, i + 1) for i in range(space - 1)]
    down = [(i + 1, i) for i in range(space - 1)]
    inner = tuple(range(2, depth - 2))
    outer = (0, 1, depth - 2, depth - 1)
    after = lax.optimization_barrier

    weights = class_weights(mobility)
    here = lax.axis_index("mode") * part
    cls = jnp.where(fixed_mask == 1, classes, material)
    cls = lax.dynamic_slice_in_dim(jnp.pad(cls, ((0, 0), (1, 1), (0, 0))), here, part + 2, 1)
    vel = lax.dynamic_slice_in_dim(velocity, here, part, 1)
    disp = lax.dynamic_slice_in_dim(dispersion, here, part, 1)

    def f32(*shape):
        return jax.ShapeDtypeStruct(shape, jnp.float32)

    def by_metal(array):
        return pl.BlockSpec((1,) + array.shape[1:], lambda m: (m,) + (0,) * (len(array.shape) - 1))

    def over_modes(array):
        return lax.all_to_all(array, "mode", split_axis=0, concat_axis=0, tiled=True)

    def run_spread(layers, *halos):
        sent = f32(blocks, metals, each, len(layers) + 1, part, width)
        operands = (field, velocity, dispersion) + halos
        return pl.pallas_call(
            functools.partial(spread_kernel, layers),
            grid=(metals,),
            in_specs=[by_metal(field), whole(velocity), whole(dispersion)] + [by_metal(h) for h in halos],
            out_specs=pl.BlockSpec((blocks, 1) + sent.shape[2:], lambda m: (0, m, 0, 0, 0, 0)),
            out_shape=pltpu.HBM(sent.shape, sent.dtype),
            compiler_params=params(1),
            cost_estimate=cost(20 * math.prod(sent.shape), field, sent),
            name="spread",
        )(*operands)

    def run_first(layers, got, pieces):
        count = len(layers)
        shapes = [f32(metals, count, part, modes, width), f32(metals, count, 2, modes, width)]
        shapes += [f32(metals, count // pieces, part, modes, width)] * pieces
        return pl.pallas_call(
            functools.partial(first_kernel, layers),
            grid=(metals,),
            in_specs=[
                pl.BlockSpec((blocks, 1) + got.shape[2:], lambda m: (0, m, 0, 0, 0, 0)),
                by_metal(weights),
                whole(cls),
            ],
            out_specs=[by_metal(s) for s in shapes],
            out_shape=[pltpu.HBM(s.shape, s.dtype) for s in shapes],
            compiler_params=params(1),
            cost_estimate=cost(300 * math.prod(got.shape), got, *shapes),
            name="first",
        )(got, weights, cls)

    def run_second(layers, g, low, high, l, beside, *halos):
        sent = f32(blocks, metals, each, len(layers), part, width)
        arrays = (g, low, high, l, beside, weights)
        return pl.pallas_call(
            functools.partial(second_kernel, layers),
            grid=(metals,),
            in_specs=[by_metal(a) for a in arrays]
            + [whole(cls), whole(vel), whole(disp)]
            + [by_metal(a) for a in halos],
            out_specs=pl.BlockSpec((blocks, 1) + sent.shape[2:], lambda m: (0, m, 0, 0, 0, 0)),
            out_shape=pltpu.HBM(sent.shape, sent.dtype),
            compiler_params=params(1),
            cost_estimate=cost(300 * math.prod(sent.shape), g, low, high, l, sent),
            name="second",
        )(*arrays, cls, vel, disp, *halos)

    def run_last(pair, got, *so_far):
        block = pl.BlockSpec((1, each, 2, rows, width), lambda m, k: (m, 0, pair(k), 0, 0))
        return pl.pallas_call(
            last_kernel,
            grid=(metals, 2),
            in_specs=[
                block,
                pl.BlockSpec((blocks, 1, each, 2, part, width), lambda m, k: (0, m, 0, k, 0, 0)),
            ]
            + [pl.BlockSpec(memory_space=pl.ANY)] * len(so_far),
            out_specs=block,
            out_shape=pltpu.HBM(field.shape, field.dtype),
            input_output_aliases={2: 0} if so_far else {},
            compiler_params=params(2),
            cost_estimate=cost(math.prod(got.shape), got, got, got),
            name="last",
        )(field, got, *so_far)

    lo = lax.ppermute(field[:, :, depth - 2 :], "space", up)
    hi = lax.ppermute(field[:, :, :2], "space", down)
    got_inner = over_modes(run_spread(inner))
    spread_outer = run_spread(outer, lo, hi)
    spread_outer, got_inner = after((spread_outer, got_inner))
    got_outer = over_modes(spread_outer)
    l_inner, beside_inner, g = run_first(inner, got_inner, 1)
    g, got_outer = after((g, got_outer))
    l_outer, beside_outer, low, high = run_first(outer, got_outer, 2)
    lo = lax.ppermute(high, "space", up)
    hi = lax.ppermute(low, "space", down)
    back_inner = over_modes(run_second(inner, g, low, high, l_inner, beside_inner))
    back_outer = run_second(outer, g, low, high, l_outer, beside_outer, lo, hi)
    back_outer, back_inner = after((back_outer, back_inner))
    back_outer = over_modes(back_outer)
    out = run_last(lambda k: k + 1, back_inner)
    return run_last(lambda k: 3 * k, back_outer, out)


def solution(mesh):
    in_specs = (
        P(None, "mode", "space", None, None),
        P("space", None, None),
        P("space", None, None),
        P(),
        P("space", None, None),
        P("space", None, None),
    )
    out_specs = P(None, "mode", "space", None, None)
    return jax.shard_map(
        on_device, mesh=mesh, in_specs=in_specs, out_specs=out_specs, check_vma=False
    )
```

time: 196 us -> 168 us (0.86)
  the two profiles are of different devices: /device:TPU:71 before, /device:TPU:224 now
where the time goes in v2:
time: 168 us; the launch traced here: 167 us
  waiting for transfers between devices  65.8 us (39%)
  starting transfers between devices  49.8 us (30%)
  Pallas kernels  33.4 us (20%)
  local copies, waits for them, and re-layouts  15.2 us (9%)
    all_to_all x4, starting transfers between devices, over_modes(): lax.all_to_all(array, 'mode', split_axis=0, concat_axis=0, tiled=True)  39 us
    ppermute x1, waiting for transfers between devices, on_device(): hi = lax.ppermute(field[:, :, :2], 'space', down)  23.2 us
    all_to_all x4, waiting for transfers between devices, over_modes(): lax.all_to_all(array, 'mode', split_axis=0, concat_axis=0, tiled=True)  22.3 us
    ppermute x1, waiting for transfers between devices, on_device(): hi = lax.ppermute(low, 'space', down)  13.8 us
    unnamed x36, local copies, waits for them, and re-layouts  13.8 us
    pallas_call x2, Pallas kernels, run_first(): pl.pallas_call(functools.partial(first_kernel, layers), grid=(metals,), i...  10 us
    pallas_call x2, Pallas kernels, run_last(): pl.pallas_call(last_kernel, grid=(metals, 2), in_specs=[block, pl.BlockSp...  9.23 us
    pallas_call x2, Pallas kernels, run_second(): pl.pallas_call(functools.partial(second_kernel, layers), grid=(metals,),...  8.24 us
  transfers between devices with their start and end apart: 8, of which 5 were waited for; matrix products, arithmetic and copies ran while one was open for 2% of the time, Pallas kernels for 10%

profile of v2, /device:TPU:224, one launch (start us, length us, event | category | flops | bytes accessed | tf_op | source)
XLA Modules:
  0.0 166.7 jit_solution(6448723281190211482)
XLA Ops:
  0.0 1.9 %copy-done.1 = f32[3,2,8,64,256]{4,3,2,1,0:T(8,128)S(1)} copy-done((f32[3,2,8,64,256]{4,3,2,1,0:T(8,128)S(1)}, f32[3,2,8,64,256]{4,3,2,1,0:T(8,128)}, u32[]{:S(2)}) %copy-start.1) | copy-done | bytes 3145752
  4.0 2.9 %spread.3 = f32[8,3,2,5,8,256]{5,4,3,2,1,0:T(8,128)} custom-call(f32[3,2,8,64,256]{4,3,2,1,0:T(8,128)S(1)} %copy-done.1, f32[8,64,256]{2,1,0:T(8,128)S(1)} %copy-done.9, f32[8,64,256]{2,1,0:T(8,128)S(1)} %copy-done.11), custom_call_target="tpu_custom_call" | custom-call | flops 9830400 | bytes 5111808 | tf_op jit(solution)/shard_map/spread/pallas_call | solution.py:217
  6.9 6.2 %all-to-all-start = ((f32[8,3,2,5,8,256]{5,4,3,2,1,0:T(8,128)}), f32[8,3,2,5,8,256]{5,4,3,2,1,0:T(8,128)}, u32[]{:S(2)}, u32[]{:S(2)}) async-start(f32[8,3,2,5,8,256]{5,4,3,2,1,0:T(8,128)} %spread.3), calls=%async_computation | async-start | bytes 3932160 | tf_op jit(solution)/shard_map/all_to_all | solution.py:212
  13.3 4.6 %collective-permute-start.1 = (f32[3,2,2,64,256]{4,3,2,1,0:T(8,128)S(1)}, f32[3,2,2,64,256]{4,3,2,1,0:T(8,128)S(1)}, u32[]{:S(2)}, u32[]{:S(2)}) collective-permute-start(f32[3,2,2,64,256]{4,3,2,1,0:T(8,128)S(1)} %get-tuple-element.31), channel_id=1, source_target_pairs={{8,0},{16,8},{24,16},{32,24},{40,32},{48,40},{56,48},{64,56},{72,6... | collective-permute-start | bytes 2359304 | tf_op jit(solution)/shard_map/ppermute | solution.py:282
  17.8 1.9 %collective-permute-start = (f32[3,2,2,64,256]{4,3,2,1,0:T(8,128)S(1)}, f32[3,2,2,64,256]{4,3,2,1,0:T(8,128)S(1)}, u32[]{:S(2)}, u32[]{:S(2)}) collective-permute-start(f32[3,2,2,64,256]{4,3,2,1,0:T(8,128)S(1)} %get-tuple-element.32), channel_id=1, source_target_pairs={{0,8},{8,16},{16,24},{24,32},{32,40},{40,48},{48,56},{56,64},{64,7... | collective-permute-start | bytes 2359304 | tf_op jit(solution)/shard_map/ppermute | solution.py:281
  19.8 23.2 %collective-permute-done.1.rest_1_ = f32[3,2,2,64,256]{4,3,2,1,0:T(8,128)S(1)} collective-permute-done((f32[3,2,2,64,256]{4,3,2,1,0:T(8,128)S(1)}, f32[3,2,2,64,256]{4,3,2,1,0:T(8,128)S(1)}, u32[]{:S(2)}, u32[]{:S(2)}) %collective-permute-start.1) | collective-permute-done | bytes 786464 | tf_op jit(solution)/shard_map/ppermute | solution.py:282
  43.0 3.0 %spread.2 = f32[8,3,2,5,8,256]{5,4,3,2,1,0:T(8,128)} custom-call(f32[3,2,8,64,256]{4,3,2,1,0:T(8,128)S(1)} %copy-done.2, f32[8,64,256]{2,1,0:T(8,128)S(1)} %copy-done.10, f32[8,64,256]{2,1,0:T(8,128)S(1)} %copy-done.12, f32[3,2,2,64,256]{4,3,2,1,0:T(8,128)S(1)} %collective-permute-done.rest_0_, f32[3,2,2,64,256]{4,3,2,1,0:T(8,128)S(1)} %collective-permute-done.1.rest_1_), custom_call_target="tpu_custom_call" | custom-call | flops 9830400 | bytes 5111808 | tf_op jit(solution)/shard_map/spread/pallas_call | solution.py:217
  46.0 17.0 %all-to-all-start.1 = ((f32[8,3,2,5,8,256]{5,4,3,2,1,0:T(8,128)}), f32[8,3,2,5,8,256]{5,4,3,2,1,0:T(8,128)}, u32[]{:S(2)}, u32[]{:S(2)}) async-start(f32[8,3,2,5,8,256]{5,4,3,2,1,0:T(8,128)} %spread.2), calls=%async_computation.1 | async-start | bytes 3932160 | tf_op jit(solution)/shard_map/all_to_all | solution.py:212
  66.7 5.1 %first.2 = (f32[3,4,8,16,256]{4,3,2,1,0:T(8,128)}, f32[3,4,2,16,256]{4,3,2,1,0:T(8,128)}, f32[3,4,8,16,256]{4,3,2,1,0:T(8,128)}) custom-call(f32[8,3,2,5,8,256]{5,4,3,2,1,0:T(8,128)} %all-to-all-done.r_ref, bf16[3,128,48]{2,1,0:T(8,128)(2,1)S(1)} %copy.15.w_ref, s32[8,10,256]{2,1,0:T(8,128)S(1)} %pad_dynamic-slice_fusion.cls_ref), custom_call_target="tpu_custom_call" | custom-call | flops 147456000 | bytes 5505024 | tf_op jit(solution)/shard_map/first/pallas_call | solution.py:232
  71.8 13.9 %all-to-all-done.1.r_ref = f32[8,3,2,5,8,256]{5,4,3,2,1,0:T(8,128)} async-done(((f32[8,3,2,5,8,256]{5,4,3,2,1,0:T(8,128)}), f32[8,3,2,5,8,256]{5,4,3,2,1,0:T(8,128)}, u32[]{:S(2)}, u32[]{:S(2)}) %all-to-all-start.1) | async-done | bytes 1966112 | tf_op jit(solution)/shard_map/all_to_all | solution.py:212
  85.7 4.9 %first.3 = (f32[3,4,8,16,256]{4,3,2,1,0:T(8,128)}, f32[3,4,2,16,256]{4,3,2,1,0:T(8,128)}, f32[3,2,8,16,256]{4,3,2,1,0:T(8,128)}, f32[3,2,8,16,256]{4,3,2,1,0:T(8,128)}) custom-call(f32[8,3,2,5,8,256]{5,4,3,2,1,0:T(8,128)} %all-to-all-done.1.r_ref, bf16[3,128,48]{2,1,0:T(8,128)(2,1)S(1)} %copy.15.w_ref, s32[8,10,256]{2,1,0:T(8,128)S(1)} %pad_dynamic-slice_fusion.cls_ref), custom_call_target="tpu_custom_call" | custom-call | flops 147456000 | bytes 5505024 | tf_op jit(solution)/shard_map/first/pallas_call | solution.py:232
  92.9 1.4 copy-done.13
  94.3 4.1 %second.3 = f32[8,3,2,4,8,256]{5,4,3,2,1,0:T(8,128)} custom-call(f32[3,4,8,16,256]{4,3,2,1,0:T(8,128)S(1)} %copy-done.3, f32[3,2,8,16,256]{4,3,2,1,0:T(8,128)S(1)} %copy-done.5, f32[3,2,8,16,256]{4,3,2,1,0:T(8,128)S(1)} %copy-done.7, f32[3,4,8,16,256]{4,3,2,1,0:T(8,128)S(1)} %copy-done.13, f32[3,4,2,16,256]{4,3,2,1,0:T(8,128)S(1)} %copy-done.16, ...), custom_call_target="tpu_custom_call" | custom-call | flops 117964800 | bytes 6291456 | tf_op jit(solution)/shard_map/second/pallas_call | solution.py:250
  98.4 4.3 %all-to-all-start.2 = ((f32[8,3,2,4,8,256]{5,4,3,2,1,0:T(8,128)}), f32[8,3,2,4,8,256]{5,4,3,2,1,0:T(8,128)}, u32[]{:S(2)}, u32[]{:S(2)}) async-start(f32[8,3,2,4,8,256]{5,4,3,2,1,0:T(8,128)} %second.3), calls=%async_computation.2 | async-start | bytes 3145728 | tf_op jit(solution)/shard_map/all_to_all | solution.py:212
  102.7 1.9 %collective-permute-start.3 = (f32[3,2,8,16,256]{4,3,2,1,0:T(8,128)}, f32[3,2,8,16,256]{4,3,2,1,0:T(8,128)S(1)}, u32[]{:S(2)}, u32[]{:S(2)}) collective-permute-start(f32[3,2,8,16,256]{4,3,2,1,0:T(8,128)} %get-tuple-element.23.low_ref), channel_id=1, source_target_pairs={{8,0},{16,8},{24,16},{32,24},{40,32},{48,40},{56,48},{64,56},{72,6... | collective-permute-start | bytes 2359304 | tf_op jit(solution)/shard_map/ppermute | solution.py:291
  104.6 2.4 %collective-permute-start.2 = (f32[3,2,8,16,256]{4,3,2,1,0:T(8,128)}, f32[3,2,8,16,256]{4,3,2,1,0:T(8,128)S(1)}, u32[]{:S(2)}, u32[]{:S(2)}) collective-permute-start(f32[3,2,8,16,256]{4,3,2,1,0:T(8,128)} %get-tuple-element.24.high_ref), channel_id=1, source_target_pairs={{0,8},{8,16},{16,24},{24,32},{32,40},{40,48},{48,56},{56,64},{64,7... | collective-permute-start | bytes 2359304 | tf_op jit(solution)/shard_map/ppermute | solution.py:290
  107.0 13.8 %collective-permute-done.3.rest_1_ = f32[3,2,8,16,256]{4,3,2,1,0:T(8,128)S(1)} collective-permute-done((f32[3,2,8,16,256]{4,3,2,1,0:T(8,128)}, f32[3,2,8,16,256]{4,3,2,1,0:T(8,128)S(1)}, u32[]{:S(2)}, u32[]{:S(2)}) %collective-permute-start.3) | collective-permute-done | bytes 786464 | tf_op jit(solution)/shard_map/ppermute | solution.py:291
  120.9 6.5 %collective-permute-done.2.rest_0_ = f32[3,2,8,16,256]{4,3,2,1,0:T(8,128)S(1)} collective-permute-done((f32[3,2,8,16,256]{4,3,2,1,0:T(8,128)}, f32[3,2,8,16,256]{4,3,2,1,0:T(8,128)S(1)}, u32[]{:S(2)}, u32[]{:S(2)}) %collective-permute-start.2) | collective-permute-done | bytes 786464 | tf_op jit(solution)/shard_map/ppermute | solution.py:290
  127.3 1.4 copy-done.4
  133.4 4.1 %second.2 = f32[8,3,2,4,8,256]{5,4,3,2,1,0:T(8,128)} custom-call(f32[3,4,8,16,256]{4,3,2,1,0:T(8,128)S(1)} %copy-done.4, f32[3,2,8,16,256]{4,3,2,1,0:T(8,128)S(1)} %copy-done.6, f32[3,2,8,16,256]{4,3,2,1,0:T(8,128)S(1)} %copy-done.8, f32[3,4,8,16,256]{4,3,2,1,0:T(8,128)S(1)} %copy-done.14, f32[3,4,2,16,256]{4,3,2,1,0:T(8,128)S(1)} %copy-done.15, ...), custom_call_target="tpu_custom_call" | custom-call | flops 117964800 | bytes 6291456 | tf_op jit(solution)/shard_map/second/pallas_call | solution.py:250
  137.6 11.6 %all-to-all-start.3 = ((f32[8,3,2,4,8,256]{5,4,3,2,1,0:T(8,128)}), f32[8,3,2,4,8,256]{5,4,3,2,1,0:T(8,128)}, u32[]{:S(2)}, u32[]{:S(2)}) async-start(f32[8,3,2,4,8,256]{5,4,3,2,1,0:T(8,128)} %second.2), calls=%async_computation.3 | async-start | bytes 3145728 | tf_op jit(solution)/shard_map/all_to_all | solution.py:212
  149.1 4.6 %last.2.rest_0_ = f32[3,2,8,64,256]{4,3,2,1,0:T(8,128)} custom-call(f32[3,2,8,64,256]{4,3,2,1,0:T(8,128)S(1)} %copy-done.2, f32[8,3,2,4,8,256]{5,4,3,2,1,0:T(8,128)} %all-to-all-done.2.r_ref), custom_call_target="tpu_custom_call" | custom-call | flops 393216 | bytes 4718592 | tf_op jit(solution)/shard_map/last/pallas_call | solution.py:265
  153.7 8.3 %all-to-all-done.3.r_ref = f32[8,3,2,4,8,256]{5,4,3,2,1,0:T(8,128)} async-done(((f32[8,3,2,4,8,256]{5,4,3,2,1,0:T(8,128)}), f32[8,3,2,4,8,256]{5,4,3,2,1,0:T(8,128)}, u32[]{:S(2)}, u32[]{:S(2)}) %all-to-all-start.3) | async-done | bytes 1572896 | tf_op jit(solution)/shard_map/all_to_all | solution.py:212
  162.1 4.6 %last.3 = f32[3,2,8,64,256]{4,3,2,1,0:T(8,128)} custom-call(f32[3,2,8,64,256]{4,3,2,1,0:T(8,128)S(1)} %copy-done.2, f32[8,3,2,4,8,256]{5,4,3,2,1,0:T(8,128)} %all-to-all-done.3.r_ref, f32[3,2,8,64,256]{4,3,2,1,0:T(8,128)} %last.2.rest_0_), custom_call_target="tpu_custom_call", output_to_operand_aliasing={{}: (2, {})} | custom-call | flops 393216 | bytes 4718592 | tf_op jit(solution)/shard_map/last/pallas_call | solution.py:265
  (47 shorter events, 12.8 us)
Async XLA Ops:
  0.0 63.0 %copy-start = (f32[3,8,16]{2,1,0:T(8,128)S(1)}, f32[3,8,16]{2,1,0:T(8,128)}, u32[]{:S(2)}) copy-start(f32[3,8,16]{2,1,0:T(8,128)} %param.10) | copy-start | bytes 4612
  0.0 1.9 %copy-start.1 = (f32[3,2,8,64,256]{4,3,2,1,0:T(8,128)S(1)}, f32[3,2,8,64,256]{4,3,2,1,0:T(8,128)}, u32[]{:S(2)}) copy-start(f32[3,2,8,64,256]{4,3,2,1,0:T(8,128)} %f_ref.7) | copy-start | bytes 9437188
  1.9 1.0 copy-start.9
  6.9 6.2 %copy-start.2 = (f32[3,2,8,64,256]{4,3,2,1,0:T(8,128)S(1)}, f32[3,2,8,64,256]{4,3,2,1,0:T(8,128)}, u32[]{:S(2)}) copy-start(f32[3,2,8,64,256]{4,3,2,1,0:T(8,128)} %f_ref.7) | copy-start | bytes 9437188
  6.9 39.1 %all-to-all-start = ((f32[8,3,2,5,8,256]{5,4,3,2,1,0:T(8,128)}), f32[8,3,2,5,8,256]{5,4,3,2,1,0:T(8,128)}, u32[]{:S(2)}, u32[]{:S(2)}) async-start(f32[8,3,2,5,8,256]{5,4,3,2,1,0:T(8,128)} %spread.3), calls=%async_computation | async-start | bytes 3932160 | tf_op jit(solution)/shard_map/all_to_all | solution.py:212
  13.1 29.9 %copy-start.10 = (f32[8,64,256]{2,1,0:T(8,128)S(1)}, f32[8,64,256]{2,1,0:T(8,128)}, u32[]{:S(2)}) copy-start(f32[8,64,256]{2,1,0:T(8,128)} %vel_ref.3) | copy-start | bytes 1572868
  13.1 29.9 %copy-start.12 = (f32[8,64,256]{2,1,0:T(8,128)S(1)}, f32[8,64,256]{2,1,0:T(8,128)}, u32[]{:S(2)}) copy-start(f32[8,64,256]{2,1,0:T(8,128)} %disp_ref.3) | copy-start | bytes 1572868
  13.3 29.7 %collective-permute-start.1 = (f32[3,2,2,64,256]{4,3,2,1,0:T(8,128)S(1)}, f32[3,2,2,64,256]{4,3,2,1,0:T(8,128)S(1)}, u32[]{:S(2)}, u32[]{:S(2)}) collective-permute-start(f32[3,2,2,64,256]{4,3,2,1,0:T(8,128)S(1)} %get-tuple-element.31), channel_id=1, source_target_pairs={{8,0},{16,8},{24,16},{32,24},{40,32},{48,40},{56,48},{64,56},{72,6... | collective-permute-start | bytes 2359304 | tf_op jit(solution)/shard_map/ppermute | solution.py:282
  17.8 25.2 %collective-permute-start = (f32[3,2,2,64,256]{4,3,2,1,0:T(8,128)S(1)}, f32[3,2,2,64,256]{4,3,2,1,0:T(8,128)S(1)}, u32[]{:S(2)}, u32[]{:S(2)}) collective-permute-start(f32[3,2,2,64,256]{4,3,2,1,0:T(8,128)S(1)} %get-tuple-element.32), channel_id=1, source_target_pairs={{0,8},{8,16},{16,24},{24,32},{32,40},{40,48},{48,56},{56,64},{64,7... | collective-permute-start | bytes 2359304 | tf_op jit(solution)/shard_map/ppermute | solution.py:281
  46.0 17.0 %copy-start.17 = (f32[16,16,16,1]{2,1,3,0:T(8,128)S(1)}, f32[16,16,16,1]{2,1,3,0:T(8,128)}, u32[]{:S(2)}) copy-start(f32[16,16,16,1]{2,1,3,0:T(8,128)} %constant.30) | copy-start | bytes 49156
  46.0 39.7 %all-to-all-start.1 = ((f32[8,3,2,5,8,256]{5,4,3,2,1,0:T(8,128)}), f32[8,3,2,5,8,256]{5,4,3,2,1,0:T(8,128)}, u32[]{:S(2)}, u32[]{:S(2)}) async-start(f32[8,3,2,5,8,256]{5,4,3,2,1,0:T(8,128)} %spread.2), calls=%async_computation.1 | async-start | bytes 3932160 | tf_op jit(solution)/shard_map/all_to_all | solution.py:212
  85.7 5.0 %copy-start.3 = (f32[3,4,8,16,256]{4,3,2,1,0:T(8,128)S(1)}, f32[3,4,8,16,256]{4,3,2,1,0:T(8,128)}, u32[]{:S(2)}) copy-start(f32[3,4,8,16,256]{4,3,2,1,0:T(8,128)} %get-tuple-element.21.g_ref) | copy-start | bytes 4718596
  85.7 5.0 %copy-start.16 = (f32[3,4,2,16,256]{4,3,2,1,0:T(8,128)S(1)}, f32[3,4,2,16,256]{4,3,2,1,0:T(8,128)}, u32[]{:S(2)}) copy-start(f32[3,4,2,16,256]{4,3,2,1,0:T(8,128)} %get-tuple-element.28.beside_ref) | copy-start | bytes 1179652
  90.6 1.1 copy-start.5
  91.8 1.1 copy-start.7
  92.9 1.4 copy-start.13
  98.4 39.1 %all-to-all-start.2 = ((f32[8,3,2,4,8,256]{5,4,3,2,1,0:T(8,128)}), f32[8,3,2,4,8,256]{5,4,3,2,1,0:T(8,128)}, u32[]{:S(2)}, u32[]{:S(2)}) async-start(f32[8,3,2,4,8,256]{5,4,3,2,1,0:T(8,128)} %second.3), calls=%async_computation.2 | async-start | bytes 3145728 | tf_op jit(solution)/shard_map/all_to_all | solution.py:212
  102.7 18.2 %collective-permute-start.3 = (f32[3,2,8,16,256]{4,3,2,1,0:T(8,128)}, f32[3,2,8,16,256]{4,3,2,1,0:T(8,128)S(1)}, u32[]{:S(2)}, u32[]{:S(2)}) collective-permute-start(f32[3,2,8,16,256]{4,3,2,1,0:T(8,128)} %get-tuple-element.23.low_ref), channel_id=1, source_target_pairs={{8,0},{16,8},{24,16},{32,24},{40,32},{48,40},{56,48},{64,56},{72,6... | collective-permute-start | bytes 2359304 | tf_op jit(solution)/shard_map/ppermute | solution.py:291
  104.6 22.7 %collective-permute-start.2 = (f32[3,2,8,16,256]{4,3,2,1,0:T(8,128)}, f32[3,2,8,16,256]{4,3,2,1,0:T(8,128)S(1)}, u32[]{:S(2)}, u32[]{:S(2)}) collective-permute-start(f32[3,2,8,16,256]{4,3,2,1,0:T(8,128)} %get-tuple-element.24.high_ref), channel_id=1, source_target_pairs={{0,8},{8,16},{16,24},{24,32},{32,40},{40,48},{48,56},{56,64},{64,7... | collective-permute-start | bytes 2359304 | tf_op jit(solution)/shard_map/ppermute | solution.py:290
  127.3 1.4 copy-start.4
  128.8 1.1 copy-start.6
  129.9 1.1 copy-start.8
  131.0 1.4 copy-start.14
  137.6 24.5 %all-to-all-start.3 = ((f32[8,3,2,4,8,256]{5,4,3,2,1,0:T(8,128)}), f32[8,3,2,4,8,256]{5,4,3,2,1,0:T(8,128)}, u32[]{:S(2)}, u32[]{:S(2)}) async-start(f32[8,3,2,4,8,256]{5,4,3,2,1,0:T(8,128)} %second.2), calls=%async_computation.3 | async-start | bytes 3145728 | tf_op jit(solution)/shard_map/all_to_all | solution.py:212
  (2 other events, 2.0 us)

commit v3 on v2

--- a/solution.py
+++ b/solution.py
@@ -12,7 +12,8 @@
 
 TIME_STEP = 0.1
 MOBILE_BASE = 0.7
-VMEM_LIMIT = 30 * 1024 * 1024
+RUN = 8
+VMEM_LIMIT = 61 * 1024 * 1024
 
 
 def legendre_weight(order):
@@ -58,7 +59,7 @@
 
 
 def spread_kernel(layers, f_ref, vel_ref, disp_ref, *rest):
-    lo_ref, hi_ref = rest[:2] if len(rest) == 3 else (None, None)
+    lo_ref, hi_ref, around_ref, ends_ref = rest[:4] if len(rest) == 5 else (None,) * 4
     out_ref = rest[-1]
     depth, rows, width = f_ref.shape[2:]
     blocks = out_ref.shape[0]
@@ -68,9 +69,9 @@
 
     def layer(e, x):
         if x < 0:
-            return lo_ref[0, e, x + 2]
+            return lo_ref[0, e, x + 2] + ends_ref[0] * around_ref[0, e, x + 2]
         if x >= depth:
-            return hi_ref[0, e, x - depth]
+            return hi_ref[0, e, x - depth] + ends_ref[1] * around_ref[0, e, x - depth]
         return f_ref[0, e, x]
 
     zero_row = jnp.zeros((1, width), jnp.float32)
@@ -126,7 +127,7 @@
 
 
 def second_kernel(layers, g_ref, low_ref, high_ref, l_ref, beside_ref, w_ref, cls_ref, vel_ref, disp_ref, *rest):
-    lo_ref, hi_ref = rest[:2] if len(rest) == 3 else (None, None)
+    lo_ref, hi_ref, around_ref, ends_ref = rest[:4] if len(rest) == 5 else (None,) * 4
     out_ref = rest[-1]
     inner, part, modes, width = g_ref.shape[1:]
     depth = inner + 4
@@ -136,14 +137,14 @@
 
     def at(x, y):
         if x < 0:
-            return lo_ref[0, x + 2, y]
+            return lo_ref[0, x + 2, y] + ends_ref[0] * around_ref[0, x + 2, y]
         if x < 2:
             return low_ref[0, x, y]
         if x < depth - 2:
             return g_ref[0, x - 2, y]
         if x < depth:
             return high_ref[0, x - depth + 2, y]
-        return hi_ref[0, x - depth, y]
+        return hi_ref[0, x - depth, y] + ends_ref[1] * around_ref[0, x - depth, y]
 
     for i, x in enumerate(layers):
         rows = []
@@ -169,17 +170,80 @@
         out_ref[0, :, :, rows] = f_ref[0, :, :, rows] + r_ref[b, 0]
 
 
-def whole(array):
-    return pl.BlockSpec(array.shape, lambda *_: (0,) * array.ndim)
-
-
-def params(grid):
-    return pltpu.CompilerParams(dimension_semantics=("arbitrary",) * grid, vmem_limit_bytes=VMEM_LIMIT)
-
-
-def cost(flops, *arrays):
-    moved = sum(math.prod(a.shape) * 4 for a in arrays)
-    return pl.CostEstimate(flops=flops, bytes_accessed=moved, transcendentals=0)
+def staged(body, steps, inputs, outputs, flops, name, scalars=(), so_far=()):
+    n_in, n_out = len(inputs), len(outputs)
+
+    def kernel(*refs):
+        in_refs, refs = refs[:n_in], refs[n_in:]
+        scalar_refs, refs = refs[: len(scalars)], refs[len(scalars) :]
+        refs = refs[len(so_far) :]
+        out_refs, refs = refs[:n_out], refs[n_out:]
+        in_bufs, out_bufs, (sems,) = refs[:n_in], refs[n_in : n_in + n_out], refs[n_in + n_out :]
+
+        def load(k, i):
+            index = inputs[k][2]
+            if index is None:
+                return pltpu.make_async_copy(in_refs[k], in_bufs[k], sems.at[k, 0])
+            return pltpu.make_async_copy(in_refs[k].at[index(i)], in_bufs[k].at[i], sems.at[k, i])
+
+        def store(k, i):
+            return pltpu.make_async_copy(out_bufs[k].at[i], out_refs[k].at[outputs[k][2](i)], sems.at[n_in + k, i])
+
+        for i in range(steps):
+            for k in range(n_in):
+                if i == 0 or inputs[k][2] is not None:
+                    load(k, i).start()
+        for k in range(n_in):
+            if inputs[k][2] is None:
+                load(k, 0).wait()
+
+        def step(i, carry):
+            for k in range(n_in):
+                if inputs[k][2] is not None:
+                    load(k, i).wait()
+            blocks = [buf if spec[2] is None else buf.at[i] for buf, spec in zip(in_bufs, inputs)]
+            body(*blocks, *scalar_refs, *[buf.at[i] for buf in out_bufs])
+            for k in range(n_out):
+                store(k, i).start()
+            return carry
+
+        lax.fori_loop(0, steps, step, 0)
+        for i in range(steps):
+            for k in range(n_out):
+                store(k, i).wait()
+
+    hbm = pl.BlockSpec(memory_space=pltpu.HBM)
+    scratch = [
+        pltpu.VMEM(block if index is None else (steps,) + block, array.dtype) for array, block, index in inputs
+    ]
+    scratch += [pltpu.VMEM((steps,) + block, shape.dtype) for shape, block, _ in outputs]
+    moved = sum(4 * math.prod(a.shape) for a, *_ in (*inputs, *outputs))
+    return pl.pallas_call(
+        kernel,
+        in_specs=[hbm] * n_in + [pl.BlockSpec(memory_space=pltpu.SMEM)] * len(scalars) + [hbm] * len(so_far),
+        out_specs=[hbm] * n_out,
+        out_shape=[pltpu.HBM(shape.shape, shape.dtype) for shape, *_ in outputs],
+        scratch_shapes=scratch + [pltpu.SemaphoreType.DMA((n_in + n_out, steps))],
+        input_output_aliases={n_in + len(scalars): 0} if so_far else {},
+        compiler_params=pltpu.CompilerParams(vmem_limit_bytes=VMEM_LIMIT),
+        cost_estimate=pl.CostEstimate(flops=flops, bytes_accessed=moved, transcendentals=0),
+        name=name,
+    )(*[array for array, *_ in inputs], *scalars, *so_far)
+
+
+def halo_routes(space, blocks):
+    direct, leave, arrive = [], [], []
+    for s in range(space - 1):
+        for m in range(blocks):
+            ends = (s * blocks + m, (s + 1) * blocks + m)
+            if (s + 1) % RUN or m < blocks // 2:
+                direct.append(ends)
+            else:
+                near = (s + 2 - RUN) * blocks + m
+                far = (s + RUN - 1) * blocks + m
+                leave += [(ends[0], near), (ends[1], far)]
+                arrive += [(near, ends[1]), (far, ends[0])]
+    return direct, leave, arrive
 
 
 def on_device(field, velocity, dispersion, mobility, material, fixed_mask):
@@ -189,8 +253,18 @@
     blocks = lax.axis_size("mode")
     part = rows // blocks
     space = lax.axis_size("space")
-    up = [(i, i + 1) for i in range(space - 1)]
-    down = [(i + 1, i) for i in range(space - 1)]
+    direct, leave, arrive = halo_routes(space, blocks)
+    back = [(b, a) for a, b in direct]
+    both = ("space", "mode")
+    place = lax.axis_index("space") % RUN
+    ends = jnp.stack([place == 0, place == RUN - 1]).astype(jnp.float32)
+
+    def exchange(low, high):
+        lo = lax.ppermute(high, both, direct)
+        hi = lax.ppermute(low, both, back)
+        around = lax.ppermute(jnp.where(place == RUN - 1, high, low), both, leave)
+        return lo, hi, lax.ppermute(around, both, arrive), ends
+
     inner = tuple(range(2, depth - 2))
     outer = (0, 1, depth - 2, depth - 1)
     after = lax.optimization_barrier
@@ -206,91 +280,93 @@
         return jax.ShapeDtypeStruct(shape, jnp.float32)
 
     def by_metal(array):
-        return pl.BlockSpec((1,) + array.shape[1:], lambda m: (m,) + (0,) * (len(array.shape) - 1))
+        return array, (1,) + array.shape[1:], lambda i: pl.ds(i, 1)
+
+    def by_unit(array):
+        return array, (array.shape[0], 1) + array.shape[2:], lambda i: (slice(None), pl.ds(i, 1))
+
+    def whole(array):
+        return array, array.shape, None
 
     def over_modes(array):
         return lax.all_to_all(array, "mode", split_axis=0, concat_axis=0, tiled=True)
 
     def run_spread(layers, *halos):
         sent = f32(blocks, metals, each, len(layers) + 1, part, width)
-        operands = (field, velocity, dispersion) + halos
-        return pl.pallas_call(
+        (out,) = staged(
             functools.partial(spread_kernel, layers),
-            grid=(metals,),
-            in_specs=[by_metal(field), whole(velocity), whole(dispersion)] + [by_metal(h) for h in halos],
-            out_specs=pl.BlockSpec((blocks, 1) + sent.shape[2:], lambda m: (0, m, 0, 0, 0, 0)),
-            out_shape=pltpu.HBM(sent.shape, sent.dtype),
-            compiler_params=params(1),
-            cost_estimate=cost(20 * math.prod(sent.shape), field, sent),
-            name="spread",
-        )(*operands)
+            metals,
+            [by_metal(field), whole(velocity), whole(dispersion)] + [by_metal(h) for h in halos[:3]],
+            [by_unit(sent)],
+            20 * math.prod(sent.shape),
+            "spread",
+            halos[3:],
+        )
+        return out
 
     def run_first(layers, got, pieces):
         count = len(layers)
         shapes = [f32(metals, count, part, modes, width), f32(metals, count, 2, modes, width)]
         shapes += [f32(metals, count // pieces, part, modes, width)] * pieces
-        return pl.pallas_call(
+        return staged(
             functools.partial(first_kernel, layers),
-            grid=(metals,),
-            in_specs=[
-                pl.BlockSpec((blocks, 1) + got.shape[2:], lambda m: (0, m, 0, 0, 0, 0)),
-                by_metal(weights),
-                whole(cls),
-            ],
-            out_specs=[by_metal(s) for s in shapes],
-            out_shape=[pltpu.HBM(s.shape, s.dtype) for s in shapes],
-            compiler_params=params(1),
-            cost_estimate=cost(300 * math.prod(got.shape), got, *shapes),
-            name="first",
-        )(got, weights, cls)
+            metals,
+            [by_unit(got), by_metal(weights), whole(cls)],
+            [by_metal(s) for s in shapes],
+            300 * math.prod(got.shape),
+            "first",
+        )
 
     def run_second(layers, g, low, high, l, beside, *halos):
         sent = f32(blocks, metals, each, len(layers), part, width)
-        arrays = (g, low, high, l, beside, weights)
-        return pl.pallas_call(
+        (out,) = staged(
             functools.partial(second_kernel, layers),
-            grid=(metals,),
-            in_specs=[by_metal(a) for a in arrays]
+            metals,
+            [by_metal(a) for a in (g, low, high, l, beside, weights)]
             + [whole(cls), whole(vel), whole(disp)]
-            + [by_metal(a) for a in halos],
-            out_specs=pl.BlockSpec((blocks, 1) + sent.shape[2:], lambda m: (0, m, 0, 0, 0, 0)),
-            out_shape=pltpu.HBM(sent.shape, sent.dtype),
-            compiler_params=params(1),
-            cost_estimate=cost(300 * math.prod(sent.shape), g, low, high, l, sent),
-            name="second",
-        )(*arrays, cls, vel, disp, *halos)
+            + [by_metal(a) for a in halos[:3]],
+            [by_unit(sent)],
+            300 * math.prod(sent.shape),
+            "second",
+            halos[3:],
+        )
+        return out
 
     def run_last(pair, got, *so_far):
-        block = pl.BlockSpec((1, each, 2, rows, width), lambda m, k: (m, 0, pair(k), 0, 0))
-        return pl.pallas_call(
+        block = (1, each, 2, rows, width)
+
+        def at(i):
+            return pl.ds(i // 2, 1), slice(None), pl.ds(2 * pair(i % 2), 2)
+
+        (out,) = staged(
             last_kernel,
-            grid=(metals, 2),
-            in_specs=[
-                block,
-                pl.BlockSpec((blocks, 1, each, 2, part, width), lambda m, k: (0, m, 0, k, 0, 0)),
-            ]
-            + [pl.BlockSpec(memory_space=pl.ANY)] * len(so_far),
-            out_specs=block,
-            out_shape=pltpu.HBM(field.shape, field.dtype),
-            input_output_aliases={2: 0} if so_far else {},
-            compiler_params=params(2),
-            cost_estimate=cost(math.prod(got.shape), got, got, got),
-            name="last",
-        )(field, got, *so_far)
-
-    lo = lax.ppermute(field[:, :, depth - 2 :], "space", up)
-    hi = lax.ppermute(field[:, :, :2], "space", down)
+            2 * metals,
+            [
+                (field, block, at),
+                (
+                    got,
+                    (blocks, 1, each, 2, part, width),
+                    lambda i: (slice(None), pl.ds(i // 2, 1), slice(None), pl.ds(2 * (i % 2), 2)),
+                ),
+            ],
+            [(field, block, at)],
+            math.prod(got.shape),
+            "last",
+            so_far=so_far,
+        )
+        return out
+
+    sides = exchange(field[:, :, :2], field[:, :, depth - 2 :])
     got_inner = over_modes(run_spread(inner))
-    spread_outer = run_spread(outer, lo, hi)
+    spread_outer = run_spread(outer, *sides)
     spread_outer, got_inner = after((spread_outer, got_inner))
     got_outer = over_modes(spread_outer)
     l_inner, beside_inner, g = run_first(inner, got_inner, 1)
     g, got_outer = after((g, got_outer))
     l_outer, beside_outer, low, high = run_first(outer, got_outer, 2)
-    lo = lax.ppermute(high, "space", up)
-    hi = lax.ppermute(low, "space", down)
+    sides = exchange(low, high)
     back_inner = over_modes(run_second(inner, g, low, high, l_inner, beside_inner))
-    back_outer = run_second(outer, g, low, high, l_outer, beside_outer, lo, hi)
+    back_outer = run_second(outer, g, low, high, l_outer, beside_outer, *sides)
     back_outer, back_inner = after((back_outer, back_inner))
     back_outer = over_modes(back_outer)
     out = run_last(lambda k: k + 1, back_inner)

time: 168 us -> 161 us (0.958)
  the two profiles are of different devices: /device:TPU:224 before, /device:TPU:71 now
where the time goes in v3:
time: 161 us; the launch traced here: 159 us
  waiting for transfers between devices  59.7 us (37%)
  starting transfers between devices  49.3 us (31%)
  Pallas kernels  37.8 us (23%)
  local copies, waits for them, and re-layouts  8.16 us (5%)
  other arithmetic  2.31 us (1%)
    pallas_call x8, Pallas kernels, staged(): pl.pallas_call(kernel, in_specs=[hbm] * n_in + [pl.BlockSpec(memory_space...  37.8 us
    all_to_all x4, waiting for transfers between devices, over_modes(): lax.all_to_all(array, 'mode', split_axis=0, concat_axis=0, tiled=True)  28.8 us
    all_to_all x4, starting transfers between devices, over_modes(): lax.all_to_all(array, 'mode', split_axis=0, concat_axis=0, tiled=True)  26.1 us
    ppermute x2, waiting for transfers between devices, exchange(): lo = lax.ppermute(high, both, direct)  17.1 us
    ppermute x2, starting transfers between devices, exchange(): lo = lax.ppermute(high, both, direct)  14.2 us
    ppermute x2, waiting for transfers between devices, exchange(): hi = lax.ppermute(low, both, back)  13.7 us
    ppermute x2, starting transfers between devices, exchange(): hi = lax.ppermute(low, both, back)  5.39 us
    unnamed x30, local copies, waits for them, and re-layouts  4.95 us
  transfers between devices with their start and end apart: 12, of which 6 were waited for; matrix products, arithmetic and copies ran while one was open for 4% of the time, Pallas kernels for 13%

profile of v3, /device:TPU:71, one launch (start us, length us, event | category | flops | bytes accessed | tf_op | source)
XLA Modules:
  0.0 158.6 jit_solution(5352217635652761410)
XLA Ops:
  0.0 4.3 %spread.3 = f32[8,3,2,5,8,256]{5,4,3,2,1,0:T(8,128)} custom-call(f32[3,2,8,64,256]{4,3,2,1,0:T(8,128)} %refs_0_.7, f32[8,64,256]{2,1,0:T(8,128)} %refs_1_.3, f32[8,64,256]{2,1,0:T(8,128)} %refs_2_.3), custom_call_target="tpu_custom_call" | custom-call | flops 9830400 | bytes 6160384 | tf_op jit(solution)/shard_map/spread/pallas_call | solution.py:221
  4.3 5.8 %all-to-all-start = ((f32[8,3,2,5,8,256]{5,4,3,2,1,0:T(8,128)}), f32[8,3,2,5,8,256]{5,4,3,2,1,0:T(8,128)}, u32[]{:S(2)}, u32[]{:S(2)}) async-start(f32[8,3,2,5,8,256]{5,4,3,2,1,0:T(8,128)} %spread.3), calls=%async_computation | async-start | bytes 3932160 | tf_op jit(solution)/shard_map/all_to_all | solution.py:292
  11.6 1.5 collective-permute-start.2
  13.1 2.9 %collective-permute-start.1 = (f32[3,2,2,64,256]{4,3,2,1,0:T(8,128)}, f32[3,2,2,64,256]{4,3,2,1,0:T(8,128)S(1)}, u32[]{:S(2)}, u32[]{:S(2)}) collective-permute-start(f32[3,2,2,64,256]{4,3,2,1,0:T(8,128)} %get-tuple-element.32), channel_id=1, source_target_pairs={{8,0},{9,1},{10,2},{11,3},{12,4},{13,5},{14,6},{15,7},{16,8},{17,9... | collective-permute-start | bytes 2359304 | tf_op jit(solution)/shard_map/ppermute | solution.py:264
  16.0 6.9 %collective-permute-start = (f32[3,2,2,64,256]{4,3,2,1,0:T(8,128)}, f32[3,2,2,64,256]{4,3,2,1,0:T(8,128)S(1)}, u32[]{:S(2)}, u32[]{:S(2)}) collective-permute-start(f32[3,2,2,64,256]{4,3,2,1,0:T(8,128)} %get-tuple-element.33), channel_id=1, source_target_pairs={{0,8},{1,9},{2,10},{3,11},{4,12},{5,13},{6,14},{7,15},{8,16},{9,17... | collective-permute-start | bytes 2359304 | tf_op jit(solution)/shard_map/ppermute | solution.py:263
  24.3 6.6 %collective-permute-done.1.refs_4_ = f32[3,2,2,64,256]{4,3,2,1,0:T(8,128)S(1)} collective-permute-done((f32[3,2,2,64,256]{4,3,2,1,0:T(8,128)}, f32[3,2,2,64,256]{4,3,2,1,0:T(8,128)S(1)}, u32[]{:S(2)}, u32[]{:S(2)}) %collective-permute-start.1) | collective-permute-done | bytes 786464 | tf_op jit(solution)/shard_map/ppermute | solution.py:264
  30.9 9.6 %collective-permute-done.refs_3_ = f32[3,2,2,64,256]{4,3,2,1,0:T(8,128)S(1)} collective-permute-done((f32[3,2,2,64,256]{4,3,2,1,0:T(8,128)}, f32[3,2,2,64,256]{4,3,2,1,0:T(8,128)S(1)}, u32[]{:S(2)}, u32[]{:S(2)}) %collective-permute-start) | collective-permute-done | bytes 786464 | tf_op jit(solution)/shard_map/ppermute | solution.py:263
  42.4 5.4 %spread.2 = f32[8,3,2,5,8,256]{5,4,3,2,1,0:T(8,128)} custom-call(f32[3,2,8,64,256]{4,3,2,1,0:T(8,128)} %refs_0_.7, f32[8,64,256]{2,1,0:T(8,128)} %refs_1_.3, f32[8,64,256]{2,1,0:T(8,128)} %refs_2_.3, f32[3,2,2,64,256]{4,3,2,1,0:T(8,128)} %copy-done.9, f32[3,2,2,64,256]{4,3,2,1,0:T(8,128)} %copy-done.8, f32[3,2,2,64,256]{4,3,2,1,0:T(8,128)} %copy-done.11, ...), custom_call_target="tpu_custom_call" | custom-call | flops 9830400 | bytes 8519680 | tf_op jit(solution)/shard_map/spread/pallas_call | solution.py:221
  47.9 8.1 %all-to-all-start.1 = ((f32[8,3,2,5,8,256]{5,4,3,2,1,0:T(8,128)}), f32[8,3,2,5,8,256]{5,4,3,2,1,0:T(8,128)S(1)}, u32[]{:S(2)}, u32[]{:S(2)}) async-start(f32[8,3,2,5,8,256]{5,4,3,2,1,0:T(8,128)} %spread.2), calls=%async_computation.1 | async-start | bytes 3932160 | tf_op jit(solution)/shard_map/all_to_all | solution.py:292
  58.0 1.5 constant_dynamic-slice_fusion
  60.3 4.7 %first.2 = (f32[3,4,8,16,256]{4,3,2,1,0:T(8,128)}, f32[3,4,2,16,256]{4,3,2,1,0:T(8,128)}, f32[3,4,8,16,256]{4,3,2,1,0:T(8,128)}) custom-call(f32[8,3,2,5,8,256]{5,4,3,2,1,0:T(8,128)} %all-to-all-done.refs_0_, bf16[3,128,48]{2,1,0:T(8,128)(2,1)} %copy.15.refs_1_.refs_5_, s32[8,10,256]{2,1,0:T(8,128)} %pad_dynamic-slice_fusion.refs_2_.refs_6_), custom_call_target="tpu_custom_call" | custom-call | flops 147456000 | bytes 5660672 | tf_op jit(solution)/shard_map/first/pallas_call | solution.py:221
  65.0 13.3 %all-to-all-done.1.refs_0_ = f32[8,3,2,5,8,256]{5,4,3,2,1,0:T(8,128)S(1)} async-done(((f32[8,3,2,5,8,256]{5,4,3,2,1,0:T(8,128)}), f32[8,3,2,5,8,256]{5,4,3,2,1,0:T(8,128)S(1)}, u32[]{:S(2)}, u32[]{:S(2)}) %all-to-all-start.1) | async-done | bytes 1966112 | tf_op jit(solution)/shard_map/all_to_all | solution.py:292
  79.6 4.7 %first.3 = (f32[3,4,8,16,256]{4,3,2,1,0:T(8,128)}, f32[3,4,2,16,256]{4,3,2,1,0:T(8,128)}, f32[3,2,8,16,256]{4,3,2,1,0:T(8,128)}, f32[3,2,8,16,256]{4,3,2,1,0:T(8,128)}) custom-call(f32[8,3,2,5,8,256]{5,4,3,2,1,0:T(8,128)} %copy-done.2, bf16[3,128,48]{2,1,0:T(8,128)(2,1)} %copy.15.refs_1_.refs_5_, s32[8,10,256]{2,1,0:T(8,128)} %pad_dynamic-slice_fusion.refs_2_.refs_6_), custom_call_target="tpu_custom_call" | custom-call | flops 147456000 | bytes 5660672 | tf_op jit(solution)/shard_map/first/pallas_call | solution.py:221
  84.3 6.0 %second.3 = f32[8,3,2,4,8,256]{5,4,3,2,1,0:T(8,128)} custom-call(f32[3,4,8,16,256]{4,3,2,1,0:T(8,128)} %get-tuple-element.21.refs_0_, f32[3,2,8,16,256]{4,3,2,1,0:T(8,128)} %get-tuple-element.23.refs_1_, f32[3,2,8,16,256]{4,3,2,1,0:T(8,128)} %get-tuple-element.24.refs_2_, f32[3,4,8,16,256]{4,3,2,1,0:T(8,128)} %get-tuple-element.27.refs_3_, ...), custom_call_target="tpu_custom_call" | custom-call | flops 117964800 | bytes 6971392 | tf_op jit(solution)/shard_map/second/pallas_call | solution.py:221
  90.3 3.7 %all-to-all-start.2 = ((f32[8,3,2,4,8,256]{5,4,3,2,1,0:T(8,128)}), f32[8,3,2,4,8,256]{5,4,3,2,1,0:T(8,128)S(1)}, u32[]{:S(2)}, u32[]{:S(2)}) async-start(f32[8,3,2,4,8,256]{5,4,3,2,1,0:T(8,128)} %second.3), calls=%async_computation.2 | async-start | bytes 3145728 | tf_op jit(solution)/shard_map/all_to_all | solution.py:292
  94.9 2.5 %collective-permute-start.5 = (f32[3,2,8,16,256]{4,3,2,1,0:T(8,128)S(1)}, f32[3,2,8,16,256]{4,3,2,1,0:T(8,128)S(1)}, u32[]{:S(2)}, u32[]{:S(2)}) collective-permute-start(f32[3,2,8,16,256]{4,3,2,1,0:T(8,128)S(1)} %copy-done.3), channel_id=1, source_target_pairs={{8,0},{9,1},{10,2},{11,3},{12,4},{13,5},{14,6},{15,7},{16,8},{17,9... | collective-permute-start | bytes 2359304 | tf_op jit(solution)/shard_map/ppermute | solution.py:264
  97.4 7.2 %collective-permute-start.4 = (f32[3,2,8,16,256]{4,3,2,1,0:T(8,128)S(1)}, f32[3,2,8,16,256]{4,3,2,1,0:T(8,128)S(1)}, u32[]{:S(2)}, u32[]{:S(2)}) collective-permute-start(f32[3,2,8,16,256]{4,3,2,1,0:T(8,128)S(1)} %copy-done.4), channel_id=1, source_target_pairs={{0,8},{1,9},{2,10},{3,11},{4,12},{5,13},{6,14},{7,15},{8,16},{9,17... | collective-permute-start | bytes 2359304 | tf_op jit(solution)/shard_map/ppermute | solution.py:263
  105.4 7.1 %collective-permute-done.5.refs_10_ = f32[3,2,8,16,256]{4,3,2,1,0:T(8,128)S(1)} collective-permute-done((f32[3,2,8,16,256]{4,3,2,1,0:T(8,128)S(1)}, f32[3,2,8,16,256]{4,3,2,1,0:T(8,128)S(1)}, u32[]{:S(2)}, u32[]{:S(2)}) %collective-permute-start.5) | collective-permute-done | bytes 786464 | tf_op jit(solution)/shard_map/ppermute | solution.py:264
  112.5 7.5 %collective-permute-done.4.refs_9_ = f32[3,2,8,16,256]{4,3,2,1,0:T(8,128)S(1)} collective-permute-done((f32[3,2,8,16,256]{4,3,2,1,0:T(8,128)S(1)}, f32[3,2,8,16,256]{4,3,2,1,0:T(8,128)S(1)}, u32[]{:S(2)}, u32[]{:S(2)}) %collective-permute-start.4) | collective-permute-done | bytes 786464 | tf_op jit(solution)/shard_map/ppermute | solution.py:263
  121.9 7.3 %second.2 = f32[8,3,2,4,8,256]{5,4,3,2,1,0:T(8,128)} custom-call(f32[3,4,8,16,256]{4,3,2,1,0:T(8,128)} %get-tuple-element.21.refs_0_, f32[3,2,8,16,256]{4,3,2,1,0:T(8,128)} %get-tuple-element.23.refs_1_, f32[3,2,8,16,256]{4,3,2,1,0:T(8,128)} %get-tuple-element.24.refs_2_, f32[3,4,8,16,256]{4,3,2,1,0:T(8,128)} %get-tuple-element.25.refs_3_, ...), custom_call_target="tpu_custom_call" | custom-call | flops 117964800 | bytes 9330688 | tf_op jit(solution)/shard_map/second/pallas_call | solution.py:221
  129.2 8.5 %all-to-all-start.3 = ((f32[8,3,2,4,8,256]{5,4,3,2,1,0:T(8,128)}), f32[8,3,2,4,8,256]{5,4,3,2,1,0:T(8,128)}, u32[]{:S(2)}, u32[]{:S(2)}) async-start(f32[8,3,2,4,8,256]{5,4,3,2,1,0:T(8,128)} %second.2), calls=%async_computation.3 | async-start | bytes 3145728 | tf_op jit(solution)/shard_map/all_to_all | solution.py:292
  137.7 2.7 %last.2.refs_2_ = f32[3,2,8,64,256]{4,3,2,1,0:T(8,128)} custom-call(f32[3,2,8,64,256]{4,3,2,1,0:T(8,128)} %refs_0_.7, f32[8,3,2,4,8,256]{5,4,3,2,1,0:T(8,128)} %copy-done.5), custom_call_target="tpu_custom_call" | custom-call | flops 393216 | bytes 7864320 | tf_op jit(solution)/shard_map/last/pallas_call | solution.py:221
  140.4 15.5 %all-to-all-done.3.refs_1_ = f32[8,3,2,4,8,256]{5,4,3,2,1,0:T(8,128)} async-done(((f32[8,3,2,4,8,256]{5,4,3,2,1,0:T(8,128)}), f32[8,3,2,4,8,256]{5,4,3,2,1,0:T(8,128)}, u32[]{:S(2)}, u32[]{:S(2)}) %all-to-all-start.3) | async-done | bytes 1572896 | tf_op jit(solution)/shard_map/all_to_all | solution.py:292
  155.9 2.7 %last.3 = f32[3,2,8,64,256]{4,3,2,1,0:T(8,128)} custom-call(f32[3,2,8,64,256]{4,3,2,1,0:T(8,128)} %refs_0_.7, f32[8,3,2,4,8,256]{5,4,3,2,1,0:T(8,128)} %all-to-all-done.3.refs_1_, f32[3,2,8,64,256]{4,3,2,1,0:T(8,128)} %last.2.refs_2_), custom_call_target="tpu_custom_call", output_to_operand_aliasing={{}: (2, {})} | custom-call | flops 393216 | bytes 7864320 | tf_op jit(solution)/shard_map/last/pallas_call | solution.py:221
  (51 shorter events, 12.1 us)
Async XLA Ops:
  0.0 55.9 %copy-start = (f32[3,8,16]{2,1,0:T(8,128)S(1)}, f32[3,8,16]{2,1,0:T(8,128)}, u32[]{:S(2)}) copy-start(f32[3,8,16]{2,1,0:T(8,128)} %param.10) | copy-start | bytes 4612
  4.3 5.8 %copy-start.1 = (f32[3,2,8,64,256]{4,3,2,1,0:T(8,128)S(1)}, f32[3,2,8,64,256]{4,3,2,1,0:T(8,128)}, u32[]{:S(2)}) copy-start(f32[3,2,8,64,256]{4,3,2,1,0:T(8,128)} %refs_0_.7) | copy-start | bytes 9437188
  4.3 43.5 %all-to-all-start = ((f32[8,3,2,5,8,256]{5,4,3,2,1,0:T(8,128)}), f32[8,3,2,5,8,256]{5,4,3,2,1,0:T(8,128)}, u32[]{:S(2)}, u32[]{:S(2)}) async-start(f32[8,3,2,5,8,256]{5,4,3,2,1,0:T(8,128)} %spread.3), calls=%async_computation | async-start | bytes 3932160 | tf_op jit(solution)/shard_map/all_to_all | solution.py:292
  11.6 11.3 %collective-permute-start.2 = (f32[3,2,2,64,256]{4,3,2,1,0:T(8,128)S(1)}, f32[3,2,2,64,256]{4,3,2,1,0:T(8,128)}, u32[]{:S(2)}, u32[]{:S(2)}) collective-permute-start(f32[3,2,2,64,256]{4,3,2,1,0:T(8,128)S(1)} %get-tuple-element.31), channel_id=1, source_target_pairs={{60,12},{68,116},{61,13},{69,117},{62,14},{70,118},{63,15},{71,119... | collective-permute-start | bytes 2359304 | tf_op jit(solution)/shard_map/ppermute | solution.py:265
  13.1 17.8 %collective-permute-start.1 = (f32[3,2,2,64,256]{4,3,2,1,0:T(8,128)}, f32[3,2,2,64,256]{4,3,2,1,0:T(8,128)S(1)}, u32[]{:S(2)}, u32[]{:S(2)}) collective-permute-start(f32[3,2,2,64,256]{4,3,2,1,0:T(8,128)} %get-tuple-element.32), channel_id=1, source_target_pairs={{8,0},{9,1},{10,2},{11,3},{12,4},{13,5},{14,6},{15,7},{16,8},{17,9... | collective-permute-start | bytes 2359304 | tf_op jit(solution)/shard_map/ppermute | solution.py:264
  16.0 24.6 %collective-permute-start = (f32[3,2,2,64,256]{4,3,2,1,0:T(8,128)}, f32[3,2,2,64,256]{4,3,2,1,0:T(8,128)S(1)}, u32[]{:S(2)}, u32[]{:S(2)}) collective-permute-start(f32[3,2,2,64,256]{4,3,2,1,0:T(8,128)} %get-tuple-element.33), channel_id=1, source_target_pairs={{0,8},{1,9},{2,10},{3,11},{4,12},{5,13},{6,14},{7,15},{8,16},{9,17... | collective-permute-start | bytes 2359304 | tf_op jit(solution)/shard_map/ppermute | solution.py:263
  22.9 17.7 %collective-permute-start.3 = (f32[3,2,2,64,256]{4,3,2,1,0:T(8,128)}, f32[3,2,2,64,256]{4,3,2,1,0:T(8,128)S(1)}, u32[]{:S(2)}, u32[]{:S(2)}) collective-permute-start(f32[3,2,2,64,256]{4,3,2,1,0:T(8,128)} %collective-permute-done.2), channel_id=1, source_target_pairs={{12,68},{116,60},{13,69},{117,61},{14,70},{118,62},{15,71},{119,63... | collective-permute-start | bytes 2359304 | tf_op jit(solution)/shard_map/ppermute | solution.py:266
  30.9 9.6 %copy-start.8 = (f32[3,2,2,64,256]{4,3,2,1,0:T(8,128)}, f32[3,2,2,64,256]{4,3,2,1,0:T(8,128)S(1)}, u32[]{:S(2)}) copy-start(f32[3,2,2,64,256]{4,3,2,1,0:T(8,128)S(1)} %collective-permute-done.1.refs_4_) | copy-start | bytes 2359300
  40.6 0.9 copy-start.9
  47.8 8.1 %copy-start.14 = (f32[16,16,16,1]{2,1,3,0:T(8,128)S(1)}, f32[16,16,16,1]{2,1,3,0:T(8,128)}, u32[]{:S(2)}) copy-start(f32[16,16,16,1]{2,1,3,0:T(8,128)} %constant.46) | copy-start | bytes 49156
  47.8 11.7 %copy-start.12 = (s32[8,64,256]{2,1,0:T(8,128)S(1)}, s32[8,64,256]{2,1,0:T(8,128)}, u32[]{:S(2)}) copy-start(s32[8,64,256]{2,1,0:T(8,128)} %param.11) | copy-start | bytes 1572868
  47.8 11.7 %copy-start.13 = (s32[8,64,256]{2,1,0:T(8,128)S(1)}, s32[8,64,256]{2,1,0:T(8,128)}, u32[]{:S(2)}) copy-start(s32[8,64,256]{2,1,0:T(8,128)} %param.12) | copy-start | bytes 1572868
  47.9 30.5 %all-to-all-start.1 = ((f32[8,3,2,5,8,256]{5,4,3,2,1,0:T(8,128)}), f32[8,3,2,5,8,256]{5,4,3,2,1,0:T(8,128)S(1)}, u32[]{:S(2)}, u32[]{:S(2)}) async-start(f32[8,3,2,5,8,256]{5,4,3,2,1,0:T(8,128)} %spread.2), calls=%async_computation.1 | async-start | bytes 3932160 | tf_op jit(solution)/shard_map/all_to_all | solution.py:292
  78.3 1.3 copy-start.2
  90.3 3.8 %copy-start.3 = (f32[3,2,8,16,256]{4,3,2,1,0:T(8,128)S(1)}, f32[3,2,8,16,256]{4,3,2,1,0:T(8,128)}, u32[]{:S(2)}) copy-start(f32[3,2,8,16,256]{4,3,2,1,0:T(8,128)} %get-tuple-element.23.refs_1_) | copy-start | bytes 2359300
  90.3 3.8 %copy-start.4 = (f32[3,2,8,16,256]{4,3,2,1,0:T(8,128)S(1)}, f32[3,2,8,16,256]{4,3,2,1,0:T(8,128)}, u32[]{:S(2)}) copy-start(f32[3,2,8,16,256]{4,3,2,1,0:T(8,128)} %get-tuple-element.24.refs_2_) | copy-start | bytes 2359300
  90.3 38.9 %all-to-all-start.2 = ((f32[8,3,2,4,8,256]{5,4,3,2,1,0:T(8,128)}), f32[8,3,2,4,8,256]{5,4,3,2,1,0:T(8,128)S(1)}, u32[]{:S(2)}, u32[]{:S(2)}) async-start(f32[8,3,2,4,8,256]{5,4,3,2,1,0:T(8,128)} %second.3), calls=%async_computation.2 | async-start | bytes 3145728 | tf_op jit(solution)/shard_map/all_to_all | solution.py:292
  94.2 10.5 %collective-permute-start.6 = (f32[3,2,8,16,256]{4,3,2,1,0:T(8,128)S(1)}, f32[3,2,8,16,256]{4,3,2,1,0:T(8,128)S(1)}, u32[]{:S(2)}, u32[]{:S(2)}) collective-permute-start(f32[3,2,8,16,256]{4,3,2,1,0:T(8,128)S(1)} %broadcast_select_fusion), channel_id=1, source_target_pairs={{60,12},{68,116},{61,13},{69,117},{62,14},{70,118},{63,15},{71,119... | collective-permute-start | bytes 2359304 | tf_op jit(solution)/shard_map/ppermute | solution.py:265
  94.9 17.6 %collective-permute-start.5 = (f32[3,2,8,16,256]{4,3,2,1,0:T(8,128)S(1)}, f32[3,2,8,16,256]{4,3,2,1,0:T(8,128)S(1)}, u32[]{:S(2)}, u32[]{:S(2)}) collective-permute-start(f32[3,2,8,16,256]{4,3,2,1,0:T(8,128)S(1)} %copy-done.3), channel_id=1, source_target_pairs={{8,0},{9,1},{10,2},{11,3},{12,4},{13,5},{14,6},{15,7},{16,8},{17,9... | collective-permute-start | bytes 2359304 | tf_op jit(solution)/shard_map/ppermute | solution.py:264
  97.4 22.6 %collective-permute-start.4 = (f32[3,2,8,16,256]{4,3,2,1,0:T(8,128)S(1)}, f32[3,2,8,16,256]{4,3,2,1,0:T(8,128)S(1)}, u32[]{:S(2)}, u32[]{:S(2)}) collective-permute-start(f32[3,2,8,16,256]{4,3,2,1,0:T(8,128)S(1)} %copy-done.4), channel_id=1, source_target_pairs={{0,8},{1,9},{2,10},{3,11},{4,12},{5,13},{6,14},{7,15},{8,16},{9,17... | collective-permute-start | bytes 2359304 | tf_op jit(solution)/shard_map/ppermute | solution.py:263
  104.7 15.4 %collective-permute-start.7 = (f32[3,2,8,16,256]{4,3,2,1,0:T(8,128)S(1)}, f32[3,2,8,16,256]{4,3,2,1,0:T(8,128)S(1)}, u32[]{:S(2)}, u32[]{:S(2)}) collective-permute-start(f32[3,2,8,16,256]{4,3,2,1,0:T(8,128)S(1)} %collective-permute-done.6), channel_id=1, source_target_pairs={{12,68},{116,60},{13,69},{117,61},{14,70},{118,62},{15,71},{119,63... | collective-permute-start | bytes 2359304 | tf_op jit(solution)/shard_map/ppermute | solution.py:266
  112.5 7.5 %copy-start.6 = (f32[3,2,8,16,256]{4,3,2,1,0:T(8,128)}, f32[3,2,8,16,256]{4,3,2,1,0:T(8,128)S(1)}, u32[]{:S(2)}) copy-start(f32[3,2,8,16,256]{4,3,2,1,0:T(8,128)S(1)} %collective-permute-done.5.refs_10_) | copy-start | bytes 2359300
  129.2 8.5 %copy-start.5 = (f32[8,3,2,4,8,256]{5,4,3,2,1,0:T(8,128)}, f32[8,3,2,4,8,256]{5,4,3,2,1,0:T(8,128)S(1)}, u32[]{:S(2)}) copy-start(f32[8,3,2,4,8,256]{5,4,3,2,1,0:T(8,128)S(1)} %all-to-all-done.2.refs_1_) | copy-start | bytes 4718596
  129.2 26.7 %all-to-all-start.3 = ((f32[8,3,2,4,8,256]{5,4,3,2,1,0:T(8,128)}), f32[8,3,2,4,8,256]{5,4,3,2,1,0:T(8,128)}, u32[]{:S(2)}, u32[]{:S(2)}) async-start(f32[8,3,2,4,8,256]{5,4,3,2,1,0:T(8,128)} %second.2), calls=%async_computation.3 | async-start | bytes 3145728 | tf_op jit(solution)/shard_map/all_to_all | solution.py:292
  (3 other events, 2.7 us)

commit v4 on v3

--- a/solution.py
+++ b/solution.py
@@ -13,6 +13,8 @@
 TIME_STEP = 0.1
 MOBILE_BASE = 0.7
 RUN = 8
+RELAYS = (((5, 2), (2, 5)), ((6, 1), (1, 6)))
+SHARED_LIMIT = 50 * 1024 * 1024
 VMEM_LIMIT = 61 * 1024 * 1024
 
 
@@ -59,7 +61,7 @@
 
 
 def spread_kernel(layers, f_ref, vel_ref, disp_ref, *rest):
-    lo_ref, hi_ref, around_ref, ends_ref = rest[:4] if len(rest) == 5 else (None,) * 4
+    lo_ref, hi_ref, *around_refs, ends_ref = rest[:5] if len(rest) == 6 else (None,) * 5
     out_ref = rest[-1]
     depth, rows, width = f_ref.shape[2:]
     blocks = out_ref.shape[0]
@@ -69,9 +71,9 @@
 
     def layer(e, x):
         if x < 0:
-            return lo_ref[0, e, x + 2] + ends_ref[0] * around_ref[0, e, x + 2]
+            return lo_ref[0, e, x + 2] + ends_ref[0] * around_refs[x + 2][0, e, 0]
         if x >= depth:
-            return hi_ref[0, e, x - depth] + ends_ref[1] * around_ref[0, e, x - depth]
+            return hi_ref[0, e, x - depth] + ends_ref[1] * around_refs[x - depth][0, e, 0]
         return f_ref[0, e, x]
 
     zero_row = jnp.zeros((1, width), jnp.float32)
@@ -97,11 +99,14 @@
     low = (value - high.astype(jnp.float32)).astype(jnp.bfloat16)
     stacked = jnp.concatenate([high, low, high], axis=0)
     mixed = jnp.dot(weights, stacked, preferred_element_type=jnp.float32)
-    picked = jnp.broadcast_to(cls_row, (modes, width))
-    total = jnp.zeros((modes, width), jnp.float32)
+    picked = jnp.broadcast_to(cls_row, (8, width))
+    totals = [jnp.zeros((8, width), jnp.float32)] * (modes // 8)
     for c in range(classes):
-        total = jnp.where(picked == c, mixed[c * modes : (c + 1) * modes], total)
-    return total
+        here = picked == c
+        for k in range(modes // 8):
+            at = c * modes + 8 * k
+            totals[k] = jnp.where(here, mixed[at : at + 8], totals[k])
+    return jnp.concatenate(totals, axis=0)
 
 
 def first_kernel(layers, r_ref, w_ref, cls_ref, l_ref, beside_ref, *g_refs):
@@ -127,7 +132,7 @@
 
 
 def second_kernel(layers, g_ref, low_ref, high_ref, l_ref, beside_ref, w_ref, cls_ref, vel_ref, disp_ref, *rest):
-    lo_ref, hi_ref, around_ref, ends_ref = rest[:4] if len(rest) == 5 else (None,) * 4
+    lo_ref, hi_ref, *around_refs, ends_ref = rest[:5] if len(rest) == 6 else (None,) * 5
     out_ref = rest[-1]
     inner, part, modes, width = g_ref.shape[1:]
     depth = inner + 4
@@ -137,14 +142,14 @@
 
     def at(x, y):
         if x < 0:
-            return lo_ref[0, x + 2, y] + ends_ref[0] * around_ref[0, x + 2, y]
+            return lo_ref[0, x + 2, y] + ends_ref[0] * around_refs[x + 2][0, 0, y]
         if x < 2:
             return low_ref[0, x, y]
         if x < depth - 2:
             return g_ref[0, x - 2, y]
         if x < depth:
             return high_ref[0, x - depth + 2, y]
-        return hi_ref[0, x - depth, y] + ends_ref[1] * around_ref[0, x - depth, y]
+        return hi_ref[0, x - depth, y] + ends_ref[1] * around_refs[x - depth][0, 0, y]
 
     for i, x in enumerate(layers):
         rows = []
@@ -170,7 +175,7 @@
         out_ref[0, :, :, rows] = f_ref[0, :, :, rows] + r_ref[b, 0]
 
 
-def staged(body, steps, inputs, outputs, flops, name, scalars=(), so_far=()):
+def staged(body, steps, inputs, outputs, flops, name, scalars=(), so_far=(), arrived=()):
     n_in, n_out = len(inputs), len(outputs)
 
     def kernel(*refs):
@@ -220,30 +225,33 @@
     moved = sum(4 * math.prod(a.shape) for a, *_ in (*inputs, *outputs))
     return pl.pallas_call(
         kernel,
-        in_specs=[hbm] * n_in + [pl.BlockSpec(memory_space=pltpu.SMEM)] * len(scalars) + [hbm] * len(so_far),
+        in_specs=[pl.BlockSpec(memory_space=pl.ANY) if k in arrived else hbm for k in range(n_in)]
+        + [pl.BlockSpec(memory_space=pltpu.SMEM)] * len(scalars) + [hbm] * len(so_far),
         out_specs=[hbm] * n_out,
         out_shape=[pltpu.HBM(shape.shape, shape.dtype) for shape, *_ in outputs],
         scratch_shapes=scratch + [pltpu.SemaphoreType.DMA((n_in + n_out, steps))],
         input_output_aliases={n_in + len(scalars): 0} if so_far else {},
-        compiler_params=pltpu.CompilerParams(vmem_limit_bytes=VMEM_LIMIT),
+        compiler_params=pltpu.CompilerParams(vmem_limit_bytes=SHARED_LIMIT if arrived else VMEM_LIMIT),
         cost_estimate=pl.CostEstimate(flops=flops, bytes_accessed=moved, transcendentals=0),
         name=name,
     )(*[array for array, *_ in inputs], *scalars, *so_far)
 
 
 def halo_routes(space, blocks):
-    direct, leave, arrive = [], [], []
+    direct, relayed = [], [([], []), ([], [])]
     for s in range(space - 1):
         for m in range(blocks):
             ends = (s * blocks + m, (s + 1) * blocks + m)
-            if (s + 1) % RUN or m < blocks // 2:
+            if (s + 1) % RUN:
                 direct.append(ends)
-            else:
-                near = (s + 2 - RUN) * blocks + m
-                far = (s + RUN - 1) * blocks + m
+                continue
+            for (leave, arrive), relays in zip(relayed, RELAYS):
+                up, down = relays[2 * m // blocks]
+                near = (s + 1 - RUN + up) * blocks + m
+                far = (s + 1 + down) * blocks + m
                 leave += [(ends[0], near), (ends[1], far)]
                 arrive += [(near, ends[1]), (far, ends[0])]
-    return direct, leave, arrive
+    return direct, relayed
 
 
 def on_device(field, velocity, dispersion, mobility, material, fixed_mask):
@@ -253,17 +261,21 @@
     blocks = lax.axis_size("mode")
     part = rows // blocks
     space = lax.axis_size("space")
-    direct, leave, arrive = halo_routes(space, blocks)
+    direct, relayed = halo_routes(space, blocks)
     back = [(b, a) for a, b in direct]
     both = ("space", "mode")
     place = lax.axis_index("space") % RUN
     ends = jnp.stack([place == 0, place == RUN - 1]).astype(jnp.float32)
 
-    def exchange(low, high):
+    def exchange(low, high, axis):
         lo = lax.ppermute(high, both, direct)
         hi = lax.ppermute(low, both, back)
-        around = lax.ppermute(jnp.where(place == RUN - 1, high, low), both, leave)
-        return lo, hi, lax.ppermute(around, both, arrive), ends
+        out = jnp.where(place == RUN - 1, high, low)
+        around = []
+        for layer, (leave, arrive) in enumerate(relayed):
+            piece = lax.slice_in_dim(out, layer, layer + 1, axis=axis)
+            around.append(lax.ppermute(lax.ppermute(piece, both, leave), both, arrive))
+        return lo, hi, *around, ends
 
     inner = tuple(range(2, depth - 2))
     outer = (0, 1, depth - 2, depth - 1)
@@ -296,11 +308,12 @@
         (out,) = staged(
             functools.partial(spread_kernel, layers),
             metals,
-            [by_metal(field), whole(velocity), whole(dispersion)] + [by_metal(h) for h in halos[:3]],
+            [by_metal(field), whole(velocity), whole(dispersion)] + [by_metal(h) for h in halos[:4]],
             [by_unit(sent)],
             20 * math.prod(sent.shape),
             "spread",
-            halos[3:],
+            halos[4:],
+            arrived=(3, 4, 5, 6) if halos else (),
         )
         return out
 
@@ -315,6 +328,7 @@
             [by_metal(s) for s in shapes],
             300 * math.prod(got.shape),
             "first",
+            arrived=(0,),
         )
 
     def run_second(layers, g, low, high, l, beside, *halos):
@@ -324,11 +338,12 @@
             metals,
             [by_metal(a) for a in (g, low, high, l, beside, weights)]
             + [whole(cls), whole(vel), whole(disp)]
-            + [by_metal(a) for a in halos[:3]],
+            + [by_metal(a) for a in halos[:4]],
             [by_unit(sent)],
             300 * math.prod(sent.shape),
             "second",
-            halos[3:],
+            halos[4:],
+            arrived=(9, 10, 11, 12) if halos else (),
         )
         return out
 
@@ -353,10 +368,11 @@
             math.prod(got.shape),
             "last",
             so_far=so_far,
+            arrived=(1,),
         )
         return out
 
-    sides = exchange(field[:, :, :2], field[:, :, depth - 2 :])
+    sides = exchange(field[:, :, :2], field[:, :, depth - 2 :], 2)
     got_inner = over_modes(run_spread(inner))
     spread_outer = run_spread(outer, *sides)
     spread_outer, got_inner = after((spread_outer, got_inner))
@@ -364,7 +380,7 @@
     l_inner, beside_inner, g = run_first(inner, got_inner, 1)
     g, got_outer = after((g, got_outer))
     l_outer, beside_outer, low, high = run_first(outer, got_outer, 2)
-    sides = exchange(low, high)
+    sides = exchange(low, high, 1)
     back_inner = over_modes(run_second(inner, g, low, high, l_inner, beside_inner))
     back_outer = run_second(outer, g, low, high, l_outer, beside_outer, *sides)
     back_outer, back_inner = after((back_outer, back_inner))

time: 161 us -> 150 us (0.932)
  the two profiles are of different devices: /device:TPU:71 before, /device:TPU:7 now
where the time goes in v4:
time: 150 us; the launch traced here: 149 us
  waiting for transfers between devices  63 us (42%)
  starting transfers between devices  42.3 us (28%)
  Pallas kernels  35.9 us (24%)
  other arithmetic  4.37 us (3%)
  local copies, waits for them, and re-layouts  2.17 us (1%)
    pallas_call x8, Pallas kernels, staged(): pl.pallas_call(kernel, in_specs=[pl.BlockSpec(memory_space=pl.ANY) if k i...  35.9 us
    all_to_all x4, waiting for transfers between devices, over_modes(): lax.all_to_all(array, 'mode', split_axis=0, concat_axis=0, tiled=True)  34.1 us
    ppermute x8, waiting for transfers between devices, exchange(): around.append(lax.ppermute(lax.ppermute(piece, both, leave), both, arrive))  28.9 us
    all_to_all x4, starting transfers between devices, over_modes(): lax.all_to_all(array, 'mode', split_axis=0, concat_axis=0, tiled=True)  21.9 us
    ppermute x8, starting transfers between devices, exchange(): around.append(lax.ppermute(lax.ppermute(piece, both, leave), both, arrive))  14.3 us
    ppermute x2, starting transfers between devices, exchange(): hi = lax.ppermute(low, both, back)  3.55 us
  transfers between devices with their start and end apart: 16, of which 8 were waited for; matrix products, arithmetic and copies ran while one was open for 4% of the time, Pallas kernels for 13%

profile of v4, /device:TPU:7, one launch (start us, length us, event | category | flops | bytes accessed | tf_op | source)
XLA Modules:
  0.0 149.1 jit_solution(11511722687246095892)
XLA Ops:
  0.0 4.2 %spread.3 = f32[8,3,2,5,8,256]{5,4,3,2,1,0:T(8,128)} custom-call(f32[3,2,8,64,256]{4,3,2,1,0:T(8,128)} %refs_0_.7, f32[8,64,256]{2,1,0:T(8,128)} %refs_1_.3, f32[8,64,256]{2,1,0:T(8,128)} %refs_2_.3), custom_call_target="tpu_custom_call" | custom-call | flops 9830400 | bytes 6160384 | tf_op jit(solution)/shard_map/spread/pallas_call | solution.py:226
  4.2 5.6 %all-to-all-start = ((f32[8,3,2,5,8,256]{5,4,3,2,1,0:T(8,128)}), f32[8,3,2,5,8,256]{5,4,3,2,1,0:T(8,128)S(1)}, u32[]{:S(2)}, u32[]{:S(2)}) async-start(f32[8,3,2,5,8,256]{5,4,3,2,1,0:T(8,128)} %spread.3), calls=%async_computation | async-start | bytes 3932160 | tf_op jit(solution)/shard_map/all_to_all | solution.py:304
  9.8 2.8 %broadcast_select_fusion.1 = (f32[3,2,2,64,256]{4,3,2,1,0:T(8,128)S(1)}, f32[3,2,2,64,256]{4,3,2,1,0:T(8,128)}, f32[3,2,2,64,256]{4,3,2,1,0:T(8,128)}) fusion(pred[]{:T(512)} %eq.23, f32[3,2,8,64,256]{4,3,2,1,0:T(8,128)} %refs_0_.7), kind=kLoop, calls=%fused_computation.6 | loop fusion | flops 196608 | bytes 3932161 | tf_op jit(solution)/shard_map/jit(_where)/select_n | solution.py:273
  12.7 3.6 %collective-permute-start.4 = (f32[3,2,1,64,256]{4,3,2,1,0:T(8,128)S(1)}, f32[3,2,1,64,256]{4,3,2,1,0:T(8,128)}, u32[]{:S(2)}, u32[]{:S(2)}) collective-permute-start(f32[3,2,1,64,256]{4,3,2,1,0:T(8,128)S(1)} %get-tuple-element.36), channel_id=1, source_target_pairs={{56,48},{64,72},{57,49},{65,73},{58,50},{66,74},{59,51},{67,75},{6... | collective-permute-start | bytes 1179656 | tf_op jit(solution)/shard_map/ppermute | solution.py:277
  18.4 2.2 %collective-permute-start.1 = (f32[3,2,2,64,256]{4,3,2,1,0:T(8,128)}, f32[3,2,2,64,256]{4,3,2,1,0:T(8,128)}, u32[]{:S(2)}, u32[]{:S(2)}) collective-permute-start(f32[3,2,2,64,256]{4,3,2,1,0:T(8,128)} %get-tuple-element.32), channel_id=1, source_target_pairs={{8,0},{9,1},{10,2},{11,3},{12,4},{13,5},{14,6},{15,7},{16,8},{17,9... | collective-permute-start | bytes 2359304 | tf_op jit(solution)/shard_map/ppermute | solution.py:272
  23.2 2.3 %collective-permute-done.2 = f32[3,2,1,64,256]{4,3,2,1,0:T(8,128)} collective-permute-done((f32[3,2,1,64,256]{4,3,2,1,0:T(8,128)S(1)}, f32[3,2,1,64,256]{4,3,2,1,0:T(8,128)}, u32[]{:S(2)}, u32[]{:S(2)}) %collective-permute-start.2) | collective-permute-done | bytes 393248 | tf_op jit(solution)/shard_map/ppermute | solution.py:277
  26.9 6.9 %collective-permute-done.5.refs_6_ = f32[3,2,1,64,256]{4,3,2,1,0:T(8,128)S(1)} collective-permute-done((f32[3,2,1,64,256]{4,3,2,1,0:T(8,128)}, f32[3,2,1,64,256]{4,3,2,1,0:T(8,128)S(1)}, u32[]{:S(2)}, u32[]{:S(2)}) %collective-permute-start.5) | collective-permute-done | bytes 393248 | tf_op jit(solution)/shard_map/ppermute | solution.py:277
  33.8 4.6 %collective-permute-done.3.refs_5_ = f32[3,2,1,64,256]{4,3,2,1,0:T(8,128)} collective-permute-done((f32[3,2,1,64,256]{4,3,2,1,0:T(8,128)}, f32[3,2,1,64,256]{4,3,2,1,0:T(8,128)}, u32[]{:S(2)}, u32[]{:S(2)}) %collective-permute-start.3) | collective-permute-done | bytes 393248 | tf_op jit(solution)/shard_map/ppermute | solution.py:277
  38.4 4.9 %spread.2 = f32[8,3,2,5,8,256]{5,4,3,2,1,0:T(8,128)} custom-call(f32[3,2,8,64,256]{4,3,2,1,0:T(8,128)} %refs_0_.7, f32[8,64,256]{2,1,0:T(8,128)S(1)} %copy-done.7, f32[8,64,256]{2,1,0:T(8,128)S(1)} %copy-done.8, f32[3,2,2,64,256]{4,3,2,1,0:T(8,128)} %collective-permute-done.refs_3_, f32[3,2,2,64,256]{4,3,2,1,0:T(8,128)} %collective-permute-done.1.refs_4_, ...), custom_call_target="tpu_custom_call" | custom-call | flops 9830400 | bytes 8519680 | tf_op jit(solution)/shard_map/spread/pallas_call | solution.py:226
  43.3 6.7 %all-to-all-start.1 = ((f32[8,3,2,5,8,256]{5,4,3,2,1,0:T(8,128)}), f32[8,3,2,5,8,256]{5,4,3,2,1,0:T(8,128)}, u32[]{:S(2)}, u32[]{:S(2)}) async-start(f32[8,3,2,5,8,256]{5,4,3,2,1,0:T(8,128)} %spread.2), calls=%async_computation.1 | async-start | bytes 3932160 | tf_op jit(solution)/shard_map/all_to_all | solution.py:304
  53.5 4.0 %first.2 = (f32[3,4,8,16,256]{4,3,2,1,0:T(8,128)}, f32[3,4,2,16,256]{4,3,2,1,0:T(8,128)}, f32[3,4,8,16,256]{4,3,2,1,0:T(8,128)}) custom-call(f32[8,3,2,5,8,256]{5,4,3,2,1,0:T(8,128)S(1)} %all-to-all-done.refs_0_, bf16[3,128,48]{2,1,0:T(8,128)(2,1)S(1)} %copy.15.refs_1_.refs_5_, s32[8,10,256]{2,1,0:T(8,128)S(1)} %pad_dynamic-slice_fusion.refs_2_.refs_6_), custom_call_target="tpu_custom_call" | custom-call | flops 147456000 | bytes 5660672 | tf_op jit(solution)/shard_map/first/pallas_call | solution.py:226
  57.5 15.9 %all-to-all-done.1.refs_0_ = f32[8,3,2,5,8,256]{5,4,3,2,1,0:T(8,128)} async-done(((f32[8,3,2,5,8,256]{5,4,3,2,1,0:T(8,128)}), f32[8,3,2,5,8,256]{5,4,3,2,1,0:T(8,128)}, u32[]{:S(2)}, u32[]{:S(2)}) %all-to-all-start.1) | async-done | bytes 1966112 | tf_op jit(solution)/shard_map/all_to_all | solution.py:304
  73.4 4.7 %first.3 = (f32[3,4,8,16,256]{4,3,2,1,0:T(8,128)}, f32[3,4,2,16,256]{4,3,2,1,0:T(8,128)}, f32[3,2,8,16,256]{4,3,2,1,0:T(8,128)}, f32[3,2,8,16,256]{4,3,2,1,0:T(8,128)}) custom-call(f32[8,3,2,5,8,256]{5,4,3,2,1,0:T(8,128)} %all-to-all-done.1.refs_0_, bf16[3,128,48]{2,1,0:T(8,128)(2,1)S(1)} %copy.15.refs_1_.refs_5_, ...), custom_call_target="tpu_custom_call" | custom-call | flops 147456000 | bytes 5660672 | tf_op jit(solution)/shard_map/first/pallas_call | solution.py:226
  78.2 5.7 %second.3 = f32[8,3,2,4,8,256]{5,4,3,2,1,0:T(8,128)} custom-call(f32[3,4,8,16,256]{4,3,2,1,0:T(8,128)} %get-tuple-element.21.refs_0_, f32[3,2,8,16,256]{4,3,2,1,0:T(8,128)} %get-tuple-element.23.refs_1_, f32[3,2,8,16,256]{4,3,2,1,0:T(8,128)} %get-tuple-element.24.refs_2_, f32[3,4,8,16,256]{4,3,2,1,0:T(8,128)} %get-tuple-element.27.refs_3_, ...), custom_call_target="tpu_custom_call" | custom-call | flops 117964800 | bytes 6971392 | tf_op jit(solution)/shard_map/second/pallas_call | solution.py:226
  83.9 4.4 %all-to-all-start.2 = ((f32[8,3,2,4,8,256]{5,4,3,2,1,0:T(8,128)}), f32[8,3,2,4,8,256]{5,4,3,2,1,0:T(8,128)}, u32[]{:S(2)}, u32[]{:S(2)}) async-start(f32[8,3,2,4,8,256]{5,4,3,2,1,0:T(8,128)} %second.3), calls=%async_computation.2 | async-start | bytes 3145728 | tf_op jit(solution)/shard_map/all_to_all | solution.py:304
  88.6 2.2 %collective-permute-start.10 = (f32[3,1,8,16,256]{4,3,2,1,0:T(8,128)S(1)}, f32[3,1,8,16,256]{4,3,2,1,0:T(8,128)S(1)}, u32[]{:S(2)}, u32[]{:S(2)}) collective-permute-start(f32[3,1,8,16,256]{4,3,2,1,0:T(8,128)S(1)} %get-tuple-element.34), channel_id=1, source_target_pairs={{56,48},{64,72},{57,49},{65,73},{58,50},{66,74},{59,51},{67,75},{6... | collective-permute-start | bytes 1179656 | tf_op jit(solution)/shard_map/ppermute | solution.py:277
  96.1 4.1 %collective-permute-done.8 = f32[3,1,8,16,256]{4,3,2,1,0:T(8,128)S(1)} collective-permute-done((f32[3,1,8,16,256]{4,3,2,1,0:T(8,128)S(1)}, f32[3,1,8,16,256]{4,3,2,1,0:T(8,128)S(1)}, u32[]{:S(2)}, u32[]{:S(2)}) %collective-permute-start.8) | collective-permute-done | bytes 393248 | tf_op jit(solution)/shard_map/ppermute | solution.py:277
  101.4 5.0 %collective-permute-done.11.refs_12_ = f32[3,1,8,16,256]{4,3,2,1,0:T(8,128)S(1)} collective-permute-done((f32[3,1,8,16,256]{4,3,2,1,0:T(8,128)S(1)}, f32[3,1,8,16,256]{4,3,2,1,0:T(8,128)S(1)}, u32[]{:S(2)}, u32[]{:S(2)}) %collective-permute-start.11) | collective-permute-done | bytes 393248 | tf_op jit(solution)/shard_map/ppermute | solution.py:277
  106.4 6.1 %collective-permute-done.9.refs_11_ = f32[3,1,8,16,256]{4,3,2,1,0:T(8,128)S(1)} collective-permute-done((f32[3,1,8,16,256]{4,3,2,1,0:T(8,128)S(1)}, f32[3,1,8,16,256]{4,3,2,1,0:T(8,128)S(1)}, u32[]{:S(2)}, u32[]{:S(2)}) %collective-permute-start.9) | collective-permute-done | bytes 393248 | tf_op jit(solution)/shard_map/ppermute | solution.py:277
  113.4 7.3 %second.2 = f32[8,3,2,4,8,256]{5,4,3,2,1,0:T(8,128)} custom-call(f32[3,4,8,16,256]{4,3,2,1,0:T(8,128)} %get-tuple-element.21.refs_0_, f32[3,2,8,16,256]{4,3,2,1,0:T(8,128)S(1)} %copy-done.1, f32[3,2,8,16,256]{4,3,2,1,0:T(8,128)S(1)} %copy-done.2, f32[3,4,8,16,256]{4,3,2,1,0:T(8,128)} %get-tuple-element.25.refs_3_, f32[3,4,2,16,256]{4,3,2,1,0:T(8,128)S(1)} %copy-done.11, ...), custom_call_target="tpu_custom_call" | custom-call | flops 117964800 | bytes 9330688 | tf_op jit(solution)/shard_map/second/pallas_call | solution.py:226
  120.8 5.2 %all-to-all-start.3 = ((f32[8,3,2,4,8,256]{5,4,3,2,1,0:T(8,128)}), f32[8,3,2,4,8,256]{5,4,3,2,1,0:T(8,128)S(1)}, u32[]{:S(2)}, u32[]{:S(2)}) async-start(f32[8,3,2,4,8,256]{5,4,3,2,1,0:T(8,128)} %second.2), calls=%async_computation.3 | async-start | bytes 3145728 | tf_op jit(solution)/shard_map/all_to_all | solution.py:304
  126.0 2.7 %last.2.refs_2_ = f32[3,2,8,64,256]{4,3,2,1,0:T(8,128)} custom-call(f32[3,2,8,64,256]{4,3,2,1,0:T(8,128)} %refs_0_.7, f32[8,3,2,4,8,256]{5,4,3,2,1,0:T(8,128)} %all-to-all-done.2.refs_1_), custom_call_target="tpu_custom_call" | custom-call | flops 393216 | bytes 7864320 | tf_op jit(solution)/shard_map/last/pallas_call | solution.py:226
  128.7 18.1 %all-to-all-done.3.refs_1_ = f32[8,3,2,4,8,256]{5,4,3,2,1,0:T(8,128)S(1)} async-done(((f32[8,3,2,4,8,256]{5,4,3,2,1,0:T(8,128)}), f32[8,3,2,4,8,256]{5,4,3,2,1,0:T(8,128)S(1)}, u32[]{:S(2)}, u32[]{:S(2)}) %all-to-all-start.3) | async-done | bytes 1572896 | tf_op jit(solution)/shard_map/all_to_all | solution.py:304
  146.9 2.3 %last.3 = f32[3,2,8,64,256]{4,3,2,1,0:T(8,128)} custom-call(f32[3,2,8,64,256]{4,3,2,1,0:T(8,128)} %refs_0_.7, f32[8,3,2,4,8,256]{5,4,3,2,1,0:T(8,128)S(1)} %all-to-all-done.3.refs_1_, f32[3,2,8,64,256]{4,3,2,1,0:T(8,128)} %last.2.refs_2_), custom_call_target="tpu_custom_call", output_to_operand_aliasing={{}: (2, {})} | custom-call | flops 393216 | bytes 7864320 | tf_op jit(solution)/shard_map/last/pallas_call | solution.py:226
  (59 shorter events, 17.2 us)
Async XLA Ops:
  0.0 50.0 %copy-start = (f32[3,8,16]{2,1,0:T(8,128)S(1)}, f32[3,8,16]{2,1,0:T(8,128)}, u32[]{:S(2)}) copy-start(f32[3,8,16]{2,1,0:T(8,128)} %param.10) | copy-start | bytes 4612
  4.2 39.1 %all-to-all-start = ((f32[8,3,2,5,8,256]{5,4,3,2,1,0:T(8,128)}), f32[8,3,2,5,8,256]{5,4,3,2,1,0:T(8,128)S(1)}, u32[]{:S(2)}, u32[]{:S(2)}) async-start(f32[8,3,2,5,8,256]{5,4,3,2,1,0:T(8,128)} %spread.3), calls=%async_computation | async-start | bytes 3932160 | tf_op jit(solution)/shard_map/all_to_all | solution.py:304
  9.8 28.6 %copy-start.7 = (f32[8,64,256]{2,1,0:T(8,128)S(1)}, f32[8,64,256]{2,1,0:T(8,128)}, u32[]{:S(2)}) copy-start(f32[8,64,256]{2,1,0:T(8,128)} %refs_1_.3) | copy-start | bytes 1572868
  9.8 28.6 %copy-start.8 = (f32[8,64,256]{2,1,0:T(8,128)S(1)}, f32[8,64,256]{2,1,0:T(8,128)}, u32[]{:S(2)}) copy-start(f32[8,64,256]{2,1,0:T(8,128)} %refs_2_.3) | copy-start | bytes 1572868
  12.7 9.2 %collective-permute-start.4 = (f32[3,2,1,64,256]{4,3,2,1,0:T(8,128)S(1)}, f32[3,2,1,64,256]{4,3,2,1,0:T(8,128)}, u32[]{:S(2)}, u32[]{:S(2)}) collective-permute-start(f32[3,2,1,64,256]{4,3,2,1,0:T(8,128)S(1)} %get-tuple-element.36), channel_id=1, source_target_pairs={{56,48},{64,72},{57,49},{65,73},{58,50},{66,74},{59,51},{67,75},{6... | collective-permute-start | bytes 1179656 | tf_op jit(solution)/shard_map/ppermute | solution.py:277
  16.4 9.1 %collective-permute-start.2 = (f32[3,2,1,64,256]{4,3,2,1,0:T(8,128)S(1)}, f32[3,2,1,64,256]{4,3,2,1,0:T(8,128)}, u32[]{:S(2)}, u32[]{:S(2)}) collective-permute-start(f32[3,2,1,64,256]{4,3,2,1,0:T(8,128)S(1)} %get-tuple-element.37), channel_id=1, source_target_pairs={{56,40},{64,80},{57,41},{65,81},{58,42},{66,82},{59,43},{67,83},{6... | collective-permute-start | bytes 1179656 | tf_op jit(solution)/shard_map/ppermute | solution.py:277
  18.4 19.9 %collective-permute-start.1 = (f32[3,2,2,64,256]{4,3,2,1,0:T(8,128)}, f32[3,2,2,64,256]{4,3,2,1,0:T(8,128)}, u32[]{:S(2)}, u32[]{:S(2)}) collective-permute-start(f32[3,2,2,64,256]{4,3,2,1,0:T(8,128)} %get-tuple-element.32), channel_id=1, source_target_pairs={{8,0},{9,1},{10,2},{11,3},{12,4},{13,5},{14,6},{15,7},{16,8},{17,9... | collective-permute-start | bytes 2359304 | tf_op jit(solution)/shard_map/ppermute | solution.py:272
  20.6 17.7 %collective-permute-start = (f32[3,2,2,64,256]{4,3,2,1,0:T(8,128)}, f32[3,2,2,64,256]{4,3,2,1,0:T(8,128)}, u32[]{:S(2)}, u32[]{:S(2)}) collective-permute-start(f32[3,2,2,64,256]{4,3,2,1,0:T(8,128)} %get-tuple-element.33), channel_id=1, source_target_pairs={{0,8},{1,9},{2,10},{3,11},{4,12},{5,13},{6,14},{7,15},{8,16},{9,17... | collective-permute-start | bytes 2359304 | tf_op jit(solution)/shard_map/ppermute | solution.py:271
  21.9 11.8 %collective-permute-start.5 = (f32[3,2,1,64,256]{4,3,2,1,0:T(8,128)}, f32[3,2,1,64,256]{4,3,2,1,0:T(8,128)S(1)}, u32[]{:S(2)}, u32[]{:S(2)}) collective-permute-start(f32[3,2,1,64,256]{4,3,2,1,0:T(8,128)} %collective-permute-done.4), channel_id=1, source_target_pairs={{48,64},{72,56},{49,65},{73,57},{50,66},{74,58},{51,67},{75,59},{1... | collective-permute-start | bytes 1179656 | tf_op jit(solution)/shard_map/ppermute | solution.py:277
  25.5 12.8 %collective-permute-start.3 = (f32[3,2,1,64,256]{4,3,2,1,0:T(8,128)}, f32[3,2,1,64,256]{4,3,2,1,0:T(8,128)}, u32[]{:S(2)}, u32[]{:S(2)}) collective-permute-start(f32[3,2,1,64,256]{4,3,2,1,0:T(8,128)} %collective-permute-done.2), channel_id=1, source_target_pairs={{40,64},{80,56},{41,65},{81,57},{42,66},{82,58},{43,67},{83,59},{2... | collective-permute-start | bytes 1179656 | tf_op jit(solution)/shard_map/ppermute | solution.py:277
  43.3 30.1 %all-to-all-start.1 = ((f32[8,3,2,5,8,256]{5,4,3,2,1,0:T(8,128)}), f32[8,3,2,5,8,256]{5,4,3,2,1,0:T(8,128)}, u32[]{:S(2)}, u32[]{:S(2)}) async-start(f32[8,3,2,5,8,256]{5,4,3,2,1,0:T(8,128)} %spread.2), calls=%async_computation.1 | async-start | bytes 3932160 | tf_op jit(solution)/shard_map/all_to_all | solution.py:304
  83.9 36.9 %all-to-all-start.2 = ((f32[8,3,2,4,8,256]{5,4,3,2,1,0:T(8,128)}), f32[8,3,2,4,8,256]{5,4,3,2,1,0:T(8,128)}, u32[]{:S(2)}, u32[]{:S(2)}) async-start(f32[8,3,2,4,8,256]{5,4,3,2,1,0:T(8,128)} %second.3), calls=%async_computation.2 | async-start | bytes 3145728 | tf_op jit(solution)/shard_map/all_to_all | solution.py:304
  88.3 25.1 %copy-start.4 = (s32[8,10,256]{2,1,0:T(8,128)S(1)}, s32[8,10,256]{2,1,0:T(8,128)}, u32[]{:S(2)}) copy-start(s32[8,10,256]{2,1,0:T(8,128)} %copy-done.3) | copy-start | bytes 245764
  88.3 25.1 %copy-start.6 = (bf16[3,128,48]{2,1,0:T(8,128)(2,1)S(1)}, bf16[3,128,48]{2,1,0:T(8,128)(2,1)}, u32[]{:S(2)}) copy-start(bf16[3,128,48]{2,1,0:T(8,128)(2,1)} %copy-done.5) | copy-start | bytes 110596
  88.4 25.1 %copy-start.9 = (f32[8,8,256]{2,1,0:T(8,128)S(1)}, f32[8,8,256]{2,1,0:T(8,128)}, u32[]{:S(2)}) copy-start(f32[8,8,256]{2,1,0:T(8,128)} %get-tuple-element.40.refs_7_) | copy-start | bytes 196612
  88.4 25.1 %copy-start.10 = (f32[8,8,256]{2,1,0:T(8,128)S(1)}, f32[8,8,256]{2,1,0:T(8,128)}, u32[]{:S(2)}) copy-start(f32[8,8,256]{2,1,0:T(8,128)} %get-tuple-element.41.refs_8_) | copy-start | bytes 196612
  88.4 25.1 %copy-start.11 = (f32[3,4,2,16,256]{4,3,2,1,0:T(8,128)S(1)}, f32[3,4,2,16,256]{4,3,2,1,0:T(8,128)}, u32[]{:S(2)}) copy-start(f32[3,4,2,16,256]{4,3,2,1,0:T(8,128)} %get-tuple-element.26.refs_4_) | copy-start | bytes 1179652
  88.6 6.1 %collective-permute-start.10 = (f32[3,1,8,16,256]{4,3,2,1,0:T(8,128)S(1)}, f32[3,1,8,16,256]{4,3,2,1,0:T(8,128)S(1)}, u32[]{:S(2)}, u32[]{:S(2)}) collective-permute-start(f32[3,1,8,16,256]{4,3,2,1,0:T(8,128)S(1)} %get-tuple-element.34), channel_id=1, source_target_pairs={{56,48},{64,72},{57,49},{65,73},{58,50},{66,74},{59,51},{67,75},{6... | collective-permute-start | bytes 1179656 | tf_op jit(solution)/shard_map/ppermute | solution.py:277
  90.8 9.4 %collective-permute-start.8 = (f32[3,1,8,16,256]{4,3,2,1,0:T(8,128)S(1)}, f32[3,1,8,16,256]{4,3,2,1,0:T(8,128)S(1)}, u32[]{:S(2)}, u32[]{:S(2)}) collective-permute-start(f32[3,1,8,16,256]{4,3,2,1,0:T(8,128)S(1)} %get-tuple-element.35), channel_id=1, source_target_pairs={{56,40},{64,80},{57,41},{65,81},{58,42},{66,82},{59,43},{67,83},{6... | collective-permute-start | bytes 1179656 | tf_op jit(solution)/shard_map/ppermute | solution.py:277
  92.1 20.4 %collective-permute-start.7 = (f32[3,2,8,16,256]{4,3,2,1,0:T(8,128)S(1)}, f32[3,2,8,16,256]{4,3,2,1,0:T(8,128)S(1)}, u32[]{:S(2)}, u32[]{:S(2)}) collective-permute-start(f32[3,2,8,16,256]{4,3,2,1,0:T(8,128)S(1)} %copy-done.1), channel_id=1, source_target_pairs={{8,0},{9,1},{10,2},{11,3},{12,4},{13,5},{14,6},{15,7},{16,8},{17,9... | collective-permute-start | bytes 2359304 | tf_op jit(solution)/shard_map/ppermute | solution.py:272
  93.5 19.1 %collective-permute-start.6 = (f32[3,2,8,16,256]{4,3,2,1,0:T(8,128)S(1)}, f32[3,2,8,16,256]{4,3,2,1,0:T(8,128)S(1)}, u32[]{:S(2)}, u32[]{:S(2)}) collective-permute-start(f32[3,2,8,16,256]{4,3,2,1,0:T(8,128)S(1)} %copy-done.2), channel_id=1, source_target_pairs={{0,8},{1,9},{2,10},{3,11},{4,12},{5,13},{6,14},{7,15},{8,16},{9,17... | collective-permute-start | bytes 2359304 | tf_op jit(solution)/shard_map/ppermute | solution.py:271
  94.8 11.6 %collective-permute-start.11 = (f32[3,1,8,16,256]{4,3,2,1,0:T(8,128)S(1)}, f32[3,1,8,16,256]{4,3,2,1,0:T(8,128)S(1)}, u32[]{:S(2)}, u32[]{:S(2)}) collective-permute-start(f32[3,1,8,16,256]{4,3,2,1,0:T(8,128)S(1)} %collective-permute-done.10), channel_id=1, source_target_pairs={{48,64},{72,56},{49,65},{73,57},{50,66},{74,58},{51,67},{75,59},{1... | collective-permute-start | bytes 1179656 | tf_op jit(solution)/shard_map/ppermute | solution.py:277
  100.2 12.4 %collective-permute-start.9 = (f32[3,1,8,16,256]{4,3,2,1,0:T(8,128)S(1)}, f32[3,1,8,16,256]{4,3,2,1,0:T(8,128)S(1)}, u32[]{:S(2)}, u32[]{:S(2)}) collective-permute-start(f32[3,1,8,16,256]{4,3,2,1,0:T(8,128)S(1)} %collective-permute-done.8), channel_id=1, source_target_pairs={{40,64},{80,56},{41,65},{81,57},{42,66},{82,58},{43,67},{83,59},{2... | collective-permute-start | bytes 1179656 | tf_op jit(solution)/shard_map/ppermute | solution.py:277
  120.8 26.1 %all-to-all-start.3 = ((f32[8,3,2,4,8,256]{5,4,3,2,1,0:T(8,128)}), f32[8,3,2,4,8,256]{5,4,3,2,1,0:T(8,128)S(1)}, u32[]{:S(2)}, u32[]{:S(2)}) async-start(f32[8,3,2,4,8,256]{5,4,3,2,1,0:T(8,128)} %second.2), calls=%async_computation.3 | async-start | bytes 3145728 | tf_op jit(solution)/shard_map/all_to_all | solution.py:304
  (6 other events, 63.1 us)

commit v5 on v4

--- a/solution.py
+++ b/solution.py
@@ -13,7 +13,7 @@
 TIME_STEP = 0.1
 MOBILE_BASE = 0.7
 RUN = 8
-RELAYS = (((5, 2), (2, 5)), ((6, 1), (1, 6)))
+RELAYS = (((6, 1), (1, 6)), ((5, 2), (2, 5)))
 SHARED_LIMIT = 50 * 1024 * 1024
 VMEM_LIMIT = 61 * 1024 * 1024
 
@@ -175,7 +175,7 @@
         out_ref[0, :, :, rows] = f_ref[0, :, :, rows] + r_ref[b, 0]
 
 
-def staged(body, steps, inputs, outputs, flops, name, scalars=(), so_far=(), arrived=()):
+def staged(body, steps, inputs, outputs, flops, name, scalars=(), so_far=(), arrived=(), limit=SHARED_LIMIT):
     n_in, n_out = len(inputs), len(outputs)
 
     def kernel(*refs):
@@ -231,7 +231,7 @@
         out_shape=[pltpu.HBM(shape.shape, shape.dtype) for shape, *_ in outputs],
         scratch_shapes=scratch + [pltpu.SemaphoreType.DMA((n_in + n_out, steps))],
         input_output_aliases={n_in + len(scalars): 0} if so_far else {},
-        compiler_params=pltpu.CompilerParams(vmem_limit_bytes=SHARED_LIMIT if arrived else VMEM_LIMIT),
+        compiler_params=pltpu.CompilerParams(vmem_limit_bytes=limit if arrived else VMEM_LIMIT),
         cost_estimate=pl.CostEstimate(flops=flops, bytes_accessed=moved, transcendentals=0),
         name=name,
     )(*[array for array, *_ in inputs], *scalars, *so_far)
@@ -346,6 +346,28 @@
             arrived=(9, 10, 11, 12) if halos else (),
         )
         return out
+
+    def run_middle(got, g, l, beside):
+        sent = f32(blocks, metals, each, len(inner), part, width)
+        shapes = [f32(metals, len(outer), part, modes, width), f32(metals, len(outer), 2, modes, width)]
+        shapes += [f32(metals, 2, part, modes, width)] * 2
+
+        def body(got, w, cls, g, l, beside, vel, disp, l_outer, beside_outer, low, high, out):
+            first_kernel(outer, got, w, cls, l_outer, beside_outer, low, high)
+            second_kernel(inner, g, low, high, l, beside, w, cls, vel, disp, out)
+
+        return staged(
+            body,
+            metals,
+            [by_unit(got), by_metal(weights), whole(cls)]
+            + [by_metal(a) for a in (g, l, beside)]
+            + [whole(vel), whole(disp)],
+            [by_metal(s) for s in shapes] + [by_unit(sent)],
+            600 * math.prod(got.shape),
+            "middle",
+            arrived=(0,),
+            limit=58 * 1024 * 1024,
+        )
 
     def run_last(pair, got, *so_far):
         block = (1, each, 2, rows, width)
@@ -379,9 +401,9 @@
     got_outer = over_modes(spread_outer)
     l_inner, beside_inner, g = run_first(inner, got_inner, 1)
     g, got_outer = after((g, got_outer))
-    l_outer, beside_outer, low, high = run_first(outer, got_outer, 2)
+    l_outer, beside_outer, low, high, back_inner = run_middle(got_outer, g, l_inner, beside_inner)
     sides = exchange(low, high, 1)
-    back_inner = over_modes(run_second(inner, g, low, high, l_inner, beside_inner))
+    back_inner = over_modes(back_inner)
     back_outer = run_second(outer, g, low, high, l_outer, beside_outer, *sides)
     back_outer, back_inner = after((back_outer, back_inner))
     back_outer = over_modes(back_outer)

time: 150 us -> 146 us (0.973)
  the two profiles are of different devices: /device:TPU:7 before, /device:TPU:71 now
where the time goes in v5:
time: 146 us; the launch traced here: 145 us
  waiting for transfers between devices  64 us (44%)
  starting transfers between devices  40 us (27%)
  Pallas kernels  33.5 us (23%)
  other arithmetic  4.37 us (3%)
  local copies, waits for them, and re-layouts  2.16 us (1%)
    pallas_call x7, Pallas kernels, staged(): pl.pallas_call(kernel, in_specs=[pl.BlockSpec(memory_space=pl.ANY) if k i...  33.5 us
    all_to_all x4, waiting for transfers between devices, over_modes(): lax.all_to_all(array, 'mode', split_axis=0, concat_axis=0, tiled=True)  32.4 us
    ppermute x8, waiting for transfers between devices, exchange(): around.append(lax.ppermute(lax.ppermute(piece, both, leave), both, arrive))  31.5 us
    all_to_all x4, starting transfers between devices, over_modes(): lax.all_to_all(array, 'mode', split_axis=0, concat_axis=0, tiled=True)  20.2 us
    ppermute x8, starting transfers between devices, exchange(): around.append(lax.ppermute(lax.ppermute(piece, both, leave), both, arrive))  13.7 us
    ppermute x2, starting transfers between devices, exchange(): hi = lax.ppermute(low, both, back)  3.55 us
    select_n x2, other arithmetic, exchange(): out = jnp.where(place == RUN - 1, high, low)  3 us
  transfers between devices with their start and end apart: 16, of which 7 were waited for; matrix products, arithmetic and copies ran while one was open for 5% of the time, Pallas kernels for 13%

profile of v5, /device:TPU:71, one launch (start us, length us, event | category | flops | bytes accessed | tf_op | source)
XLA Modules:
  0.0 145.4 jit_solution(166383356006329482)
XLA Ops:
  0.0 4.2 %spread.3 = f32[8,3,2,5,8,256]{5,4,3,2,1,0:T(8,128)} custom-call(f32[3,2,8,64,256]{4,3,2,1,0:T(8,128)} %refs_0_.7, f32[8,64,256]{2,1,0:T(8,128)} %refs_1_.3, f32[8,64,256]{2,1,0:T(8,128)} %refs_2_.3), custom_call_target="tpu_custom_call" | custom-call | flops 9830400 | bytes 6160384 | tf_op jit(solution)/shard_map/spread/pallas_call | solution.py:226
  4.2 5.6 %all-to-all-start = ((f32[8,3,2,5,8,256]{5,4,3,2,1,0:T(8,128)}), f32[8,3,2,5,8,256]{5,4,3,2,1,0:T(8,128)S(1)}, u32[]{:S(2)}, u32[]{:S(2)}) async-start(f32[8,3,2,5,8,256]{5,4,3,2,1,0:T(8,128)} %spread.3), calls=%async_computation | async-start | bytes 3932160 | tf_op jit(solution)/shard_map/all_to_all | solution.py:304
  9.8 2.8 %broadcast_select_fusion.1 = (f32[3,2,2,64,256]{4,3,2,1,0:T(8,128)S(1)}, f32[3,2,2,64,256]{4,3,2,1,0:T(8,128)}, f32[3,2,2,64,256]{4,3,2,1,0:T(8,128)}) fusion(pred[]{:T(512)} %eq.23, f32[3,2,8,64,256]{4,3,2,1,0:T(8,128)} %refs_0_.7), kind=kLoop, calls=%fused_computation.6 | loop fusion | flops 196608 | bytes 3932161 | tf_op jit(solution)/shard_map/jit(_where)/select_n | solution.py:273
  12.7 3.2 %collective-permute-start.4 = (f32[3,2,1,64,256]{4,3,2,1,0:T(8,128)S(1)}, f32[3,2,1,64,256]{4,3,2,1,0:T(8,128)}, u32[]{:S(2)}, u32[]{:S(2)}) collective-permute-start(f32[3,2,1,64,256]{4,3,2,1,0:T(8,128)S(1)} %get-tuple-element.38), channel_id=1, source_target_pairs={{56,40},{64,80},{57,41},{65,81},{58,42},{66,82},{59,43},{67,83},{6... | collective-permute-start | bytes 1179656 | tf_op jit(solution)/shard_map/ppermute | solution.py:277
  16.0 2.0 %collective-permute-start.2 = (f32[3,2,1,64,256]{4,3,2,1,0:T(8,128)S(1)}, f32[3,2,1,64,256]{4,3,2,1,0:T(8,128)}, u32[]{:S(2)}, u32[]{:S(2)}) collective-permute-start(f32[3,2,1,64,256]{4,3,2,1,0:T(8,128)S(1)} %get-tuple-element.39), channel_id=1, source_target_pairs={{56,48},{64,72},{57,49},{65,73},{58,50},{66,74},{59,51},{67,75},{6... | collective-permute-start | bytes 1179656 | tf_op jit(solution)/shard_map/ppermute | solution.py:277
  18.0 2.2 %collective-permute-start.1 = (f32[3,2,2,64,256]{4,3,2,1,0:T(8,128)}, f32[3,2,2,64,256]{4,3,2,1,0:T(8,128)}, u32[]{:S(2)}, u32[]{:S(2)}) collective-permute-start(f32[3,2,2,64,256]{4,3,2,1,0:T(8,128)} %get-tuple-element.34), channel_id=1, source_target_pairs={{8,0},{9,1},{10,2},{11,3},{12,4},{13,5},{14,6},{15,7},{16,8},{17,9... | collective-permute-start | bytes 2359304 | tf_op jit(solution)/shard_map/ppermute | solution.py:272
  21.5 1.3 collective-permute-start.5
  22.8 1.3 collective-permute-start.3
  24.2 14.8 %collective-permute-done.5.refs_6_ = f32[3,2,1,64,256]{4,3,2,1,0:T(8,128)S(1)} collective-permute-done((f32[3,2,1,64,256]{4,3,2,1,0:T(8,128)}, f32[3,2,1,64,256]{4,3,2,1,0:T(8,128)S(1)}, u32[]{:S(2)}, u32[]{:S(2)}) %collective-permute-start.5) | collective-permute-done | bytes 393248 | tf_op jit(solution)/shard_map/ppermute | solution.py:277
  39.8 4.9 %spread.2 = f32[8,3,2,5,8,256]{5,4,3,2,1,0:T(8,128)} custom-call(f32[3,2,8,64,256]{4,3,2,1,0:T(8,128)} %refs_0_.7, f32[8,64,256]{2,1,0:T(8,128)S(1)} %copy-done.3, f32[8,64,256]{2,1,0:T(8,128)S(1)} %copy-done.4, f32[3,2,2,64,256]{4,3,2,1,0:T(8,128)} %collective-permute-done.refs_3_, f32[3,2,2,64,256]{4,3,2,1,0:T(8,128)} %collective-permute-done.1.refs_4_, ...), custom_call_target="tpu_custom_call" | custom-call | flops 9830400 | bytes 8519680 | tf_op jit(solution)/shard_map/spread/pallas_call | solution.py:226
  44.7 5.5 %all-to-all-start.1 = ((f32[8,3,2,5,8,256]{5,4,3,2,1,0:T(8,128)}), f32[8,3,2,5,8,256]{5,4,3,2,1,0:T(8,128)}, u32[]{:S(2)}, u32[]{:S(2)}) async-start(f32[8,3,2,5,8,256]{5,4,3,2,1,0:T(8,128)} %spread.2), calls=%async_computation.1 | async-start | bytes 3932160 | tf_op jit(solution)/shard_map/all_to_all | solution.py:304
  53.7 4.0 %first.1 = (f32[3,4,8,16,256]{4,3,2,1,0:T(8,128)}, f32[3,4,2,16,256]{4,3,2,1,0:T(8,128)}, f32[3,4,8,16,256]{4,3,2,1,0:T(8,128)}) custom-call(f32[8,3,2,5,8,256]{5,4,3,2,1,0:T(8,128)S(1)} %all-to-all-done.refs_0_, bf16[3,128,48]{2,1,0:T(8,128)(2,1)S(1)} %copy.14.refs_1_.refs_5_, s32[8,10,256]{2,1,0:T(8,128)S(1)} %pad_dynamic-slice_fusion.refs_2_.refs_6_), custom_call_target="tpu_custom_call" | custom-call | flops 147456000 | bytes 5660672 | tf_op jit(solution)/shard_map/first/pallas_call | solution.py:226
  57.7 16.0 %all-to-all-done.1.refs_0_ = f32[8,3,2,5,8,256]{5,4,3,2,1,0:T(8,128)} async-done(((f32[8,3,2,5,8,256]{5,4,3,2,1,0:T(8,128)}), f32[8,3,2,5,8,256]{5,4,3,2,1,0:T(8,128)}, u32[]{:S(2)}, u32[]{:S(2)}) %all-to-all-start.1) | async-done | bytes 1966112 | tf_op jit(solution)/shard_map/all_to_all | solution.py:304
  73.7 8.0 %middle.1 = (f32[3,4,8,16,256]{4,3,2,1,0:T(8,128)}, f32[3,4,2,16,256]{4,3,2,1,0:T(8,128)}, f32[3,2,8,16,256]{4,3,2,1,0:T(8,128)}, f32[3,2,8,16,256]{4,3,2,1,0:T(8,128)}, f32[8,3,2,4,8,256]{5,4,3,2,1,0:T(8,128)}) custom-call(f32[8,3,2,5,8,256]{5,4,3,2,1,0:T(8,128)} %all-to-all-done.1.refs_0_, bf16[3,128,48]{2,1,0:T(8,128)(2,1)} %copy-done.7, ...), custom_call_target="tpu_custom_call" | custom-call | flops 294912000 | bytes 10903552 | tf_op jit(solution)/shard_map/middle/pallas_call | solution.py:226
  81.7 3.7 %all-to-all-start.2 = ((f32[8,3,2,4,8,256]{5,4,3,2,1,0:T(8,128)}), f32[8,3,2,4,8,256]{5,4,3,2,1,0:T(8,128)S(1)}, u32[]{:S(2)}, u32[]{:S(2)}) async-start(f32[8,3,2,4,8,256]{5,4,3,2,1,0:T(8,128)} %get-tuple-element.30), calls=%async_computation.2 | async-start | bytes 3145728 | tf_op jit(solution)/shard_map/all_to_all | solution.py:304
  85.8 1.3 collective-permute-start.10
  87.1 2.0 %collective-permute-start.8 = (f32[3,1,8,16,256]{4,3,2,1,0:T(8,128)S(1)}, f32[3,1,8,16,256]{4,3,2,1,0:T(8,128)S(1)}, u32[]{:S(2)}, u32[]{:S(2)}) collective-permute-start(f32[3,1,8,16,256]{4,3,2,1,0:T(8,128)S(1)} %get-tuple-element.37), channel_id=1, source_target_pairs={{56,48},{64,72},{57,49},{65,73},{58,50},{66,74},{59,51},{67,75},{6... | collective-permute-start | bytes 1179656 | tf_op jit(solution)/shard_map/ppermute | solution.py:277
  89.1 1.3 collective-permute-start.7
  95.1 14.6 %collective-permute-done.11.refs_12_ = f32[3,1,8,16,256]{4,3,2,1,0:T(8,128)S(1)} collective-permute-done((f32[3,1,8,16,256]{4,3,2,1,0:T(8,128)S(1)}, f32[3,1,8,16,256]{4,3,2,1,0:T(8,128)S(1)}, u32[]{:S(2)}, u32[]{:S(2)}) %collective-permute-start.11) | collective-permute-done | bytes 393248 | tf_op jit(solution)/shard_map/ppermute | solution.py:277
  111.2 7.3 %second.1 = f32[8,3,2,4,8,256]{5,4,3,2,1,0:T(8,128)} custom-call(f32[3,4,8,16,256]{4,3,2,1,0:T(8,128)} %get-tuple-element.22.refs_3_.refs_0_, f32[3,2,8,16,256]{4,3,2,1,0:T(8,128)S(1)} %copy-done.1, f32[3,2,8,16,256]{4,3,2,1,0:T(8,128)S(1)} %copy-done.2, f32[3,4,8,16,256]{4,3,2,1,0:T(8,128)} %get-tuple-element.28.refs_3_, ...), custom_call_target="tpu_custom_call" | custom-call | flops 117964800 | bytes 9330688 | tf_op jit(solution)/shard_map/second/pallas_call | solution.py:226
  118.6 5.5 %all-to-all-start.3 = ((f32[8,3,2,4,8,256]{5,4,3,2,1,0:T(8,128)}), f32[8,3,2,4,8,256]{5,4,3,2,1,0:T(8,128)}, u32[]{:S(2)}, u32[]{:S(2)}) async-start(f32[8,3,2,4,8,256]{5,4,3,2,1,0:T(8,128)} %second.1), calls=%async_computation.3 | async-start | bytes 3145728 | tf_op jit(solution)/shard_map/all_to_all | solution.py:304
  124.0 2.3 %last.2.refs_2_ = f32[3,2,8,64,256]{4,3,2,1,0:T(8,128)} custom-call(f32[3,2,8,64,256]{4,3,2,1,0:T(8,128)} %refs_0_.7, f32[8,3,2,4,8,256]{5,4,3,2,1,0:T(8,128)S(1)} %all-to-all-done.2.refs_1_), custom_call_target="tpu_custom_call" | custom-call | flops 393216 | bytes 7864320 | tf_op jit(solution)/shard_map/last/pallas_call | solution.py:226
  126.3 16.4 %all-to-all-done.3.refs_1_ = f32[8,3,2,4,8,256]{5,4,3,2,1,0:T(8,128)} async-done(((f32[8,3,2,4,8,256]{5,4,3,2,1,0:T(8,128)}), f32[8,3,2,4,8,256]{5,4,3,2,1,0:T(8,128)}, u32[]{:S(2)}, u32[]{:S(2)}) %all-to-all-start.3) | async-done | bytes 1572896 | tf_op jit(solution)/shard_map/all_to_all | solution.py:304
  142.7 2.7 %last.3 = f32[3,2,8,64,256]{4,3,2,1,0:T(8,128)} custom-call(f32[3,2,8,64,256]{4,3,2,1,0:T(8,128)} %refs_0_.7, f32[8,3,2,4,8,256]{5,4,3,2,1,0:T(8,128)} %all-to-all-done.3.refs_1_, f32[3,2,8,64,256]{4,3,2,1,0:T(8,128)} %last.2.refs_2_), custom_call_target="tpu_custom_call", output_to_operand_aliasing={{}: (2, {})} | custom-call | flops 393216 | bytes 7864320 | tf_op jit(solution)/shard_map/last/pallas_call | solution.py:226
  (58 shorter events, 12.0 us)
Async XLA Ops:
  0.0 50.2 %copy-start = (f32[3,8,16]{2,1,0:T(8,128)S(1)}, f32[3,8,16]{2,1,0:T(8,128)}, u32[]{:S(2)}) copy-start(f32[3,8,16]{2,1,0:T(8,128)} %param.10) | copy-start | bytes 4612
  4.2 40.5 %all-to-all-start = ((f32[8,3,2,5,8,256]{5,4,3,2,1,0:T(8,128)}), f32[8,3,2,5,8,256]{5,4,3,2,1,0:T(8,128)S(1)}, u32[]{:S(2)}, u32[]{:S(2)}) async-start(f32[8,3,2,5,8,256]{5,4,3,2,1,0:T(8,128)} %spread.3), calls=%async_computation | async-start | bytes 3932160 | tf_op jit(solution)/shard_map/all_to_all | solution.py:304
  9.8 30.0 %copy-start.3 = (f32[8,64,256]{2,1,0:T(8,128)S(1)}, f32[8,64,256]{2,1,0:T(8,128)}, u32[]{:S(2)}) copy-start(f32[8,64,256]{2,1,0:T(8,128)} %refs_1_.3) | copy-start | bytes 1572868
  9.8 30.0 %copy-start.4 = (f32[8,64,256]{2,1,0:T(8,128)S(1)}, f32[8,64,256]{2,1,0:T(8,128)}, u32[]{:S(2)}) copy-start(f32[8,64,256]{2,1,0:T(8,128)} %refs_2_.3) | copy-start | bytes 1572868
  12.7 8.8 %collective-permute-start.4 = (f32[3,2,1,64,256]{4,3,2,1,0:T(8,128)S(1)}, f32[3,2,1,64,256]{4,3,2,1,0:T(8,128)}, u32[]{:S(2)}, u32[]{:S(2)}) collective-permute-start(f32[3,2,1,64,256]{4,3,2,1,0:T(8,128)S(1)} %get-tuple-element.38), channel_id=1, source_target_pairs={{56,40},{64,80},{57,41},{65,81},{58,42},{66,82},{59,43},{67,83},{6... | collective-permute-start | bytes 1179656 | tf_op jit(solution)/shard_map/ppermute | solution.py:277
  16.0 6.8 %collective-permute-start.2 = (f32[3,2,1,64,256]{4,3,2,1,0:T(8,128)S(1)}, f32[3,2,1,64,256]{4,3,2,1,0:T(8,128)}, u32[]{:S(2)}, u32[]{:S(2)}) collective-permute-start(f32[3,2,1,64,256]{4,3,2,1,0:T(8,128)S(1)} %get-tuple-element.39), channel_id=1, source_target_pairs={{56,48},{64,72},{57,49},{65,73},{58,50},{66,74},{59,51},{67,75},{6... | collective-permute-start | bytes 1179656 | tf_op jit(solution)/shard_map/ppermute | solution.py:277
  18.0 21.7 %collective-permute-start.1 = (f32[3,2,2,64,256]{4,3,2,1,0:T(8,128)}, f32[3,2,2,64,256]{4,3,2,1,0:T(8,128)}, u32[]{:S(2)}, u32[]{:S(2)}) collective-permute-start(f32[3,2,2,64,256]{4,3,2,1,0:T(8,128)} %get-tuple-element.34), channel_id=1, source_target_pairs={{8,0},{9,1},{10,2},{11,3},{12,4},{13,5},{14,6},{15,7},{16,8},{17,9... | collective-permute-start | bytes 2359304 | tf_op jit(solution)/shard_map/ppermute | solution.py:272
  20.2 19.5 %collective-permute-start = (f32[3,2,2,64,256]{4,3,2,1,0:T(8,128)}, f32[3,2,2,64,256]{4,3,2,1,0:T(8,128)}, u32[]{:S(2)}, u32[]{:S(2)}) collective-permute-start(f32[3,2,2,64,256]{4,3,2,1,0:T(8,128)} %get-tuple-element.35), channel_id=1, source_target_pairs={{0,8},{1,9},{2,10},{3,11},{4,12},{5,13},{6,14},{7,15},{8,16},{9,17... | collective-permute-start | bytes 2359304 | tf_op jit(solution)/shard_map/ppermute | solution.py:271
  21.5 17.5 %collective-permute-start.5 = (f32[3,2,1,64,256]{4,3,2,1,0:T(8,128)}, f32[3,2,1,64,256]{4,3,2,1,0:T(8,128)S(1)}, u32[]{:S(2)}, u32[]{:S(2)}) collective-permute-start(f32[3,2,1,64,256]{4,3,2,1,0:T(8,128)} %collective-permute-done.4), channel_id=1, source_target_pairs={{40,64},{80,56},{41,65},{81,57},{42,66},{82,58},{43,67},{83,59},{2... | collective-permute-start | bytes 1179656 | tf_op jit(solution)/shard_map/ppermute | solution.py:277
  22.8 16.9 %collective-permute-start.3 = (f32[3,2,1,64,256]{4,3,2,1,0:T(8,128)}, f32[3,2,1,64,256]{4,3,2,1,0:T(8,128)}, u32[]{:S(2)}, u32[]{:S(2)}) collective-permute-start(f32[3,2,1,64,256]{4,3,2,1,0:T(8,128)} %collective-permute-done.2), channel_id=1, source_target_pairs={{48,64},{72,56},{49,65},{73,57},{50,66},{74,58},{51,67},{75,59},{1... | collective-permute-start | bytes 1179656 | tf_op jit(solution)/shard_map/ppermute | solution.py:277
  44.7 29.0 %all-to-all-start.1 = ((f32[8,3,2,5,8,256]{5,4,3,2,1,0:T(8,128)}), f32[8,3,2,5,8,256]{5,4,3,2,1,0:T(8,128)}, u32[]{:S(2)}, u32[]{:S(2)}) async-start(f32[8,3,2,5,8,256]{5,4,3,2,1,0:T(8,128)} %spread.2), calls=%async_computation.1 | async-start | bytes 3932160 | tf_op jit(solution)/shard_map/all_to_all | solution.py:304
  81.7 36.8 %all-to-all-start.2 = ((f32[8,3,2,4,8,256]{5,4,3,2,1,0:T(8,128)}), f32[8,3,2,4,8,256]{5,4,3,2,1,0:T(8,128)S(1)}, u32[]{:S(2)}, u32[]{:S(2)}) async-start(f32[8,3,2,4,8,256]{5,4,3,2,1,0:T(8,128)} %get-tuple-element.30), calls=%async_computation.2 | async-start | bytes 3145728 | tf_op jit(solution)/shard_map/all_to_all | solution.py:304
  85.5 25.7 %copy-start.6 = (s32[8,10,256]{2,1,0:T(8,128)S(1)}, s32[8,10,256]{2,1,0:T(8,128)}, u32[]{:S(2)}) copy-start(s32[8,10,256]{2,1,0:T(8,128)} %copy-done.5) | copy-start | bytes 245764
  85.5 25.7 %copy-start.8 = (bf16[3,128,48]{2,1,0:T(8,128)(2,1)S(1)}, bf16[3,128,48]{2,1,0:T(8,128)(2,1)}, u32[]{:S(2)}) copy-start(bf16[3,128,48]{2,1,0:T(8,128)(2,1)} %copy-done.7) | copy-start | bytes 110596
  85.5 25.7 %copy-start.9 = (f32[8,8,256]{2,1,0:T(8,128)S(1)}, f32[8,8,256]{2,1,0:T(8,128)}, u32[]{:S(2)}) copy-start(f32[8,8,256]{2,1,0:T(8,128)} %get-tuple-element.42.refs_6_.refs_7_) | copy-start | bytes 196612
  85.5 25.7 %copy-start.10 = (f32[8,8,256]{2,1,0:T(8,128)S(1)}, f32[8,8,256]{2,1,0:T(8,128)}, u32[]{:S(2)}) copy-start(f32[8,8,256]{2,1,0:T(8,128)} %get-tuple-element.43.refs_7_.refs_8_) | copy-start | bytes 196612
  85.5 25.7 %copy-start.11 = (f32[3,4,2,16,256]{4,3,2,1,0:T(8,128)S(1)}, f32[3,4,2,16,256]{4,3,2,1,0:T(8,128)}, u32[]{:S(2)}) copy-start(f32[3,4,2,16,256]{4,3,2,1,0:T(8,128)} %get-tuple-element.29.refs_4_) | copy-start | bytes 1179652
  85.8 6.7 %collective-permute-start.10 = (f32[3,1,8,16,256]{4,3,2,1,0:T(8,128)S(1)}, f32[3,1,8,16,256]{4,3,2,1,0:T(8,128)S(1)}, u32[]{:S(2)}, u32[]{:S(2)}) collective-permute-start(f32[3,1,8,16,256]{4,3,2,1,0:T(8,128)S(1)} %get-tuple-element.36), channel_id=1, source_target_pairs={{56,40},{64,80},{57,41},{65,81},{58,42},{66,82},{59,43},{67,83},{6... | collective-permute-start | bytes 1179656 | tf_op jit(solution)/shard_map/ppermute | solution.py:277
  87.1 6.7 %collective-permute-start.8 = (f32[3,1,8,16,256]{4,3,2,1,0:T(8,128)S(1)}, f32[3,1,8,16,256]{4,3,2,1,0:T(8,128)S(1)}, u32[]{:S(2)}, u32[]{:S(2)}) collective-permute-start(f32[3,1,8,16,256]{4,3,2,1,0:T(8,128)S(1)} %get-tuple-element.37), channel_id=1, source_target_pairs={{56,48},{64,72},{57,49},{65,73},{58,50},{66,74},{59,51},{67,75},{6... | collective-permute-start | bytes 1179656 | tf_op jit(solution)/shard_map/ppermute | solution.py:277
  89.1 21.2 %collective-permute-start.7 = (f32[3,2,8,16,256]{4,3,2,1,0:T(8,128)S(1)}, f32[3,2,8,16,256]{4,3,2,1,0:T(8,128)S(1)}, u32[]{:S(2)}, u32[]{:S(2)}) collective-permute-start(f32[3,2,8,16,256]{4,3,2,1,0:T(8,128)S(1)} %copy-done.1), channel_id=1, source_target_pairs={{8,0},{9,1},{10,2},{11,3},{12,4},{13,5},{14,6},{15,7},{16,8},{17,9... | collective-permute-start | bytes 2359304 | tf_op jit(solution)/shard_map/ppermute | solution.py:272
  90.4 19.9 %collective-permute-start.6 = (f32[3,2,8,16,256]{4,3,2,1,0:T(8,128)S(1)}, f32[3,2,8,16,256]{4,3,2,1,0:T(8,128)S(1)}, u32[]{:S(2)}, u32[]{:S(2)}) collective-permute-start(f32[3,2,8,16,256]{4,3,2,1,0:T(8,128)S(1)} %copy-done.2), channel_id=1, source_target_pairs={{0,8},{1,9},{2,10},{3,11},{4,12},{5,13},{6,14},{7,15},{8,16},{9,17... | collective-permute-start | bytes 2359304 | tf_op jit(solution)/shard_map/ppermute | solution.py:271
  92.5 17.2 %collective-permute-start.11 = (f32[3,1,8,16,256]{4,3,2,1,0:T(8,128)S(1)}, f32[3,1,8,16,256]{4,3,2,1,0:T(8,128)S(1)}, u32[]{:S(2)}, u32[]{:S(2)}) collective-permute-start(f32[3,1,8,16,256]{4,3,2,1,0:T(8,128)S(1)} %collective-permute-done.10), channel_id=1, source_target_pairs={{40,64},{80,56},{41,65},{81,57},{42,66},{82,58},{43,67},{83,59},{2... | collective-permute-start | bytes 1179656 | tf_op jit(solution)/shard_map/ppermute | solution.py:277
  93.8 16.5 %collective-permute-start.9 = (f32[3,1,8,16,256]{4,3,2,1,0:T(8,128)S(1)}, f32[3,1,8,16,256]{4,3,2,1,0:T(8,128)S(1)}, u32[]{:S(2)}, u32[]{:S(2)}) collective-permute-start(f32[3,1,8,16,256]{4,3,2,1,0:T(8,128)S(1)} %collective-permute-done.8), channel_id=1, source_target_pairs={{48,64},{72,56},{49,65},{73,57},{50,66},{74,58},{51,67},{75,59},{1... | collective-permute-start | bytes 1179656 | tf_op jit(solution)/shard_map/ppermute | solution.py:277
  118.6 24.2 %all-to-all-start.3 = ((f32[8,3,2,4,8,256]{5,4,3,2,1,0:T(8,128)}), f32[8,3,2,4,8,256]{5,4,3,2,1,0:T(8,128)}, u32[]{:S(2)}, u32[]{:S(2)}) async-start(f32[8,3,2,4,8,256]{5,4,3,2,1,0:T(8,128)} %second.1), calls=%async_computation.3 | async-start | bytes 3145728 | tf_op jit(solution)/shard_map/all_to_all | solution.py:304
  (6 other events, 40.0 us)

commit v6 on v5

--- a/solution.py
+++ b/solution.py
@@ -13,7 +13,7 @@
 TIME_STEP = 0.1
 MOBILE_BASE = 0.7
 RUN = 8
-RELAYS = (((6, 1), (1, 6)), ((5, 2), (2, 5)))
+RELAYS = (((6, 1), (1, 6)), ((2, 5), (5, 2)))
 SHARED_LIMIT = 50 * 1024 * 1024
 VMEM_LIMIT = 61 * 1024 * 1024
 

time: 146 us -> 146 us (level)
  waiting for transfers between devices: 64 us -> 56.3 us
  starting transfers between devices: 40 us -> 47.2 us
    ppermute x8, waiting for transfers between devices: 31.5 us -> 24.7 us  [exchange(): around.append(lax.ppermute(lax.ppermute(piece, both, leave), both, arrive))]
    all_to_all x4, starting transfers between devices: 20.2 us -> 26 us  [over_modes(): lax.all_to_all(array, 'mode', split_axis=0, concat_axis=0, tiled=True)]
  transfers between devices with their start and end apart: 16 -> 16, of which waited for: 7 -> 8; matrix products, arithmetic and copies ran while one was open for 5% -> 5% of each run, Pallas kernels for 13% -> 13%
where the time goes in v6:
time: 146 us; the launch traced here: 145 us
  waiting for transfers between devices  56.3 us (39%)
  starting transfers between devices  47.2 us (32%)
  Pallas kernels  33.5 us (23%)
  other arithmetic  4.37 us (3%)
  local copies, waits for them, and re-layouts  2.16 us (1%)
    pallas_call x7, Pallas kernels, staged(): pl.pallas_call(kernel, in_specs=[pl.BlockSpec(memory_space=pl.ANY) if k i...  33.5 us
    all_to_all x4, waiting for transfers between devices, over_modes(): lax.all_to_all(array, 'mode', split_axis=0, concat_axis=0, tiled=True)  31.6 us
    all_to_all x4, starting transfers between devices, over_modes(): lax.all_to_all(array, 'mode', split_axis=0, concat_axis=0, tiled=True)  26 us
    ppermute x8, waiting for transfers between devices, exchange(): around.append(lax.ppermute(lax.ppermute(piece, both, leave), both, arrive))  24.7 us
    ppermute x8, starting transfers between devices, exchange(): around.append(lax.ppermute(lax.ppermute(piece, both, leave), both, arrive))  15.1 us
    ppermute x2, starting transfers between devices, exchange(): hi = lax.ppermute(low, both, back)  3.55 us
    select_n x2, other arithmetic, exchange(): out = jnp.where(place == RUN - 1, high, low)  3 us
  transfers between devices with their start and end apart: 16, of which 8 were waited for; matrix products, arithmetic and copies ran while one was open for 5% of the time, Pallas kernels for 13%

profile of v6, /device:TPU:71, one launch (start us, length us, event | category | flops | bytes accessed | tf_op | source)
XLA Modules:
  0.0 144.9 jit_solution(4521902707919852303)
XLA Ops:
  0.0 4.2 %spread.3 = f32[8,3,2,5,8,256]{5,4,3,2,1,0:T(8,128)} custom-call(f32[3,2,8,64,256]{4,3,2,1,0:T(8,128)} %refs_0_.7, f32[8,64,256]{2,1,0:T(8,128)} %refs_1_.3, f32[8,64,256]{2,1,0:T(8,128)} %refs_2_.3), custom_call_target="tpu_custom_call" | custom-call | flops 9830400 | bytes 6160384 | tf_op jit(solution)/shard_map/spread/pallas_call | solution.py:226
  4.2 5.6 %all-to-all-start = ((f32[8,3,2,5,8,256]{5,4,3,2,1,0:T(8,128)}), f32[8,3,2,5,8,256]{5,4,3,2,1,0:T(8,128)S(1)}, u32[]{:S(2)}, u32[]{:S(2)}) async-start(f32[8,3,2,5,8,256]{5,4,3,2,1,0:T(8,128)} %spread.3), calls=%async_computation | async-start | bytes 3932160 | tf_op jit(solution)/shard_map/all_to_all | solution.py:304
  9.8 2.8 %broadcast_select_fusion.1 = (f32[3,2,2,64,256]{4,3,2,1,0:T(8,128)S(1)}, f32[3,2,2,64,256]{4,3,2,1,0:T(8,128)}, f32[3,2,2,64,256]{4,3,2,1,0:T(8,128)}) fusion(pred[]{:T(512)} %eq.23, f32[3,2,8,64,256]{4,3,2,1,0:T(8,128)} %refs_0_.7), kind=kLoop, calls=%fused_computation.6 | loop fusion | flops 196608 | bytes 3932161 | tf_op jit(solution)/shard_map/jit(_where)/select_n | solution.py:273
  12.7 4.6 %collective-permute-start.4 = (f32[3,2,1,64,256]{4,3,2,1,0:T(8,128)S(1)}, f32[3,2,1,64,256]{4,3,2,1,0:T(8,128)}, u32[]{:S(2)}, u32[]{:S(2)}) collective-permute-start(f32[3,2,1,64,256]{4,3,2,1,0:T(8,128)S(1)} %get-tuple-element.38), channel_id=1, source_target_pairs={{56,16},{64,104},{57,17},{65,105},{58,18},{66,106},{59,19},{67,107... | collective-permute-start | bytes 1179656 | tf_op jit(solution)/shard_map/ppermute | solution.py:277
  17.4 2.0 %collective-permute-start.2 = (f32[3,2,1,64,256]{4,3,2,1,0:T(8,128)S(1)}, f32[3,2,1,64,256]{4,3,2,1,0:T(8,128)}, u32[]{:S(2)}, u32[]{:S(2)}) collective-permute-start(f32[3,2,1,64,256]{4,3,2,1,0:T(8,128)S(1)} %get-tuple-element.39), channel_id=1, source_target_pairs={{56,48},{64,72},{57,49},{65,73},{58,50},{66,74},{59,51},{67,75},{6... | collective-permute-start | bytes 1179656 | tf_op jit(solution)/shard_map/ppermute | solution.py:277
  19.4 2.2 %collective-permute-start.1 = (f32[3,2,2,64,256]{4,3,2,1,0:T(8,128)}, f32[3,2,2,64,256]{4,3,2,1,0:T(8,128)}, u32[]{:S(2)}, u32[]{:S(2)}) collective-permute-start(f32[3,2,2,64,256]{4,3,2,1,0:T(8,128)} %get-tuple-element.34), channel_id=1, source_target_pairs={{8,0},{9,1},{10,2},{11,3},{12,4},{13,5},{14,6},{15,7},{16,8},{17,9... | collective-permute-start | bytes 2359304 | tf_op jit(solution)/shard_map/ppermute | solution.py:272
  26.0 9.2 %collective-permute-done.5.refs_6_ = f32[3,2,1,64,256]{4,3,2,1,0:T(8,128)S(1)} collective-permute-done((f32[3,2,1,64,256]{4,3,2,1,0:T(8,128)}, f32[3,2,1,64,256]{4,3,2,1,0:T(8,128)S(1)}, u32[]{:S(2)}, u32[]{:S(2)}) %collective-permute-start.5) | collective-permute-done | bytes 393248 | tf_op jit(solution)/shard_map/ppermute | solution.py:277
  35.2 2.6 %collective-permute-done.3.refs_5_ = f32[3,2,1,64,256]{4,3,2,1,0:T(8,128)} collective-permute-done((f32[3,2,1,64,256]{4,3,2,1,0:T(8,128)}, f32[3,2,1,64,256]{4,3,2,1,0:T(8,128)}, u32[]{:S(2)}, u32[]{:S(2)}) %collective-permute-start.3) | collective-permute-done | bytes 393248 | tf_op jit(solution)/shard_map/ppermute | solution.py:277
  37.8 4.9 %spread.2 = f32[8,3,2,5,8,256]{5,4,3,2,1,0:T(8,128)} custom-call(f32[3,2,8,64,256]{4,3,2,1,0:T(8,128)} %refs_0_.7, f32[8,64,256]{2,1,0:T(8,128)S(1)} %copy-done.3, f32[8,64,256]{2,1,0:T(8,128)S(1)} %copy-done.4, f32[3,2,2,64,256]{4,3,2,1,0:T(8,128)} %collective-permute-done.refs_3_, f32[3,2,2,64,256]{4,3,2,1,0:T(8,128)} %collective-permute-done.1.refs_4_, ...), custom_call_target="tpu_custom_call" | custom-call | flops 9830400 | bytes 8519680 | tf_op jit(solution)/shard_map/spread/pallas_call | solution.py:226
  42.8 8.0 %all-to-all-start.1 = ((f32[8,3,2,5,8,256]{5,4,3,2,1,0:T(8,128)}), f32[8,3,2,5,8,256]{5,4,3,2,1,0:T(8,128)}, u32[]{:S(2)}, u32[]{:S(2)}) async-start(f32[8,3,2,5,8,256]{5,4,3,2,1,0:T(8,128)} %spread.2), calls=%async_computation.1 | async-start | bytes 3932160 | tf_op jit(solution)/shard_map/all_to_all | solution.py:304
  54.3 4.0 %first.1 = (f32[3,4,8,16,256]{4,3,2,1,0:T(8,128)}, f32[3,4,2,16,256]{4,3,2,1,0:T(8,128)}, f32[3,4,8,16,256]{4,3,2,1,0:T(8,128)}) custom-call(f32[8,3,2,5,8,256]{5,4,3,2,1,0:T(8,128)S(1)} %all-to-all-done.refs_0_, bf16[3,128,48]{2,1,0:T(8,128)(2,1)S(1)} %copy.14.refs_1_.refs_5_, s32[8,10,256]{2,1,0:T(8,128)S(1)} %pad_dynamic-slice_fusion.refs_2_.refs_6_), custom_call_target="tpu_custom_call" | custom-call | flops 147456000 | bytes 5660672 | tf_op jit(solution)/shard_map/first/pallas_call | solution.py:226
  58.3 14.9 %all-to-all-done.1.refs_0_ = f32[8,3,2,5,8,256]{5,4,3,2,1,0:T(8,128)} async-done(((f32[8,3,2,5,8,256]{5,4,3,2,1,0:T(8,128)}), f32[8,3,2,5,8,256]{5,4,3,2,1,0:T(8,128)}, u32[]{:S(2)}, u32[]{:S(2)}) %all-to-all-start.1) | async-done | bytes 1966112 | tf_op jit(solution)/shard_map/all_to_all | solution.py:304
  73.2 8.0 %middle.1 = (f32[3,4,8,16,256]{4,3,2,1,0:T(8,128)}, f32[3,4,2,16,256]{4,3,2,1,0:T(8,128)}, f32[3,2,8,16,256]{4,3,2,1,0:T(8,128)}, f32[3,2,8,16,256]{4,3,2,1,0:T(8,128)}, f32[8,3,2,4,8,256]{5,4,3,2,1,0:T(8,128)}) custom-call(f32[8,3,2,5,8,256]{5,4,3,2,1,0:T(8,128)} %all-to-all-done.1.refs_0_, bf16[3,128,48]{2,1,0:T(8,128)(2,1)} %copy-done.7, ...), custom_call_target="tpu_custom_call" | custom-call | flops 294912000 | bytes 10903552 | tf_op jit(solution)/shard_map/middle/pallas_call | solution.py:226
  81.3 3.7 %all-to-all-start.2 = ((f32[8,3,2,4,8,256]{5,4,3,2,1,0:T(8,128)}), f32[8,3,2,4,8,256]{5,4,3,2,1,0:T(8,128)S(1)}, u32[]{:S(2)}, u32[]{:S(2)}) async-start(f32[8,3,2,4,8,256]{5,4,3,2,1,0:T(8,128)} %get-tuple-element.30), calls=%async_computation.2 | async-start | bytes 3145728 | tf_op jit(solution)/shard_map/all_to_all | solution.py:304
  85.3 1.3 collective-permute-start.10
  86.6 1.9 %collective-permute-start.8 = (f32[3,1,8,16,256]{4,3,2,1,0:T(8,128)S(1)}, f32[3,1,8,16,256]{4,3,2,1,0:T(8,128)S(1)}, u32[]{:S(2)}, u32[]{:S(2)}) collective-permute-start(f32[3,1,8,16,256]{4,3,2,1,0:T(8,128)S(1)} %get-tuple-element.37), channel_id=1, source_target_pairs={{56,48},{64,72},{57,49},{65,73},{58,50},{66,74},{59,51},{67,75},{6... | collective-permute-start | bytes 1179656 | tf_op jit(solution)/shard_map/ppermute | solution.py:277
  88.6 1.3 collective-permute-start.7
  94.7 9.1 %collective-permute-done.11.refs_12_ = f32[3,1,8,16,256]{4,3,2,1,0:T(8,128)S(1)} collective-permute-done((f32[3,1,8,16,256]{4,3,2,1,0:T(8,128)S(1)}, f32[3,1,8,16,256]{4,3,2,1,0:T(8,128)S(1)}, u32[]{:S(2)}, u32[]{:S(2)}) %collective-permute-start.11) | collective-permute-done | bytes 393248 | tf_op jit(solution)/shard_map/ppermute | solution.py:277
  103.8 2.5 %collective-permute-done.9.refs_11_ = f32[3,1,8,16,256]{4,3,2,1,0:T(8,128)S(1)} collective-permute-done((f32[3,1,8,16,256]{4,3,2,1,0:T(8,128)S(1)}, f32[3,1,8,16,256]{4,3,2,1,0:T(8,128)S(1)}, u32[]{:S(2)}, u32[]{:S(2)}) %collective-permute-start.9) | collective-permute-done | bytes 393248 | tf_op jit(solution)/shard_map/ppermute | solution.py:277
  107.2 7.3 %second.1 = f32[8,3,2,4,8,256]{5,4,3,2,1,0:T(8,128)} custom-call(f32[3,4,8,16,256]{4,3,2,1,0:T(8,128)} %get-tuple-element.22.refs_3_.refs_0_, f32[3,2,8,16,256]{4,3,2,1,0:T(8,128)S(1)} %copy-done.1, f32[3,2,8,16,256]{4,3,2,1,0:T(8,128)S(1)} %copy-done.2, f32[3,4,8,16,256]{4,3,2,1,0:T(8,128)} %get-tuple-element.28.refs_3_, ...), custom_call_target="tpu_custom_call" | custom-call | flops 117964800 | bytes 9330688 | tf_op jit(solution)/shard_map/second/pallas_call | solution.py:226
  114.5 8.8 %all-to-all-start.3 = ((f32[8,3,2,4,8,256]{5,4,3,2,1,0:T(8,128)}), f32[8,3,2,4,8,256]{5,4,3,2,1,0:T(8,128)}, u32[]{:S(2)}, u32[]{:S(2)}) async-start(f32[8,3,2,4,8,256]{5,4,3,2,1,0:T(8,128)} %second.1), calls=%async_computation.3 | async-start | bytes 3145728 | tf_op jit(solution)/shard_map/all_to_all | solution.py:304
  123.3 2.3 %last.2.refs_2_ = f32[3,2,8,64,256]{4,3,2,1,0:T(8,128)} custom-call(f32[3,2,8,64,256]{4,3,2,1,0:T(8,128)} %refs_0_.7, f32[8,3,2,4,8,256]{5,4,3,2,1,0:T(8,128)S(1)} %all-to-all-done.2.refs_1_), custom_call_target="tpu_custom_call" | custom-call | flops 393216 | bytes 7864320 | tf_op jit(solution)/shard_map/last/pallas_call | solution.py:226
  125.5 16.7 %all-to-all-done.3.refs_1_ = f32[8,3,2,4,8,256]{5,4,3,2,1,0:T(8,128)} async-done(((f32[8,3,2,4,8,256]{5,4,3,2,1,0:T(8,128)}), f32[8,3,2,4,8,256]{5,4,3,2,1,0:T(8,128)}, u32[]{:S(2)}, u32[]{:S(2)}) %all-to-all-start.3) | async-done | bytes 1572896 | tf_op jit(solution)/shard_map/all_to_all | solution.py:304
  142.2 2.7 %last.3 = f32[3,2,8,64,256]{4,3,2,1,0:T(8,128)} custom-call(f32[3,2,8,64,256]{4,3,2,1,0:T(8,128)} %refs_0_.7, f32[8,3,2,4,8,256]{5,4,3,2,1,0:T(8,128)} %all-to-all-done.3.refs_1_, f32[3,2,8,64,256]{4,3,2,1,0:T(8,128)} %last.2.refs_2_), custom_call_target="tpu_custom_call", output_to_operand_aliasing={{}: (2, {})} | custom-call | flops 393216 | bytes 7864320 | tf_op jit(solution)/shard_map/last/pallas_call | solution.py:226
  (58 shorter events, 13.8 us)
Async XLA Ops:
  0.0 50.8 %copy-start = (f32[3,8,16]{2,1,0:T(8,128)S(1)}, f32[3,8,16]{2,1,0:T(8,128)}, u32[]{:S(2)}) copy-start(f32[3,8,16]{2,1,0:T(8,128)} %param.10) | copy-start | bytes 4612
  4.2 38.5 %all-to-all-start = ((f32[8,3,2,5,8,256]{5,4,3,2,1,0:T(8,128)}), f32[8,3,2,5,8,256]{5,4,3,2,1,0:T(8,128)S(1)}, u32[]{:S(2)}, u32[]{:S(2)}) async-start(f32[8,3,2,5,8,256]{5,4,3,2,1,0:T(8,128)} %spread.3), calls=%async_computation | async-start | bytes 3932160 | tf_op jit(solution)/shard_map/all_to_all | solution.py:304
  9.8 28.0 %copy-start.3 = (f32[8,64,256]{2,1,0:T(8,128)S(1)}, f32[8,64,256]{2,1,0:T(8,128)}, u32[]{:S(2)}) copy-start(f32[8,64,256]{2,1,0:T(8,128)} %refs_1_.3) | copy-start | bytes 1572868
  9.8 28.0 %copy-start.4 = (f32[8,64,256]{2,1,0:T(8,128)S(1)}, f32[8,64,256]{2,1,0:T(8,128)}, u32[]{:S(2)}) copy-start(f32[8,64,256]{2,1,0:T(8,128)} %refs_2_.3) | copy-start | bytes 1572868
  12.7 10.6 %collective-permute-start.4 = (f32[3,2,1,64,256]{4,3,2,1,0:T(8,128)S(1)}, f32[3,2,1,64,256]{4,3,2,1,0:T(8,128)}, u32[]{:S(2)}, u32[]{:S(2)}) collective-permute-start(f32[3,2,1,64,256]{4,3,2,1,0:T(8,128)S(1)} %get-tuple-element.38), channel_id=1, source_target_pairs={{56,16},{64,104},{57,17},{65,105},{58,18},{66,106},{59,19},{67,107... | collective-permute-start | bytes 1179656 | tf_op jit(solution)/shard_map/ppermute | solution.py:277
  17.4 7.2 %collective-permute-start.2 = (f32[3,2,1,64,256]{4,3,2,1,0:T(8,128)S(1)}, f32[3,2,1,64,256]{4,3,2,1,0:T(8,128)}, u32[]{:S(2)}, u32[]{:S(2)}) collective-permute-start(f32[3,2,1,64,256]{4,3,2,1,0:T(8,128)S(1)} %get-tuple-element.39), channel_id=1, source_target_pairs={{56,48},{64,72},{57,49},{65,73},{58,50},{66,74},{59,51},{67,75},{6... | collective-permute-start | bytes 1179656 | tf_op jit(solution)/shard_map/ppermute | solution.py:277
  19.4 18.4 %collective-permute-start.1 = (f32[3,2,2,64,256]{4,3,2,1,0:T(8,128)}, f32[3,2,2,64,256]{4,3,2,1,0:T(8,128)}, u32[]{:S(2)}, u32[]{:S(2)}) collective-permute-start(f32[3,2,2,64,256]{4,3,2,1,0:T(8,128)} %get-tuple-element.34), channel_id=1, source_target_pairs={{8,0},{9,1},{10,2},{11,3},{12,4},{13,5},{14,6},{15,7},{16,8},{17,9... | collective-permute-start | bytes 2359304 | tf_op jit(solution)/shard_map/ppermute | solution.py:272
  21.6 16.2 %collective-permute-start = (f32[3,2,2,64,256]{4,3,2,1,0:T(8,128)}, f32[3,2,2,64,256]{4,3,2,1,0:T(8,128)}, u32[]{:S(2)}, u32[]{:S(2)}) collective-permute-start(f32[3,2,2,64,256]{4,3,2,1,0:T(8,128)} %get-tuple-element.35), channel_id=1, source_target_pairs={{0,8},{1,9},{2,10},{3,11},{4,12},{5,13},{6,14},{7,15},{8,16},{9,17... | collective-permute-start | bytes 2359304 | tf_op jit(solution)/shard_map/ppermute | solution.py:271
  23.3 11.9 %collective-permute-start.5 = (f32[3,2,1,64,256]{4,3,2,1,0:T(8,128)}, f32[3,2,1,64,256]{4,3,2,1,0:T(8,128)S(1)}, u32[]{:S(2)}, u32[]{:S(2)}) collective-permute-start(f32[3,2,1,64,256]{4,3,2,1,0:T(8,128)} %collective-permute-done.4), channel_id=1, source_target_pairs={{16,64},{104,56},{17,65},{105,57},{18,66},{106,58},{19,67},{107,59... | collective-permute-start | bytes 1179656 | tf_op jit(solution)/shard_map/ppermute | solution.py:277
  24.6 13.2 %collective-permute-start.3 = (f32[3,2,1,64,256]{4,3,2,1,0:T(8,128)}, f32[3,2,1,64,256]{4,3,2,1,0:T(8,128)}, u32[]{:S(2)}, u32[]{:S(2)}) collective-permute-start(f32[3,2,1,64,256]{4,3,2,1,0:T(8,128)} %collective-permute-done.2), channel_id=1, source_target_pairs={{48,64},{72,56},{49,65},{73,57},{50,66},{74,58},{51,67},{75,59},{1... | collective-permute-start | bytes 1179656 | tf_op jit(solution)/shard_map/ppermute | solution.py:277
  42.8 30.4 %all-to-all-start.1 = ((f32[8,3,2,5,8,256]{5,4,3,2,1,0:T(8,128)}), f32[8,3,2,5,8,256]{5,4,3,2,1,0:T(8,128)}, u32[]{:S(2)}, u32[]{:S(2)}) async-start(f32[8,3,2,5,8,256]{5,4,3,2,1,0:T(8,128)} %spread.2), calls=%async_computation.1 | async-start | bytes 3932160 | tf_op jit(solution)/shard_map/all_to_all | solution.py:304
  81.3 33.2 %all-to-all-start.2 = ((f32[8,3,2,4,8,256]{5,4,3,2,1,0:T(8,128)}), f32[8,3,2,4,8,256]{5,4,3,2,1,0:T(8,128)S(1)}, u32[]{:S(2)}, u32[]{:S(2)}) async-start(f32[8,3,2,4,8,256]{5,4,3,2,1,0:T(8,128)} %get-tuple-element.30), calls=%async_computation.2 | async-start | bytes 3145728 | tf_op jit(solution)/shard_map/all_to_all | solution.py:304
  85.0 22.1 %copy-start.6 = (s32[8,10,256]{2,1,0:T(8,128)S(1)}, s32[8,10,256]{2,1,0:T(8,128)}, u32[]{:S(2)}) copy-start(s32[8,10,256]{2,1,0:T(8,128)} %copy-done.5) | copy-start | bytes 245764
  85.0 22.1 %copy-start.8 = (bf16[3,128,48]{2,1,0:T(8,128)(2,1)S(1)}, bf16[3,128,48]{2,1,0:T(8,128)(2,1)}, u32[]{:S(2)}) copy-start(bf16[3,128,48]{2,1,0:T(8,128)(2,1)} %copy-done.7) | copy-start | bytes 110596
  85.0 22.1 %copy-start.9 = (f32[8,8,256]{2,1,0:T(8,128)S(1)}, f32[8,8,256]{2,1,0:T(8,128)}, u32[]{:S(2)}) copy-start(f32[8,8,256]{2,1,0:T(8,128)} %get-tuple-element.42.refs_6_.refs_7_) | copy-start | bytes 196612
  85.0 22.1 %copy-start.10 = (f32[8,8,256]{2,1,0:T(8,128)S(1)}, f32[8,8,256]{2,1,0:T(8,128)}, u32[]{:S(2)}) copy-start(f32[8,8,256]{2,1,0:T(8,128)} %get-tuple-element.43.refs_7_.refs_8_) | copy-start | bytes 196612
  85.0 22.1 %copy-start.11 = (f32[3,4,2,16,256]{4,3,2,1,0:T(8,128)S(1)}, f32[3,4,2,16,256]{4,3,2,1,0:T(8,128)}, u32[]{:S(2)}) copy-start(f32[3,4,2,16,256]{4,3,2,1,0:T(8,128)} %get-tuple-element.29.refs_4_) | copy-start | bytes 1179652
  85.3 6.8 %collective-permute-start.10 = (f32[3,1,8,16,256]{4,3,2,1,0:T(8,128)S(1)}, f32[3,1,8,16,256]{4,3,2,1,0:T(8,128)S(1)}, u32[]{:S(2)}, u32[]{:S(2)}) collective-permute-start(f32[3,1,8,16,256]{4,3,2,1,0:T(8,128)S(1)} %get-tuple-element.36), channel_id=1, source_target_pairs={{56,16},{64,104},{57,17},{65,105},{58,18},{66,106},{59,19},{67,107... | collective-permute-start | bytes 1179656 | tf_op jit(solution)/shard_map/ppermute | solution.py:277
  86.6 6.8 %collective-permute-start.8 = (f32[3,1,8,16,256]{4,3,2,1,0:T(8,128)S(1)}, f32[3,1,8,16,256]{4,3,2,1,0:T(8,128)S(1)}, u32[]{:S(2)}, u32[]{:S(2)}) collective-permute-start(f32[3,1,8,16,256]{4,3,2,1,0:T(8,128)S(1)} %get-tuple-element.37), channel_id=1, source_target_pairs={{56,48},{64,72},{57,49},{65,73},{58,50},{66,74},{59,51},{67,75},{6... | collective-permute-start | bytes 1179656 | tf_op jit(solution)/shard_map/ppermute | solution.py:277
  88.6 17.7 %collective-permute-start.7 = (f32[3,2,8,16,256]{4,3,2,1,0:T(8,128)S(1)}, f32[3,2,8,16,256]{4,3,2,1,0:T(8,128)S(1)}, u32[]{:S(2)}, u32[]{:S(2)}) collective-permute-start(f32[3,2,8,16,256]{4,3,2,1,0:T(8,128)S(1)} %copy-done.1), channel_id=1, source_target_pairs={{8,0},{9,1},{10,2},{11,3},{12,4},{13,5},{14,6},{15,7},{16,8},{17,9... | collective-permute-start | bytes 2359304 | tf_op jit(solution)/shard_map/ppermute | solution.py:272
  89.9 16.4 %collective-permute-start.6 = (f32[3,2,8,16,256]{4,3,2,1,0:T(8,128)S(1)}, f32[3,2,8,16,256]{4,3,2,1,0:T(8,128)S(1)}, u32[]{:S(2)}, u32[]{:S(2)}) collective-permute-start(f32[3,2,8,16,256]{4,3,2,1,0:T(8,128)S(1)} %copy-done.2), channel_id=1, source_target_pairs={{0,8},{1,9},{2,10},{3,11},{4,12},{5,13},{6,14},{7,15},{8,16},{9,17... | collective-permute-start | bytes 2359304 | tf_op jit(solution)/shard_map/ppermute | solution.py:271
  92.1 11.7 %collective-permute-start.11 = (f32[3,1,8,16,256]{4,3,2,1,0:T(8,128)S(1)}, f32[3,1,8,16,256]{4,3,2,1,0:T(8,128)S(1)}, u32[]{:S(2)}, u32[]{:S(2)}) collective-permute-start(f32[3,1,8,16,256]{4,3,2,1,0:T(8,128)S(1)} %collective-permute-done.10), channel_id=1, source_target_pairs={{16,64},{104,56},{17,65},{105,57},{18,66},{106,58},{19,67},{107,59... | collective-permute-start | bytes 1179656 | tf_op jit(solution)/shard_map/ppermute | solution.py:277
  93.4 12.8 %collective-permute-start.9 = (f32[3,1,8,16,256]{4,3,2,1,0:T(8,128)S(1)}, f32[3,1,8,16,256]{4,3,2,1,0:T(8,128)S(1)}, u32[]{:S(2)}, u32[]{:S(2)}) collective-permute-start(f32[3,1,8,16,256]{4,3,2,1,0:T(8,128)S(1)} %collective-permute-done.8), channel_id=1, source_target_pairs={{48,64},{72,56},{49,65},{73,57},{50,66},{74,58},{51,67},{75,59},{1... | collective-permute-start | bytes 1179656 | tf_op jit(solution)/shard_map/ppermute | solution.py:277
  114.5 27.7 %all-to-all-start.3 = ((f32[8,3,2,4,8,256]{5,4,3,2,1,0:T(8,128)}), f32[8,3,2,4,8,256]{5,4,3,2,1,0:T(8,128)}, u32[]{:S(2)}, u32[]{:S(2)}) async-start(f32[8,3,2,4,8,256]{5,4,3,2,1,0:T(8,128)} %second.1), calls=%async_computation.3 | async-start | bytes 3145728 | tf_op jit(solution)/shard_map/all_to_all | solution.py:304
  (6 other events, 41.4 us)
